TPU v7x, 256 devices: a whole 4x4x8 slice. The times are simulated.
256 devices in a mesh: dp: 32 (over z, y), frame: 8 (over x, core).
Axes of the slice: x: 4, y: 4, z: 8, core: 2. Of those that a mesh axis runs over, the one named last changes fastest.
Arguments:
- qkv: bfloat16 [32, 8, 192, 4224], P('dp', 'frame'), may hold values from -24 to 24
- keep: int32 [32, 8, 192], P('dp', 'frame'), may hold values from 0 to 255, as said below
- counts: int32 [32, 8], P('dp', 'frame'), may hold values from 96 to 192, as said below
- grad_out: bfloat16 [32, 8, 192, 1408], P('dp', 'frame'), may hold values from -6 to 6
- w_out: bfloat16 [1408, 1408], P('dp', 'frame'), may hold values from -0.15625 to 0.15625
Outputs:
- mixed: bfloat16 [32, 8, 192, 1408], P('dp', 'frame')
- grad_qkv: bfloat16 [32, 8, 192, 4224], P('dp', 'frame')
- grad_w_out: float32 [1408, 1408], P('dp', 'frame')
Inputs may be any that keep to these rules, and one draw needn't show every extreme that they name: `keep`: the 192 entries of one frame are distinct and increasing; slots past the frame's count hold positions too, which are not used. `counts`: every clip has a frame whose 192 slots are all valid.
All inputs are finite; a program needn't handle non-finite values.
Results may differ from a plain program's by a relative error of at most 0.0057.
Values may be sent and summed in bfloat16 or wider, within the bound.
No kernel may reach another device: no remote copies, remote signals or barrier semaphores. Data moves between devices by JAX's collectives and lax.ppermute only.
A program may use at most 128 MiB of HBM per device.

v0:
```python
import math

import jax
import jax.numpy as jnp
from jax import lax
from jax.sharding import PartitionSpec as P

HEADS = 16
PATCHES = 256


def temporal_forward(grid_pos, kept_pos):
    frames_all, near_pos, triple = grid_pos.shape
    width_all = triple // 3
    head_size = width_all // HEADS
    shape_heads = (frames_all, near_pos, HEADS, head_size)
    query_part = grid_pos[..., :width_all].reshape(shape_heads)
    key_part = grid_pos[..., width_all : 2 * width_all].reshape(shape_heads)
    value_part = grid_pos[..., 2 * width_all :].reshape(shape_heads)
    scaling = 1.0 / math.sqrt(head_size)
    scores = (
        jnp.einsum("tphd,sphd->phts", query_part, key_part, preferred_element_type=jnp.float32)
        * scaling
    )
    present = (jnp.transpose(kept_pos) > 0)[:, None, None, :]
    scores = jnp.where(present, scores, -1e30)
    expo = jnp.exp(scores - jnp.max(scores, axis=-1, keepdims=True))
    soft_full = expo / jnp.sum(expo, axis=-1, keepdims=True)
    soft_half = soft_full.astype(jnp.bfloat16)
    heads_out = jnp.einsum(
        "phts,sphd->tphd", soft_half, value_part, preferred_element_type=jnp.float32
    )
    att_grid = heads_out.astype(jnp.bfloat16).reshape(frames_all, near_pos, width_all)
    return (att_grid, (query_part, key_part, value_part, soft_full, soft_half))


def temporal_backward(saved, grad_pos):
    query_part, key_part, value_part, soft_full, soft_half = saved
    frames_all, near_pos, heads_all, head_size = query_part.shape
    scaling = 1.0 / math.sqrt(head_size)
    grad_heads = grad_pos.reshape(query_part.shape)
    grad_soft = jnp.einsum(
        "tphd,sphd->phts", grad_heads, value_part, preferred_element_type=jnp.float32
    )
    grad_value = jnp.einsum(
        "phts,tphd->sphd", soft_half, grad_heads, preferred_element_type=jnp.float32
    ).astype(jnp.bfloat16)
    inner = jnp.sum(soft_full * grad_soft, axis=-1, keepdims=True)
    grad_score = (soft_full * (grad_soft - inner)).astype(jnp.bfloat16)
    grad_query = jnp.einsum(
        "phts,sphd->tphd", grad_score, key_part, preferred_element_type=jnp.float32
    )
    grad_key = jnp.einsum(
        "phts,tphd->sphd", grad_score, query_part, preferred_element_type=jnp.float32
    )
    grad_query = (grad_query * scaling).astype(jnp.bfloat16)
    grad_key = (grad_key * scaling).astype(jnp.bfloat16)
    flat_shape = (frames_all, near_pos, heads_all * head_size)
    return jnp.concatenate(
        [
            grad_query.reshape(flat_shape),
            grad_key.reshape(flat_shape),
            grad_value.reshape(flat_shape),
        ],
        axis=-1,
    )


def shards(qkv, keep, counts, grad_out, w_out):
    frames_here = qkv.shape[1]
    slots = qkv.shape[2]
    width_all = grad_out.shape[3]
    rows_here = frames_here * slots
    positions = jnp.arange(PATCHES, dtype=jnp.int32)
    live = jnp.arange(slots, dtype=jnp.int32)[None, :] < counts[0][:, None]
    placing = ((keep[0][:, :, None] == positions[None, None, :]) & live[:, :, None]).astype(
        jnp.bfloat16
    )
    grid = jnp.einsum("fjp,fjc->fpc", placing, qkv[0], preferred_element_type=jnp.float32).astype(
        jnp.bfloat16
    )
    kept = jnp.sum(placing, axis=1)
    grid_pos, kept_pos = (
        lax.all_to_all(grid, "frame", split_axis=1, concat_axis=0, tiled=True),
        lax.all_to_all(kept, "frame", split_axis=1, concat_axis=0, tiled=True),
    )
    att_grid, saved = temporal_forward(grid_pos, kept_pos)
    att_back = lax.all_to_all(att_grid, "frame", split_axis=0, concat_axis=1, tiled=True)
    att_slots = jnp.einsum("fjp,fpd->fjd", placing, att_back, preferred_element_type=jnp.float32)
    att_flat = att_slots.astype(jnp.bfloat16).reshape(rows_here, width_all)
    w_rows = lax.all_gather(w_out, "frame", axis=1, tiled=True)
    columns = att_flat
    mixed = jnp.dot(
        columns,
        lax.all_gather(w_rows, "dp", axis=0, tiled=True),
        preferred_element_type=jnp.float32,
    )
    mixed = mixed.astype(jnp.bfloat16).reshape(1, frames_here, slots, width_all)
    grad_flat = grad_out.reshape(rows_here, width_all)
    grad_att = lax.dot_general(
        grad_flat,
        lax.all_gather(w_rows, "dp", axis=0, tiled=True),
        (((1,), (1,)), ((), ())),
        preferred_element_type=jnp.float32,
    ).astype(jnp.bfloat16)
    dp_count = lax.axis_size("dp")
    columns = att_flat
    partial_rows = lax.psum_scatter(
        lax.dot_general(
            columns, grad_flat, (((0,), (0,)), ((), ())), preferred_element_type=jnp.float32
        ),
        "dp",
        scatter_dimension=0,
        tiled=True,
    )
    grad_weight = lax.psum_scatter(partial_rows, "frame", scatter_dimension=1, tiled=True)
    grad_weight = grad_weight * (1.0 / dp_count)
    grad_grid = jnp.einsum(
        "fjp,fjd->fpd",
        placing,
        grad_att.reshape(frames_here, slots, width_all),
        preferred_element_type=jnp.float32,
    ).astype(jnp.bfloat16)
    grad_pos = lax.all_to_all(grad_grid, "frame", split_axis=1, concat_axis=0, tiled=True)
    grad_qkv_pos = temporal_backward(saved, grad_pos)
    grad_qkv_grid = lax.all_to_all(grad_qkv_pos, "frame", split_axis=0, concat_axis=1, tiled=True)
    grad_qkv = jnp.einsum(
        "fjp,fpc->fjc", placing, grad_qkv_grid, preferred_element_type=jnp.float32
    ).astype(jnp.bfloat16)
    return (mixed, grad_qkv[None], grad_weight)


def solution(mesh):
    return jax.shard_map(
        shards,
        mesh=mesh,
        in_specs=(
            P("dp", "frame", None, None),
            P("dp", "frame", None),
            P("dp", "frame"),
            P("dp", "frame", None, None),
            P("dp", "frame"),
        ),
        out_specs=(P("dp", "frame", None, None), P("dp", "frame", None, None), P("dp", "frame")),
        check_vma=False,
    )
```

profile of v0, /device:TPU:8, one launch (start us, length us, event | category | flops | bytes accessed | tf_op | source)
XLA Modules:
  0.0 375.4 jit_solution(5501548188195513537)
XLA Ops:
  8.1 13.5 %all-gather = bf16[8,176,44]{1,2,0:T(8,128)(2,1)S(1)} all-gather(bf16[1,176,44]{1,2,0:T(8,128)(2,1)} %bitcast.90), channel_id=1, replica_groups=mesh['dp'=32,'frame'=8] {'frame'}, dimensions={0}, use_global_device_ids=true | all-gather | bytes 139392 | tf_op jit(solution)/shard_map/all_gather | solution.py:91
  24.7 3.7 all-to-all-start.1
  29.9 5.4 %copy.121 = bf16[1,256,4224]{2,0,1:T(2,128)(2,1)} copy(bf16[1,256,4224]{2,1,0:T(8,128)(2,1)S(1)} %fusion.2) | data formatting | bytes 4325376 | tf_op jit(solution)/shard_map/convert_element_type | solution.py:79
  35.9 15.4 %reduce.4 = bf16[256,4224]{1,0:T(8,128)(2,1)} reduce(bf16[256,1,4224]{2,1,0:T(2,128)(2,1)} %bitcast.78, bf16[]{:T(256)} %broadcast.117), dimensions={1}, to_apply=%bitcast.75.reduce_sub_computation | reduce | bytes 4325378
  51.3 5.9 %reshape.319 = bf16[8,2,67584]{2,1,0:T(2,128)(2,1)} reshape(bf16[256,4224]{1,0:T(8,128)(2,1)} %reduce.4) | data formatting | bytes 4325376
  57.1 5.2 %all-to-all-start = ((bf16[8,2,67584]{2,1,0:T(2,128)(2,1)}), bf16[8,2,67584]{2,1,0:T(2,128)(2,1)}, u32[]{:S(2)}, u32[]{:S(2)}) async-start(bf16[8,2,67584]{2,1,0:T(2,128)(2,1)} %reshape.319), calls=%async_computation | async-start | bytes 4325376 | tf_op jit(solution)/shard_map/all_to_all | solution.py:84
  62.4 27.8 %all-to-all-done = bf16[8,2,67584]{2,1,0:T(2,128)(2,1)} async-done(((bf16[8,2,67584]{2,1,0:T(2,128)(2,1)}), bf16[8,2,67584]{2,1,0:T(2,128)(2,1)}, u32[]{:S(2)}, u32[]{:S(2)}) %all-to-all-start) | async-done | bytes 2162720 | tf_op jit(solution)/shard_map/all_to_all | solution.py:84
  90.3 6.9 %reshape.320 = bf16[256,1,4224]{2,1,0:T(2,128)(2,1)} reshape(bf16[8,2,67584]{2,1,0:T(2,128)(2,1)} %all-to-all-done) | data formatting | bytes 4325376
  97.2 2.5 copy.89
  102.7 3.2 reshape.301
  105.9 3.0 reshape.299
  108.9 3.6 fusion.52
  112.5 3.0 fusion.8
  115.7 2.3 reshape.302
  117.9 4.7 %all-to-all-start.2 = ((bf16[8,32,1408]{2,1,0:T(8,128)(2,1)}), bf16[8,32,1408]{2,1,0:T(8,128)(2,1)}, u32[]{:S(2)}, u32[]{:S(2)}) async-start(bf16[8,32,1408]{2,1,0:T(8,128)(2,1)} %reshape.302), calls=%async_computation.2 | async-start | bytes 1441792 | tf_op jit(solution)/shard_map/all_to_all | solution.py:88
  122.7 6.0 %reshape.314 = bf16[1408,1408]{1,0:T(8,128)(2,1)} reshape(bf16[32,44,1408]{2,1,0:T(8,128)(2,1)} %all-gather.4.cloned.1.call-done) | data formatting | bytes 7929856
  128.7 3.8 %fusion.4 = bf16[1,256,1408]{2,1,0:T(8,128)(2,1)S(1)} fusion(bf16[1408,1408]{1,0:T(8,128)(2,1)} %reshape.314, bf16[1,1,192,1408]{3,2,1,0:T(8,128)(2,1)S(1)} %copy-done.10, s32[192]{0:T(256)S(1)} %bitcast.87, pred[192]{0:T(512)(128)(4,1)S(1)} %iota_compare_fusion.3), kind=kOutput, calls=%fused_computation.9 | convolution fusion | flops 900407296 | bytes 5227456 | tf_op jit(solution)/shard_map/fjp,fjd->fpd/dot_general | solution.py:118
  133.6 5.0 %reduce.5 = bf16[256,1408]{1,0:T(8,128)(2,1)S(1)} reduce(bf16[256,1,1408]{2,1,0:T(2,128)(2,1)S(1)} %bitcast.81, bf16[]{:T(256)} %broadcast.117), dimensions={1}, to_apply=%bitcast.76.reduce_sub_computation | reduce | bytes 1441794
  139.7 4.8 %all-to-all-start.3 = ((bf16[8,2,22528]{2,1,0:T(2,128)(2,1)}), bf16[8,2,22528]{2,1,0:T(2,128)(2,1)S(1)}, u32[]{:S(2)}, u32[]{:S(2)}) async-start(bf16[8,2,22528]{2,1,0:T(2,128)(2,1)} %reshape.321), calls=%async_computation.3 | async-start | bytes 1441792 | tf_op jit(solution)/shard_map/all_to_all | solution.py:124
  146.0 4.4 %fusion.25 = f32[1408,1408]{1,0:T(8,128)} fusion(bf16[192,1408]{1,0:T(8,128)(2,1)S(1)} %convolution_convert_fusion.5, bf16[1,1,192,1408]{3,2,1,0:T(8,128)(2,1)S(1)} %copy-done.11), kind=kOutput, calls=%fused_computation.40 | convolution fusion | flops 761266176 | bytes 9011200 | tf_op jit(solution)/shard_map/dot_general | solution.py:109
  150.4 6.5 %all-to-all-done.3 = bf16[8,2,22528]{2,1,0:T(2,128)(2,1)S(1)} async-done(((bf16[8,2,22528]{2,1,0:T(2,128)(2,1)}), bf16[8,2,22528]{2,1,0:T(2,128)(2,1)S(1)}, u32[]{:S(2)}, u32[]{:S(2)}) %all-to-all-start.3) | async-done | bytes 720928 | tf_op jit(solution)/shard_map/all_to_all | solution.py:124
  157.9 4.2 %bitcast_reduce_fusion = bf16[256,1408]{1,0:T(8,128)(2,1)S(1)} fusion(bf16[256,1,1408]{2,1,0:T(2,128)(2,1)S(1)} %reshape.322), kind=kLoop, calls=%fused_computation.71 | loop fusion | bytes 1441792 | tf_op jit(solution)/shard_map/all_to_all | solution.py:124
  162.1 2.0 reshape.306
  164.1 2.7 fusion.9
  175.0 2.9 reshape.307
  180.9 4.3 %all-to-all-start.4 = ((bf16[8,32,4224]{2,1,0:T(8,128)(2,1)}), bf16[8,32,4224]{2,1,0:T(8,128)(2,1)}, u32[]{:S(2)}, u32[]{:S(2)}) async-start(bf16[8,32,4224]{2,1,0:T(8,128)(2,1)} %pad_maximum_fusion), calls=%async_computation.4 | async-start | bytes 4325376 | tf_op jit(solution)/shard_map/all_to_all | solution.py:126
  185.4 116.8 %fusion = f32[48,1408]{1,0:T(8,128)S(1)} fusion(f32[1408,1408]{1,0:T(8,128)} %fusion.25), kind=kCustom, calls=%all-reduce-scatter | all-reduce-scatter fusion | flops 2162689 | bytes 8201216
  303.5 4.8 %collective-permute-start = (f32[48,1408]{1,0:T(8,128)S(1)}, f32[48,1408]{1,0:T(8,128)S(1)}, u32[]{:S(2)}, u32[]{:S(2)}) collective-permute-start(f32[48,1408]{1,0:T(8,128)S(1)} %fusion), channel_id=1, source_target_pairs={{0,8},{8,16},{16,24},{24,32},{32,40},{40,48},{48,56},{56,64},{64,7... | collective-permute-start | bytes 811016
  312.7 3.2 collective-permute-done
  317.7 40.9 %reduce-scatter.6.cloned.1.call-done = f32[176,44]{1,0:T(8,128)} async-done(((f32[1408,44]{1,0:T(8,128)}), f32[176,44]{1,0:T(8,128)}) %reduce-scatter.6.cloned.1.call-update) | async-done | bytes 30992
  360.2 4.1 %fusion.5 = bf16[1,1,192,1408]{3,2,1,0:T(8,128)(2,1)} fusion(bf16[192,1408]{1,0:T(8,128)(2,1)S(1)} %copy-done.7, bf16[1408,1408]{1,0:T(8,128)(2,1)} %reshape.314), kind=kOutput, calls=%fused_computation.10 | convolution fusion | flops 761536512 | bytes 5046272 | tf_op jit(solution)/shard_map/dot_general | solution.py:93
  364.3 3.4 fusion.3
  (77 shorter events, 32.1 us)
Async XLA Ops:
  8.0 20.4 %copy-start = (bf16[1,1,192,4224]{3,2,1,0:T(8,128)(2,1)S(1)}, bf16[1,1,192,4224]{3,2,1,0:T(8,128)(2,1)}, u32[]{:S(2)}) copy-start(bf16[1,1,192,4224]{3,2,1,0:T(8,128)(2,1)} %param.5) | copy-start | bytes 4866052
  8.0 114.7 %all-gather.4.cloned.1.call-start = ((), (), s32[]{:S(2)}) async-start(), calls=%async_computation.6 | async-start | bytes 4460544 | tf_op jit(solution)/shard_map/all_gather | solution.py:95
  24.7 32.5 %all-to-all-start.1 = ((bf16[1,8,32]{2,0,1:T(2,128)(2,1)}), bf16[1,8,32]{2,0,1:T(2,128)(2,1)S(1)}, u32[]{:S(2)}, u32[]{:S(2)}) async-start(bf16[1,8,32]{2,0,1:T(2,128)(2,1)} %all_to_all.22), calls=%async_computation.1 | async-start | bytes 8192 | tf_op jit(solution)/shard_map/all_to_all | solution.py:85
  57.1 33.1 %all-to-all-start = ((bf16[8,2,67584]{2,1,0:T(2,128)(2,1)}), bf16[8,2,67584]{2,1,0:T(2,128)(2,1)}, u32[]{:S(2)}, u32[]{:S(2)}) async-start(bf16[8,2,67584]{2,1,0:T(2,128)(2,1)} %reshape.319), calls=%async_computation | async-start | bytes 4325376 | tf_op jit(solution)/shard_map/all_to_all | solution.py:84
  105.9 6.6 %copy-start.2 = (bf16[8,32,16,88]{3,2,1,0:T(8,128)(2,1)}, bf16[8,32,16,88]{3,2,1,0:T(8,128)(2,1)S(1)}, u32[]{:S(2)}) copy-start(bf16[8,32,16,88]{3,2,1,0:T(8,128)(2,1)S(1)} %reshape.301) | copy-start | bytes 2162692
  112.5 3.0 copy-start.12
  117.9 21.8 %all-to-all-start.2 = ((bf16[8,32,1408]{2,1,0:T(8,128)(2,1)}), bf16[8,32,1408]{2,1,0:T(8,128)(2,1)}, u32[]{:S(2)}, u32[]{:S(2)}) async-start(bf16[8,32,1408]{2,1,0:T(8,128)(2,1)} %reshape.302), calls=%async_computation.2 | async-start | bytes 1441792 | tf_op jit(solution)/shard_map/all_to_all | solution.py:88
  122.7 6.0 %copy-start.10 = (bf16[1,1,192,1408]{3,2,1,0:T(8,128)(2,1)S(1)}, bf16[1,1,192,1408]{3,2,1,0:T(8,128)(2,1)}, u32[]{:S(2)}) copy-start(bf16[1,1,192,1408]{3,2,1,0:T(8,128)(2,1)} %param.8) | copy-start | bytes 1622020
  122.7 6.0 %copy-start.14 = (s32[1,1,192]{2,1,0:T(1,128)S(1)}, s32[1,1,192]{2,1,0:T(1,128)}, u32[]{:S(2)}) copy-start(s32[1,1,192]{2,1,0:T(1,128)} %param.6) | copy-start | bytes 2308
  138.7 7.3 %copy-start.11 = (bf16[1,1,192,1408]{3,2,1,0:T(8,128)(2,1)S(1)}, bf16[1,1,192,1408]{3,2,1,0:T(8,128)(2,1)}, u32[]{:S(2)}) copy-start(bf16[1,1,192,1408]{3,2,1,0:T(8,128)(2,1)} %param.8) | copy-start | bytes 1622020
  139.7 17.2 %all-to-all-start.3 = ((bf16[8,2,22528]{2,1,0:T(2,128)(2,1)}), bf16[8,2,22528]{2,1,0:T(2,128)(2,1)S(1)}, u32[]{:S(2)}, u32[]{:S(2)}) async-start(bf16[8,2,22528]{2,1,0:T(2,128)(2,1)} %reshape.321), calls=%async_computation.3 | async-start | bytes 1441792 | tf_op jit(solution)/shard_map/all_to_all | solution.py:124
  146.0 4.4 %copy-start.6 = (bf16[192,1408]{1,0:T(8,128)(2,1)}, bf16[192,1408]{1,0:T(8,128)(2,1)S(1)}, u32[]{:S(2)}) copy-start(bf16[192,1408]{1,0:T(8,128)(2,1)S(1)} %convolution_convert_fusion.5) | copy-start | bytes 1622020
  164.1 2.8 copy-start.8
  164.1 2.8 copy-start.9
  164.1 2.8 copy-start.13
  169.2 1.9 copy-start.3
  173.8 4.1 %copy-start.4 = (bf16[8,32,16,88]{3,0,2,1:T(8,128)(2,1)S(1)}, bf16[8,32,16,88]{3,0,2,1:T(8,128)(2,1)}, u32[]{:S(2)}) copy-start(bf16[8,32,16,88]{3,0,2,1:T(8,128)(2,1)} %fusion.11) | copy-start | bytes 2162692
  178.1 1.4 copy-start.5
  180.9 183.4 %all-to-all-start.4 = ((bf16[8,32,4224]{2,1,0:T(8,128)(2,1)}), bf16[8,32,4224]{2,1,0:T(8,128)(2,1)}, u32[]{:S(2)}, u32[]{:S(2)}) async-start(bf16[8,32,4224]{2,1,0:T(8,128)(2,1)} %pad_maximum_fusion), calls=%async_computation.4 | async-start | bytes 4325376 | tf_op jit(solution)/shard_map/all_to_all | solution.py:126
  185.3 124.4 %copy-start.15 = (u32[256]{0:T(256)S(1)}, u32[256]{0:T(256)}, u32[]{:S(2)}) copy-start(u32[256]{0:T(256)} %constant.21) | copy-start | bytes 3076
  185.3 173.3 %reduce-scatter.6.cloned.1.call-start = ((), (), s32[]{:S(2)}) async-start(), calls=%async_computation.7 | async-start | bytes 811008
  302.2 10.5 %collective-permute-start.1 = (f32[48,1408]{1,0:T(8,128)S(1)}, f32[48,1408]{1,0:T(8,128)S(1)}, u32[]{:S(2)}, u32[]{:S(2)}) collective-permute-start(f32[48,1408]{1,0:T(8,128)S(1)} %fusion), channel_id=1, source_target_pairs={{0,16},{8,24},{16,32},{24,40},{32,48},{40,56},{48,64},{56,72},{64,... | collective-permute-start | bytes 811016
  303.5 12.3 %collective-permute-start = (f32[48,1408]{1,0:T(8,128)S(1)}, f32[48,1408]{1,0:T(8,128)S(1)}, u32[]{:S(2)}, u32[]{:S(2)}) collective-permute-start(f32[48,1408]{1,0:T(8,128)S(1)} %fusion), channel_id=1, source_target_pairs={{0,8},{8,16},{16,24},{24,32},{32,40},{40,48},{48,56},{56,64},{64,7... | collective-permute-start | bytes 811016
  308.4 4.3 %collective-permute-start.2 = (f32[28,1408]{1,0:T(8,128)S(1)}, f32[28,1408]{1,0:T(8,128)S(1)}, u32[]{:S(2)}, u32[]{:S(2)}) collective-permute-start(f32[28,1408]{1,0:T(8,128)S(1)} %slice.15), channel_id=1, source_target_pairs={{0,24},{8,32},{16,40},{24,48},{32,56},{40,64},{48,72},{56,80},{64,... | collective-permute-start | bytes 473096
  311.0 49.3 %copy-start.7 = (bf16[192,1408]{1,0:T(8,128)(2,1)S(1)}, bf16[192,1408]{1,0:T(8,128)(2,1)}, u32[]{:S(2)}) copy-start(bf16[192,1408]{1,0:T(8,128)(2,1)} %copy-done.6) | copy-start | bytes 1622020
  360.2 7.5 %copy-start.1 = (bf16[1,1,192,4224]{3,2,1,0:T(8,128)(2,1)S(1)}, bf16[1,1,192,4224]{3,2,1,0:T(8,128)(2,1)}, u32[]{:S(2)}) copy-start(bf16[1,1,192,4224]{3,2,1,0:T(8,128)(2,1)} %param.5) | copy-start | bytes 4866052
Sparse Core Ops, SparseCore 0:
  22.6 83.4 all-gather.3
Sparse Core Ops, SparseCore 1:
  317.8 40.7 reduce-scatter.5
where the time goes:
time: 382 us; the launch traced here: 375 us
  blocking collectives  130 us (34%)
  waiting for transfers between devices  80.2 us (21%)
  local copies, waits for them, and re-layouts  60.6 us (16%)
  matrix products  32.8 us (9%)
  starting transfers between devices  30.2 us (8%)
  other arithmetic  23.9 us (6%)
  between operations  17.4 us (5%)
    unnamed x1, blocking collectives  117 us
    unnamed x6, waiting for transfers between devices  45.8 us
    unnamed x46, local copies, waits for them, and re-layouts  28.2 us
    all_to_all x1, waiting for transfers between devices, shards(): lax.all_to_all(grid, 'frame', split_axis=1, concat_axis=0, tiled=True)  27.8 us
    unnamed x2, other arithmetic  20.4 us
    all_gather x1, blocking collectives, shards(): w_rows = lax.all_gather(w_out, 'frame', axis=1, tiled=True)  13.5 us
  transfers between devices with their start and end apart: 10, of which 5 were waited for; matrix products, arithmetic and copies ran while one was open for 55% of the time, Pallas kernels for 0%

commit v1 on v0

v1 whole, which is shorter than its diff:
```python
import functools
import math

import jax
import jax.numpy as jnp
from jax import lax
from jax.experimental import pallas as pl
from jax.experimental.pallas import tpu as pltpu
from jax.sharding import Mesh
from jax.sharding import PartitionSpec as P

HEADS = 16
PATCHES = 256
FRAMES = 8
CAP = 192
D = 1408
WIDE = D // FRAMES
HEAD = D // HEADS
SUB = 44
SUBP = 48
PACK = 640
GROUP = 16
BLOCK = GROUP * FRAMES
BIG = 1e30
VMEM = pltpu.VMEM
bf16 = jnp.bfloat16
f32 = jnp.float32


STEPS = [(0, 0), (0, 1), (3, 0), (3, 1), (1, 0), (1, 1), (2, 0), (2, 1)]
ALL = ("z", "y", "x", "core")
FRAME = ("x", "core")
WHERE, ORIGIN, Z_FLIP, Y_FLIP = 0, 8, 16, 24


def dot(a, b):
    return jnp.dot(a, b, preferred_element_type=f32)


def dot_t(a, b):
    return lax.dot_general(a, b, (((1,), (1,)), ((), ())), preferred_element_type=f32)


def t_dot(a, b):
    return lax.dot_general(a, b, (((0,), (0,)), ((), ())), preferred_element_type=f32)


def iota(shape, dim):
    return lax.broadcasted_iota(jnp.int32, shape, dim)


def call(kernel, out_shape, n_in, flops=0, scratch=(), smem=()):
    def spec(shape):
        return pl.BlockSpec(shape, lambda i: (0,) * len(shape), pipeline_mode=pl.Buffered(1))

    def run(*args):
        specs = [
            pl.BlockSpec(memory_space=pltpu.SMEM) if i in smem else spec(a.shape)
            for i, a in enumerate(args)
        ]
        return pl.pallas_call(
            kernel,
            grid=(1,),
            out_shape=out_shape,
            in_specs=specs,
            out_specs=jax.tree.map(lambda s: spec(s.shape), out_shape),
            scratch_shapes=list(scratch),
            compiler_params=pltpu.CompilerParams(vmem_limit_bytes=60 * 1024 * 1024),
            cost_estimate=pl.CostEstimate(flops=flops, bytes_accessed=0, transcendentals=0),
        )(*args)

    return run


def pack_kernel(counts_ref, qkv_ref, keep_ref, out_ref):
    keep = keep_ref[0, 0:1, :]
    slot = iota((CAP, CAP), 1)
    diag = iota((CAP, CAP), 0) == slot
    held = jnp.where(slot < counts_ref[0, 0], keep.astype(f32), -1.0)
    column = jnp.sum(jnp.where(diag, held, 0.0), axis=1, keepdims=True)
    tail = jnp.broadcast_to(column, (CAP, PACK - 3 * WIDE)).astype(bf16)
    for f in range(FRAMES):
        parts = [
            qkv_ref[0, 0, :, part * D + WIDE * f : part * D + WIDE * (f + 1)] for part in range(3)
        ]
        out_ref[f] = jnp.concatenate(parts + [tail], axis=1)


def rows_from(keep_column):
    diag = iota((CAP, CAP), 0) == iota((CAP, CAP), 1)
    return jnp.sum(jnp.where(diag, keep_column, 0.0), axis=0, keepdims=True)


def forward_kernel(
    recv_ref, att_ref, hot_ref, hot_t_ref, qg, kg, vg, probs_ref, ag
):
    scaling = 1.0 / math.sqrt(HEAD)
    lane = iota((PATCHES, PATCHES), 1)
    patch = lax.rem(iota((PATCHES, PATCHES), 0), GROUP)
    extra = lane >= WIDE
    q_extra = jnp.where((lane == WIDE) | (lane == WIDE + 1 + patch), 1.0, 0.0)
    pick = (lane > WIDE) & (lane <= WIDE + GROUP)
    k_extra = jnp.where(pick & (lane != WIDE + 1 + patch), -BIG, 0.0)
    zeros = jnp.zeros((CAP, PATCHES - WIDE), bf16)
    ones = jnp.ones((CAP, PATCHES - WIDE), bf16)
    for t in range(FRAMES):
        recv = recv_ref.at[t]
        column = recv[:, 3 * WIDE : 3 * WIDE + 1].astype(f32)
        row = rows_from(column)
        hot = jnp.where(column == iota((CAP, PATCHES), 1).astype(f32), 1.0, 0.0)
        hot_ref[t] = hot.astype(bf16)
        hot_t = jnp.where(row == iota((PATCHES, CAP), 0).astype(f32), 1.0, 0.0).astype(bf16)
        hot_t_ref[t] = jnp.concatenate([hot_t, jnp.zeros((PATCHES, PATCHES - CAP), bf16)], axis=1)
        q = recv[:, :WIDE]
        k = recv[:, WIDE : 2 * WIDE]
        v = recv[:, 2 * WIDE : 3 * WIDE]
        placed = dot(hot_t, jnp.concatenate([q, zeros, k, ones, v], axis=1))
        qg[t] = (placed[:, :PATCHES] + q_extra).astype(bf16)
        kk = placed[:, PATCHES : 2 * PATCHES]
        kk = jnp.where(extra, jnp.where(lane == WIDE, (kk - 1.0) * BIG, k_extra), kk)
        kg[t] = kk.astype(bf16)
        vg[t] = placed[:, 2 * PATCHES :].astype(bf16)

    wide_lane = iota((BLOCK, PATCHES), 1)
    first = (wide_lane < HEAD) | (wide_lane >= WIDE)
    second = wide_lane >= HEAD
    slim = iota((BLOCK, WIDE), 1) < HEAD
    for b in range(PATCHES // GROUP):
        rows = slice(b * GROUP, (b + 1) * GROUP)
        q = jnp.concatenate([qg[t, rows, :] for t in range(FRAMES)], axis=0)
        k = jnp.concatenate([kg[t, rows, :] for t in range(FRAMES)], axis=0)
        v = jnp.concatenate([vg[t, rows, :] for t in range(FRAMES)], axis=0)
        zero = jnp.zeros_like(q)
        q2 = jnp.concatenate([jnp.where(first, q, zero), jnp.where(second, q, zero)], axis=0)
        scores = dot_t(k, q2) * scaling
        expo = jnp.exp(scores - jnp.max(scores, axis=0, keepdims=True))
        probs = expo * (1.0 / jnp.sum(expo, axis=0, keepdims=True))
        probs_ref[b] = probs
        out = t_dot(probs.astype(bf16), v)
        att = jnp.where(slim, out[:BLOCK], out[BLOCK:]).astype(bf16)
        for t in range(FRAMES):
            ag[t, rows, :] = att[t * GROUP : (t + 1) * GROUP]
    tail = jnp.zeros((CAP, PATCHES - WIDE), bf16)
    for t in range(FRAMES):
        slots = dot(hot_ref[t], ag[t]).astype(bf16)
        att_ref[t] = jnp.concatenate([slots, tail], axis=1)


def backward_kernel(
    table_ref, grad_att_ref, att_ref, hot_ref, hot_t_ref, qg, kg, vg, probs_ref, *refs
):
    grad_ref, gg, dq, dk, dv = refs
    scaling = 1.0 / math.sqrt(HEAD)
    for i in range(FRAMES):
        t = table_ref[0, WHERE + i]
        gg[t] = dot(hot_t_ref[t][:, :CAP], grad_att_ref[i]).astype(bf16)
    slim = iota((BLOCK, WIDE), 1) < HEAD

    def two(x):
        zero = jnp.zeros_like(x)
        return jnp.concatenate([jnp.where(slim, x, zero), jnp.where(slim, zero, x)], axis=0)

    for b in range(PATCHES // GROUP):
        rows = slice(b * GROUP, (b + 1) * GROUP)
        q = jnp.concatenate([qg[t, rows, :WIDE] for t in range(FRAMES)], axis=0)
        k = jnp.concatenate([kg[t, rows, :WIDE] for t in range(FRAMES)], axis=0)
        v = jnp.concatenate([vg[t, rows, :] for t in range(FRAMES)], axis=0)
        g2 = two(jnp.concatenate([gg[t, rows, :] for t in range(FRAMES)], axis=0))
        probs = probs_ref[b]
        grad_probs = dot_t(v, g2)
        grad_v = dot(probs.astype(bf16), g2).astype(bf16)
        inner = jnp.sum(probs * grad_probs, axis=0, keepdims=True)
        grad_scores = (probs * (grad_probs - inner)).astype(bf16)
        out = t_dot(grad_scores, k)
        grad_q = (jnp.where(slim, out[:BLOCK], out[BLOCK:]) * scaling).astype(bf16)
        grad_k = (dot(grad_scores, two(q)) * scaling).astype(bf16)
        for t in range(FRAMES):
            own = slice(t * GROUP, (t + 1) * GROUP)
            dq[t, rows, :] = grad_q[own]
            dk[t, rows, :] = grad_k[own]
            dv[t, rows, :] = grad_v[own]
    for t in range(FRAMES):
        parts = [dot(hot_ref[t], x[t]).astype(bf16) for x in (dq, dk, dv)]
        grad_ref[t] = jnp.concatenate(parts + [att_ref[t, :, :WIDE]], axis=1)


def grad_att_kernel(w_ref, *refs):
    for i in range(FRAMES):
        refs[FRAMES][i] = dot_t(refs[i][...], w_ref[...]).astype(bf16)


def weight_kernel(table_ref, att_ref, *refs):
    keep_ref, send_ref, scr = refs[FRAMES:]
    total = None
    for i in range(FRAMES):
        term = t_dot(att_ref[table_ref[0, WHERE + i]][:, :WIDE], refs[i][...])
        total = term if total is None else total + term
    down = jnp.zeros((SUBP - SUB, D), f32)
    for s in range(4):
        scr[s] = jnp.concatenate([total[SUB * s : SUB * (s + 1)], down], axis=0)
    for r in range(2):
        keep_ref[r] = scr[table_ref[0, Y_FLIP + r]]
        send_ref[r] = scr[table_ref[0, Y_FLIP + 2 + r]].astype(bf16)


def halve_kernel(own_ref, in_ref, keep_ref, send_ref):
    half = own_ref.shape[0] // 2
    keep_ref[...] = own_ref[:half] + in_ref[:half].astype(f32)
    send_ref[...] = (own_ref[half:] + in_ref[half:].astype(f32)).astype(bf16)


def planes_kernel(table_ref, own_ref, in_ref, keep_ref, send_ref, scr):
    total = own_ref[0] + in_ref[0].astype(f32)
    for f in range(FRAMES):
        scr[f] = total[:, WIDE * f : WIDE * (f + 1)]
    for r in range(4):
        keep_ref[r] = scr[table_ref[0, Z_FLIP + r]]
        send_ref[r] = scr[table_ref[0, Z_FLIP + 4 + r]].astype(bf16)


def last_kernel(own_ref, in_ref, out_ref):
    out_ref[...] = ((own_ref[0] + in_ref[0].astype(f32)) * (1.0 / 32))[:SUB]


def columns_kernel(table_ref, *refs):
    out_ref, scr = refs[4:]
    at = 0
    for ref in refs[:4]:
        for i in range(ref.shape[0]):
            scr[table_ref[0, Z_FLIP + at]] = ref[i]
            at = at + 1
    out_ref[0] = jnp.concatenate([scr[f] for f in range(FRAMES)], axis=1)


def features_kernel(table_ref, one_ref, two_ref, four_ref, out_ref, scr):
    subs = [one_ref[0], two_ref[0], four_ref[0], four_ref[1]]
    for r in range(4):
        scr[table_ref[0, Y_FLIP + r]] = subs[r]
    out_ref[...] = jnp.concatenate([scr[s][:SUB] for s in range(4)], axis=0)


def final_kernel(table_ref, in_ref, *refs):
    mixed_ref, grad_ref = refs[FRAMES:]
    total = None
    for i in range(FRAMES):
        att = in_ref[table_ref[0, ORIGIN + i], :, 3 * WIDE :]
        term = dot(att, refs[i][...])
        total = term if total is None else total + term
    mixed_ref[0, 0] = total.astype(bf16)
    for part in range(3):
        pieces = [in_ref[f, :, part * WIDE : (part + 1) * WIDE] for f in range(FRAMES)]
        grad_ref[0, 0, :, part * D : (part + 1) * D] = jnp.concatenate(pieces, axis=1)


def shift(x, axis, count, k):
    return lax.ppermute(x, axis, [(i, (i + k) % count) for i in range(count)])


def device(z, y, f):
    return (z * 4 + y) * 8 + f


EVERY = [(z, y, f) for z in range(8) for y in range(4) for f in range(8)]


def flip(x, axis, count, mask):
    return lax.ppermute(x, axis, [(i, i ^ mask) for i in range(count)])


def turn(x):
    return lax.ppermute(x, ALL, [(device(z, y, f), device(f, y, z)) for z, y, f in EVERY])


def shards(qkv, keep, counts, grad_out, w_out):
    x_here = lax.axis_index("x").astype(jnp.int32)
    y_here = lax.axis_index("y").astype(jnp.int32)
    z_here = lax.axis_index("z").astype(jnp.int32)
    core = lax.axis_index("core").astype(jnp.int32)
    sds = jax.ShapeDtypeStruct
    swap = lambda a: shift(a, "core", 2, 1)
    table = [2 * lax.rem(x_here + dx, 4) + (core ^ dc) for dx, dc in STEPS]
    table += [2 * lax.rem(x_here + 4 - dx, 4) + (core ^ dc) for dx, dc in STEPS]
    table += [z_here ^ r for r in (0, 4, 2, 6, 1, 5, 3, 7)] + [y_here ^ r for r in (0, 2, 1, 3)]
    table = jnp.stack(table)[None]

    w_one = turn(jnp.pad(w_out, ((0, SUBP - SUB), (0, 0))))[None]
    packed = call(pack_kernel, sds((FRAMES, CAP, PACK), bf16), 3, smem=(0,))(counts, qkv, keep)
    recv = lax.all_to_all(packed, FRAME, 0, 0, tiled=True)
    w_two = flip(w_one, "z", 8, 4)
    w_four = flip(jnp.concatenate([w_one, w_two]), "z", 8, 2)
    w_eight = flip(jnp.concatenate([w_one, w_two, w_four]), "z", 8, 1)
    w_sub = call(
        columns_kernel,
        sds((1, SUBP, D), bf16),
        5,
        scratch=[VMEM((8, SUBP, WIDE), bf16)],
        smem=(0,),
    )(table, w_one, w_two, w_four, w_eight)
    w_next = flip(w_sub, "y", 4, 2)
    w_last = flip(jnp.concatenate([w_sub, w_next]), "y", 4, 1)
    g_chips = [grad_out[0, 0]]
    g_chips += [shift(g_chips[0], "x", 4, k) for k in (1, 3, 2)]
    g_all = [g for chip in g_chips for g in (chip, swap(chip))]

    grid = (FRAMES, PATCHES, PATCHES)
    slim = (FRAMES, PATCHES, WIDE)
    att, *saved = call(
        forward_kernel,
        (
            sds((FRAMES, CAP, PATCHES), bf16),
            sds((FRAMES, CAP, PATCHES), bf16),
            sds(grid, bf16),
            sds(grid, bf16),
            sds(grid, bf16),
            sds(slim, bf16),
            sds((PATCHES // GROUP, BLOCK, 2 * BLOCK), f32),
        ),
        1,
        scratch=[VMEM(slim, bf16)],
    )(recv)
    own, other = call(
        weight_kernel,
        (sds((2, SUBP, D), f32), sds((2, SUBP, D), bf16)),
        10,
        scratch=[VMEM((4, SUBP, D), f32)],
        smem=(0,),
    )(table, att, *g_all)
    other = flip(other, "y", 4, 1)
    w_last, own = lax.optimization_barrier((w_last, own))
    w_mine = call(
        features_kernel,
        sds((WIDE, D), bf16),
        4,
        scratch=[VMEM((4, SUBP, D), bf16)],
        smem=(0,),
    )(table, w_sub, w_next, w_last)
    grad_att = call(grad_att_kernel, sds((FRAMES, CAP, WIDE), bf16), 9)(w_mine, *g_all)
    other, _ = lax.optimization_barrier((other, grad_att))
    own, other = call(
        halve_kernel, (sds((1, SUBP, D), f32), sds((1, SUBP, D), bf16)), 2
    )(own, other)
    grad_att, own = lax.optimization_barrier((grad_att, own))
    grads = call(
        backward_kernel,
        sds((FRAMES, CAP, 4 * WIDE), bf16),
        9,
        scratch=[VMEM(slim, bf16)] * 4,
        smem=(0,),
    )(table, grad_att, att, *saved)
    w_chips = [w_mine] + [shift(w_mine, "x", 4, k) for k in (3, 1, 2)]
    grads, w_chips = lax.optimization_barrier((grads, w_chips))
    w_all = [w for chip in w_chips for w in (chip, swap(chip))]
    grad_back = lax.all_to_all(grads, FRAME, 0, 0, tiled=True)

    own, _ = lax.optimization_barrier((own, grads))
    own, other = call(
        planes_kernel,
        (sds((4, SUBP, WIDE), f32), sds((4, SUBP, WIDE), bf16)),
        3,
        scratch=[VMEM((8, SUBP, WIDE), f32)],
        smem=(0,),
    )(table, own, flip(other, "y", 4, 2))
    for mask, count in ((1, 2), (2, 1)):
        half = (count, SUBP, WIDE)
        own, other = call(halve_kernel, (sds(half, f32), sds(half, bf16)), 2)(
            own, flip(other, "z", 8, mask)
        )
    grad_weight = turn(call(last_kernel, sds((SUB, WIDE), f32), 2)(own, flip(other, "z", 8, 4)))

    mixed, grad_qkv = call(
        final_kernel,
        (sds((1, 1, CAP, D), bf16), sds((1, 1, CAP, 3 * D), bf16)),
        10,
        smem=(0,),
    )(table, grad_back, *w_all)
    return mixed, grad_qkv, grad_weight


def solution(mesh):
    fine = Mesh(mesh.devices.reshape(8, 4, 4, 2), ALL)
    dp = ("z", "y")
    return jax.shard_map(
        shards,
        mesh=fine,
        in_specs=(
            P(dp, FRAME, None, None),
            P(dp, FRAME, None),
            P(dp, FRAME),
            P(dp, FRAME, None, None),
            P(dp, FRAME),
        ),
        out_specs=(P(dp, FRAME, None, None), P(dp, FRAME, None, None), P(dp, FRAME)),
        check_vma=False,
    )
```

time: 382 us -> 165 us (0.43)
  the two profiles are of different devices: /device:TPU:8 before, /device:TPU:128 now
where the time goes in v1:
time: 165 us; the launch traced here: 163 us
  waiting for transfers between devices  67.9 us (41%)
  Pallas kernels  47 us (28%)
  starting transfers between devices  35.5 us (22%)
  local copies, waits for them, and re-layouts  9.37 us (6%)
  other arithmetic  1.74 us (1%)
    pallas_call x13, Pallas kernels, run(): pl.pallas_call(kernel, grid=(1,), out_shape=out_shape, in_specs=specs, ou...  47 us
    ppermute x10, waiting for transfers between devices, flip(): return lax.ppermute(x, axis, [(i, i ^ mask) for i in range(count)])  40.3 us
    ppermute x2, waiting for transfers between devices, turn(): lax.ppermute(x, ALL, [(device(z, y, f), device(f, y, z)) for z, y, f in E...  17.3 us
    ppermute x10, starting transfers between devices, flip(): return lax.ppermute(x, axis, [(i, i ^ mask) for i in range(count)])  10.4 us
    ppermute x14, waiting for transfers between devices, shift(): return lax.ppermute(x, axis, [(i, (i + k) % count) for i in range(count)])  10.3 us
    ppermute x14, starting transfers between devices, shift(): return lax.ppermute(x, axis, [(i, (i + k) % count) for i in range(count)])  9.62 us
    unnamed x39, local copies, waits for them, and re-layouts  8.71 us
    ppermute x2, starting transfers between devices, turn(): lax.ppermute(x, ALL, [(device(z, y, f), device(f, y, z)) for z, y, f in E...  7.4 us
  transfers between devices with their start and end apart: 28, of which 12 were waited for; matrix products, arithmetic and copies ran while one was open for 1% of the time, Pallas kernels for 22%

profile of v1, /device:TPU:128, one launch (start us, length us, event | category | flops | bytes accessed | tf_op | source)
XLA Modules:
  0.0 163.0 jit_solution(7459151689578191095)
XLA Ops:
  1.3 3.4 %shard_map.77 = bf16[8,192,640]{2,1,0:T(8,128)(2,1)} custom-call(s32[1,1]{1,0:T(1,128)S(6)} %copy.9.counts_ref, bf16[1,1,192,4224]{3,2,1,0:T(8,128)(2,1)} %qkv_ref.1, s32[1,1,192]{2,1,0:T(1,128)} %keep_ref.1), custom_call_target="tpu_custom_call" | custom-call | tf_op jit(solution)/shard_map/pallas_call | solution.py:61
  4.7 4.4 %all-to-all-start = ((bf16[8,192,640]{2,1,0:T(8,128)(2,1)}), bf16[8,192,640]{2,1,0:T(8,128)(2,1)S(1)}, u32[]{:S(2)}, u32[]{:S(2)}) async-start(bf16[8,192,640]{2,1,0:T(8,128)(2,1)} %shard_map.77), calls=%async_computation | async-start | bytes 3932160 | tf_op jit(solution)/shard_map/all_to_all | solution.py:288
  9.1 3.2 %collective-permute-start.9 = (bf16[192,1408]{1,0:T(8,128)(2,1)S(1)}, bf16[192,1408]{1,0:T(8,128)(2,1)S(1)}, u32[]{:S(2)}, u32[]{:S(2)}) collective-permute-start(bf16[192,1408]{1,0:T(8,128)(2,1)S(1)} %bitcast.27), channel_id=1, source_target_pairs={{0,6},{2,0},{4,2},{6,4},{1,7},{3,1},{5,3},{7,5},{8,14},{10,8},{12,... | collective-permute-start | bytes 1622024 | tf_op jit(solution)/shard_map/ppermute | solution.py:256
  14.1 2.9 %collective-permute-start = (bf16[48,176]{1,0:T(8,128)(2,1)S(1)}, bf16[48,176]{1,0:T(8,128)(2,1)S(1)}, u32[]{:S(2)}, u32[]{:S(2)}) collective-permute-start(bf16[48,176]{1,0:T(8,128)(2,1)S(1)} %pad.4), channel_id=1, source_target_pairs={{0,0},{1,32},{2,64},{3,96},{4,128},{5,160},{6,192},{7,224},{8,8},{... | collective-permute-start | bytes 50696 | tf_op jit(solution)/shard_map/ppermute | solution.py:271
  17.0 9.3 %collective-permute-done = bf16[48,176]{1,0:T(8,128)(2,1)S(1)} collective-permute-done((bf16[48,176]{1,0:T(8,128)(2,1)S(1)}, bf16[48,176]{1,0:T(8,128)(2,1)S(1)}, u32[]{:S(2)}, u32[]{:S(2)}) %collective-permute-start) | collective-permute-done | bytes 16928 | tf_op jit(solution)/shard_map/ppermute | solution.py:271
  26.3 7.7 %collective-permute-done.1.refs_1_ = bf16[1,48,176]{2,1,0:T(8,128)(2,1)S(1)} collective-permute-done((bf16[1,48,176]{2,1,0:T(8,128)(2,1)S(1)}, bf16[1,48,176]{2,1,0:T(8,128)(2,1)S(1)}, u32[]{:S(2)}, u32[]{:S(2)}) %collective-permute-start.1) | collective-permute-done | bytes 16928 | tf_op jit(solution)/shard_map/ppermute | solution.py:267
  34.1 5.1 %collective-permute-done.2.refs_2_ = bf16[2,48,176]{2,1,0:T(8,128)(2,1)S(1)} collective-permute-done((bf16[2,48,176]{2,1,0:T(8,128)(2,1)S(1)}, bf16[2,48,176]{2,1,0:T(8,128)(2,1)S(1)}, u32[]{:S(2)}, u32[]{:S(2)}) %collective-permute-start.2) | collective-permute-done | bytes 33824 | tf_op jit(solution)/shard_map/ppermute | solution.py:267
  40.0 3.9 %collective-permute-done.3.refs_3_ = bf16[4,48,176]{2,1,0:T(8,128)(2,1)S(1)} collective-permute-done((bf16[4,48,176]{2,1,0:T(8,128)(2,1)S(1)}, bf16[4,48,176]{2,1,0:T(8,128)(2,1)S(1)}, u32[]{:S(2)}, u32[]{:S(2)}) %collective-permute-start.3) | collective-permute-done | bytes 67616 | tf_op jit(solution)/shard_map/ppermute | solution.py:267
  44.6 1.8 %shard_map.76.one_ref = bf16[1,48,1408]{2,1,0:T(8,128)(2,1)} custom-call(s32[1,28]{1,0:T(1,128)} %bitcast.35, bf16[1,48,176]{2,1,0:T(8,128)(2,1)} %bitcast.34, bf16[1,48,176]{2,1,0:T(8,128)(2,1)} %copy-done.11, bf16[2,48,176]{2,1,0:T(8,128)(2,1)} %copy-done.12, bf16[4,48,176]{2,1,0:T(8,128)(2,1)} %copy-done.15), custom_call_target="tpu_custom_call" | custom-call | tf_op jit(solution)/shard_map/pallas_call | solution.py:61
  46.3 3.2 %collective-permute-start.4 = (bf16[1,48,1408]{2,1,0:T(8,128)(2,1)}, bf16[1,48,1408]{2,1,0:T(8,128)(2,1)S(1)}, u32[]{:S(2)}, u32[]{:S(2)}) collective-permute-start(bf16[1,48,1408]{2,1,0:T(8,128)(2,1)} %shard_map.76.one_ref), channel_id=1, source_target_pairs={{0,16},{8,24},{16,0},{24,8},{1,17},{9,25},{17,1},{25,9},{2,18},{10... | collective-permute-start | bytes 405512 | tf_op jit(solution)/shard_map/ppermute | solution.py:267
  50.2 8.3 %collective-permute-done.7.refs_2_ = bf16[192,1408]{1,0:T(8,128)(2,1)} collective-permute-done((bf16[192,1408]{1,0:T(8,128)(2,1)S(1)}, bf16[192,1408]{1,0:T(8,128)(2,1)}, u32[]{:S(2)}, u32[]{:S(2)}) %collective-permute-start.7) | collective-permute-done | bytes 540704 | tf_op jit(solution)/shard_map/ppermute | solution.py:256
  58.4 1.7 %pad_maximum_fusion = bf16[2,48,1408]{2,1,0:T(8,128)(2,1)} fusion(bf16[1,48,1408]{2,1,0:T(8,128)(2,1)S(1)} %collective-permute-done.4.two_ref, bf16[1,48,1408]{2,1,0:T(8,128)(2,1)} %shard_map.76.one_ref), kind=kLoop, calls=%fused_computation | loop fusion | flops 135168 | bytes 540672 | tf_op jit(solution)/shard_map/concatenate | solution.py:300
  60.1 1.6 collective-permute-start.5
  63.0 5.7 %shard_map.78 = (bf16[8,192,256]{2,1,0:T(8,128)(2,1)}, bf16[8,192,256]{2,1,0:T(8,128)(2,1)}, bf16[8,256,256]{2,1,0:T(8,128)(2,1)}, bf16[8,256,256]{2,1,0:T(8,128...) custom-call(bf16[8,192,640]{2,1,0:T(8,128)(2,1)} %copy-done.1), custom_call_target="tpu_custom_call" | custom-call | tf_op jit(solution)/shard_map/pallas_call | solution.py:61
  68.7 4.7 %shard_map.79 = (f32[2,48,1408]{2,1,0:T(8,128)}, bf16[2,48,1408]{2,1,0:T(8,128)(2,1)}) custom-call(s32[1,28]{1,0:T(1,128)} %bitcast.36, bf16[8,192,256]{2,1,0:T(8,128)(2,1)} %get-tuple-element.33.att_ref, bf16[192,1408]{1,0:T(8,128)(2,1)} %bitcast.25, bf16[192,1408]{1,0:T(8,128)(2,1)} %collective-permute-done.6.refs_1_, ...), custom_call_target="tpu_custom_call" | custom-call | tf_op jit(solution)/shard_map/pallas_call | solution.py:61
  74.1 2.0 %shard_map.80.w_ref.refs_0_ = bf16[176,1408]{1,0:T(8,128)(2,1)} custom-call(s32[1,28]{1,0:T(1,128)} %bitcast.37, bf16[1,48,1408]{2,1,0:T(8,128)(2,1)} %shard_map.76.one_ref, bf16[1,48,1408]{2,1,0:T(8,128)(2,1)} %copy-done.5, bf16[2,48,1408]{2,1,0:T(8,128)(2,1)} %copy-done.8), custom_call_target="tpu_custom_call" | custom-call | tf_op jit(solution)/shard_map/pallas_call | solution.py:61
  79.5 4.7 %shard_map.81.grad_att_ref = bf16[8,192,176]{2,1,0:T(8,128)(2,1)} custom-call(bf16[176,1408]{1,0:T(8,128)(2,1)} %shard_map.80.w_ref.refs_0_, bf16[192,1408]{1,0:T(8,128)(2,1)} %bitcast.26, bf16[192,1408]{1,0:T(8,128)(2,1)} %collective-permute-done.6.refs_1_, bf16[192,1408]{1,0:T(8,128)(2,1)} %collective-permute-done.7.refs_2_, ...), custom_call_target="tpu_custom_call" | custom-call | tf_op jit(solution)/shard_map/pallas_call | solution.py:61
  84.2 3.1 %collective-permute-done.13.in_ref = bf16[2,48,1408]{2,1,0:T(8,128)(2,1)S(1)} collective-permute-done((bf16[2,48,1408]{2,1,0:T(8,128)(2,1)}, bf16[2,48,1408]{2,1,0:T(8,128)(2,1)S(1)}, u32[]{:S(2)}, u32[]{:S(2)}) %collective-permute-start.13) | collective-permute-done | bytes 270368 | tf_op jit(solution)/shard_map/ppermute | solution.py:267
  88.0 1.9 %shard_map.82 = (f32[1,48,1408]{2,1,0:T(8,128)}, bf16[1,48,1408]{2,1,0:T(8,128)(2,1)}) custom-call(f32[2,48,1408]{2,1,0:T(8,128)} %get-tuple-element.36.own_ref, bf16[2,48,1408]{2,1,0:T(8,128)(2,1)} %copy-done.9), custom_call_target="tpu_custom_call" | custom-call | tf_op jit(solution)/shard_map/pallas_call | solution.py:61
  89.9 10.9 %shard_map.83 = bf16[8,192,704]{2,1,0:T(8,128)(2,1)} custom-call(s32[1,28]{1,0:T(1,128)} %bitcast.38, bf16[8,192,176]{2,1,0:T(8,128)(2,1)} %shard_map.81.grad_att_ref, bf16[8,192,256]{2,1,0:T(8,128)(2,1)} %get-tuple-element.33.att_ref, bf16[8,192,256]{2,1,0:T(8,128)(2,1)} %get-tuple-element.41.hot_ref, bf16[8,256,256]{2,1,0:T(8,128)(2,1)} %get-tuple-element.42.hot_t_ref, ...), custom_call_target="tpu_custom_call" | custom-call | tf_op jit(solution)/shard_map/pallas_call | solution.py:61
  100.8 2.0 %collective-permute-done.15.refs_4_ = bf16[176,1408]{1,0:T(8,128)(2,1)} collective-permute-done((bf16[176,1408]{1,0:T(8,128)(2,1)}, bf16[176,1408]{1,0:T(8,128)(2,1)}, u32[]{:S(2)}, u32[]{:S(2)}) %collective-permute-start.15) | collective-permute-done | bytes 495648 | tf_op jit(solution)/shard_map/ppermute | solution.py:256
  102.9 3.6 %all-to-all-start.1 = ((bf16[8,192,704]{2,1,0:T(8,128)(2,1)}), bf16[8,192,704]{2,1,0:T(8,128)(2,1)S(1)}, u32[]{:S(2)}, u32[]{:S(2)}) async-start(bf16[8,192,704]{2,1,0:T(8,128)(2,1)} %shard_map.83), calls=%async_computation.1 | async-start | bytes 4718592 | tf_op jit(solution)/shard_map/all_to_all | solution.py:353
  107.6 2.9 %collective-permute-start.21 = (bf16[1,48,1408]{2,1,0:T(8,128)(2,1)}, bf16[1,48,1408]{2,1,0:T(8,128)(2,1)S(1)}, u32[]{:S(2)}, u32[]{:S(2)}) collective-permute-start(bf16[1,48,1408]{2,1,0:T(8,128)(2,1)} %get-tuple-element.56), channel_id=1, source_target_pairs={{0,16},{8,24},{16,0},{24,8},{1,17},{9,25},{17,1},{25,9},{2,18},{10... | collective-permute-start | bytes 405512 | tf_op jit(solution)/shard_map/ppermute | solution.py:267
  110.5 4.6 %collective-permute-done.21.in_ref = bf16[1,48,1408]{2,1,0:T(8,128)(2,1)S(1)} collective-permute-done((bf16[1,48,1408]{2,1,0:T(8,128)(2,1)}, bf16[1,48,1408]{2,1,0:T(8,128)(2,1)S(1)}, u32[]{:S(2)}, u32[]{:S(2)}) %collective-permute-start.21) | collective-permute-done | bytes 135200 | tf_op jit(solution)/shard_map/ppermute | solution.py:267
  115.8 1.9 %shard_map.85 = (f32[4,48,176]{2,1,0:T(8,128)}, bf16[4,48,176]{2,1,0:T(8,128)(2,1)}) custom-call(s32[1,28]{1,0:T(1,128)} %bitcast.39, f32[1,48,1408]{2,1,0:T(8,128)} %get-tuple-element.55.own_ref, bf16[1,48,1408]{2,1,0:T(8,128)(2,1)} %copy-done.13), custom_call_target="tpu_custom_call" | custom-call | tf_op jit(solution)/shard_map/pallas_call | solution.py:61
  118.7 3.8 %collective-permute-done.22.in_ref = bf16[4,48,176]{2,1,0:T(8,128)(2,1)S(1)} collective-permute-done((bf16[4,48,176]{2,1,0:T(8,128)(2,1)}, bf16[4,48,176]{2,1,0:T(8,128)(2,1)S(1)}, u32[]{:S(2)}, u32[]{:S(2)}) %collective-permute-start.22) | collective-permute-done | bytes 67616 | tf_op jit(solution)/shard_map/ppermute | solution.py:267
  123.1 1.7 %shard_map.86 = (f32[2,48,176]{2,1,0:T(8,128)}, bf16[2,48,176]{2,1,0:T(8,128)(2,1)}) custom-call(f32[4,48,176]{2,1,0:T(8,128)} %get-tuple-element.57.own_ref, bf16[4,48,176]{2,1,0:T(8,128)(2,1)} %copy-done.14), custom_call_target="tpu_custom_call" | custom-call | tf_op jit(solution)/shard_map/pallas_call | solution.py:61
  125.8 4.2 %collective-permute-done.23.in_ref = bf16[2,48,176]{2,1,0:T(8,128)(2,1)S(1)} collective-permute-done((bf16[2,48,176]{2,1,0:T(8,128)(2,1)}, bf16[2,48,176]{2,1,0:T(8,128)(2,1)S(1)}, u32[]{:S(2)}, u32[]{:S(2)}) %collective-permute-start.23) | collective-permute-done | bytes 33824 | tf_op jit(solution)/shard_map/ppermute | solution.py:267
  132.1 7.9 %collective-permute-done.24.in_ref = bf16[1,48,176]{2,1,0:T(8,128)(2,1)S(1)} collective-permute-done((bf16[1,48,176]{2,1,0:T(8,128)(2,1)}, bf16[1,48,176]{2,1,0:T(8,128)(2,1)S(1)}, u32[]{:S(2)}, u32[]{:S(2)}) %collective-permute-start.24) | collective-permute-done | bytes 16928 | tf_op jit(solution)/shard_map/ppermute | solution.py:267
  142.1 4.5 %collective-permute-start.25 = (f32[44,176]{1,0:T(8,128)}, f32[44,176]{1,0:T(8,128)S(1)}, u32[]{:S(2)}, u32[]{:S(2)}) collective-permute-start(f32[44,176]{1,0:T(8,128)} %shard_map.88), channel_id=1, source_target_pairs={{0,0},{1,32},{2,64},{3,96},{4,128},{5,160},{6,192},{7,224},{8,8},{... | collective-permute-start | bytes 92936 | tf_op jit(solution)/shard_map/ppermute | solution.py:271
  146.6 8.0 %collective-permute-done.25 = f32[44,176]{1,0:T(8,128)S(1)} collective-permute-done((f32[44,176]{1,0:T(8,128)}, f32[44,176]{1,0:T(8,128)S(1)}, u32[]{:S(2)}, u32[]{:S(2)}) %collective-permute-start.25) | collective-permute-done | bytes 31008 | tf_op jit(solution)/shard_map/ppermute | solution.py:271
  156.9 5.5 %shard_map.84 = (bf16[1,1,192,1408]{3,2,1,0:T(8,128)(2,1)}, bf16[1,1,192,4224]{3,2,1,0:T(8,128)(2,1)}) custom-call(s32[1,28]{1,0:T(1,128)} %bitcast.40, bf16[8,192,704]{2,1,0:T(8,128)(2,1)} %copy-done, bf16[176,1408]{1,0:T(8,128)(2,1)} %shard_map.80.w_ref.refs_0_, bf16[176,1408]{1,0:T(8,128)(2,1)} %copy-done.7, bf16[176,1408]{1,0:T(8,128)(2,1)} %copy-done.6, ...), custom_call_target="tpu_custom_call" | custom-call | tf_op jit(solution)/shard_map/pallas_call | solution.py:61
  (81 shorter events, 21.5 us)
Async XLA Ops:
  4.7 57.0 %all-to-all-start = ((bf16[8,192,640]{2,1,0:T(8,128)(2,1)}), bf16[8,192,640]{2,1,0:T(8,128)(2,1)S(1)}, u32[]{:S(2)}, u32[]{:S(2)}) async-start(bf16[8,192,640]{2,1,0:T(8,128)(2,1)} %shard_map.77), calls=%async_computation | async-start | bytes 3932160 | tf_op jit(solution)/shard_map/all_to_all | solution.py:288
  9.1 40.4 %collective-permute-start.9 = (bf16[192,1408]{1,0:T(8,128)(2,1)S(1)}, bf16[192,1408]{1,0:T(8,128)(2,1)S(1)}, u32[]{:S(2)}, u32[]{:S(2)}) collective-permute-start(bf16[192,1408]{1,0:T(8,128)(2,1)S(1)} %bitcast.27), channel_id=1, source_target_pairs={{0,6},{2,0},{4,2},{6,4},{1,7},{3,1},{5,3},{7,5},{8,14},{10,8},{12,... | collective-permute-start | bytes 1622024 | tf_op jit(solution)/shard_map/ppermute | solution.py:256
  12.3 37.7 %collective-permute-start.11 = (bf16[192,1408]{1,0:T(8,128)(2,1)S(1)}, bf16[192,1408]{1,0:T(8,128)(2,1)}, u32[]{:S(2)}, u32[]{:S(2)}) collective-permute-start(bf16[192,1408]{1,0:T(8,128)(2,1)S(1)} %bitcast.28), channel_id=1, source_target_pairs={{0,4},{2,6},{4,0},{6,2},{1,5},{3,7},{5,1},{7,3},{8,12},{10,14},{12... | collective-permute-start | bytes 1622024 | tf_op jit(solution)/shard_map/ppermute | solution.py:256
  13.2 45.2 %collective-permute-start.7 = (bf16[192,1408]{1,0:T(8,128)(2,1)S(1)}, bf16[192,1408]{1,0:T(8,128)(2,1)}, u32[]{:S(2)}, u32[]{:S(2)}) collective-permute-start(bf16[192,1408]{1,0:T(8,128)(2,1)S(1)} %bitcast.29), channel_id=1, source_target_pairs={{0,2},{2,4},{4,6},{6,0},{1,3},{3,5},{5,7},{7,1},{8,10},{10,12},{12... | collective-permute-start | bytes 1622024 | tf_op jit(solution)/shard_map/ppermute | solution.py:256
  14.1 12.2 %collective-permute-start = (bf16[48,176]{1,0:T(8,128)(2,1)S(1)}, bf16[48,176]{1,0:T(8,128)(2,1)S(1)}, u32[]{:S(2)}, u32[]{:S(2)}) collective-permute-start(bf16[48,176]{1,0:T(8,128)(2,1)S(1)} %pad.4), channel_id=1, source_target_pairs={{0,0},{1,32},{2,64},{3,96},{4,128},{5,160},{6,192},{7,224},{8,8},{... | collective-permute-start | bytes 50696 | tf_op jit(solution)/shard_map/ppermute | solution.py:271
  26.3 17.7 %copy-start.10 = (bf16[48,176]{1,0:T(8,128)(2,1)}, bf16[48,176]{1,0:T(8,128)(2,1)S(1)}, u32[]{:S(2)}) copy-start(bf16[48,176]{1,0:T(8,128)(2,1)S(1)} %collective-permute-done) | copy-start | bytes 50692
  26.3 7.7 %collective-permute-start.1 = (bf16[1,48,176]{2,1,0:T(8,128)(2,1)S(1)}, bf16[1,48,176]{2,1,0:T(8,128)(2,1)S(1)}, u32[]{:S(2)}, u32[]{:S(2)}) collective-permute-start(bf16[1,48,176]{2,1,0:T(8,128)(2,1)S(1)} %bitcast.31), channel_id=1, source_target_pairs={{0,128},{32,160},{64,192},{96,224},{128,0},{160,32},{192,64},{224,... | collective-permute-start | bytes 50696 | tf_op jit(solution)/shard_map/ppermute | solution.py:267
  34.0 9.9 %copy-start.11 = (bf16[1,48,176]{2,1,0:T(8,128)(2,1)}, bf16[1,48,176]{2,1,0:T(8,128)(2,1)S(1)}, u32[]{:S(2)}) copy-start(bf16[1,48,176]{2,1,0:T(8,128)(2,1)S(1)} %collective-permute-done.1.refs_1_) | copy-start | bytes 50692
  34.0 5.2 %collective-permute-start.2 = (bf16[2,48,176]{2,1,0:T(8,128)(2,1)S(1)}, bf16[2,48,176]{2,1,0:T(8,128)(2,1)S(1)}, u32[]{:S(2)}, u32[]{:S(2)}) collective-permute-start(bf16[2,48,176]{2,1,0:T(8,128)(2,1)S(1)} %pad_maximum_fusion.2), channel_id=1, source_target_pairs={{0,64},{32,96},{64,0},{96,32},{128,192},{160,224},{192,128},{224,1... | collective-permute-start | bytes 101384 | tf_op jit(solution)/shard_map/ppermute | solution.py:267
  39.2 4.7 %collective-permute-start.3 = (bf16[4,48,176]{2,1,0:T(8,128)(2,1)S(1)}, bf16[4,48,176]{2,1,0:T(8,128)(2,1)S(1)}, u32[]{:S(2)}, u32[]{:S(2)}) collective-permute-start(bf16[4,48,176]{2,1,0:T(8,128)(2,1)S(1)} %pad_maximum_fusion.1), channel_id=1, source_target_pairs={{0,32},{32,0},{64,96},{96,64},{128,160},{160,128},{192,224},{224,1... | collective-permute-start | bytes 202760 | tf_op jit(solution)/shard_map/ppermute | solution.py:267
  46.3 12.1 %collective-permute-start.4 = (bf16[1,48,1408]{2,1,0:T(8,128)(2,1)}, bf16[1,48,1408]{2,1,0:T(8,128)(2,1)S(1)}, u32[]{:S(2)}, u32[]{:S(2)}) collective-permute-start(bf16[1,48,1408]{2,1,0:T(8,128)(2,1)} %shard_map.76.one_ref), channel_id=1, source_target_pairs={{0,16},{8,24},{16,0},{24,8},{1,17},{9,25},{17,1},{25,9},{2,18},{10... | collective-permute-start | bytes 405512 | tf_op jit(solution)/shard_map/ppermute | solution.py:267
  49.5 19.1 %collective-permute-start.6 = (bf16[192,1408]{1,0:T(8,128)(2,1)S(1)}, bf16[192,1408]{1,0:T(8,128)(2,1)}, u32[]{:S(2)}, u32[]{:S(2)}) collective-permute-start(bf16[192,1408]{1,0:T(8,128)(2,1)S(1)} %bitcast.30), channel_id=1, source_target_pairs={{0,1},{1,0},{2,3},{3,2},{4,5},{5,4},{6,7},{7,6},{8,9},{9,8},{10,11... | collective-permute-start | bytes 1622024 | tf_op jit(solution)/shard_map/ppermute | solution.py:256
  49.5 19.2 %copy-start.4 = (bf16[192,1408]{1,0:T(8,128)(2,1)}, bf16[192,1408]{1,0:T(8,128)(2,1)S(1)}, u32[]{:S(2)}) copy-start(bf16[192,1408]{1,0:T(8,128)(2,1)S(1)} %collective-permute-done.9.refs_4_) | copy-start | bytes 1622020
  49.5 19.1 %collective-permute-start.10 = (bf16[192,1408]{1,0:T(8,128)(2,1)S(1)}, bf16[192,1408]{1,0:T(8,128)(2,1)}, u32[]{:S(2)}, u32[]{:S(2)}) collective-permute-start(bf16[192,1408]{1,0:T(8,128)(2,1)S(1)} %collective-permute-done.9.refs_4_), channel_id=1, source_target_pairs={{0,1},{1,0},{2,3},{3,2},{4,5},{5,4},{6,7},{7,6},{8,9},{9,8},{10,11... | collective-permute-start | bytes 1622024 | tf_op jit(solution)/shard_map/ppermute | solution.py:256
  50.1 18.6 %collective-permute-start.12 = (bf16[192,1408]{1,0:T(8,128)(2,1)}, bf16[192,1408]{1,0:T(8,128)(2,1)}, u32[]{:S(2)}, u32[]{:S(2)}) collective-permute-start(bf16[192,1408]{1,0:T(8,128)(2,1)} %collective-permute-done.11.refs_6_), channel_id=1, source_target_pairs={{0,1},{1,0},{2,3},{3,2},{4,5},{5,4},{6,7},{7,6},{8,9},{9,8},{10,11... | collective-permute-start | bytes 1622024 | tf_op jit(solution)/shard_map/ppermute | solution.py:256
  58.4 10.3 %collective-permute-start.8 = (bf16[192,1408]{1,0:T(8,128)(2,1)}, bf16[192,1408]{1,0:T(8,128)(2,1)}, u32[]{:S(2)}, u32[]{:S(2)}) collective-permute-start(bf16[192,1408]{1,0:T(8,128)(2,1)} %collective-permute-done.7.refs_2_), channel_id=1, source_target_pairs={{0,1},{1,0},{2,3},{3,2},{4,5},{5,4},{6,7},{7,6},{8,9},{9,8},{10,11... | collective-permute-start | bytes 1622024 | tf_op jit(solution)/shard_map/ppermute | solution.py:256
  58.4 15.0 %copy-start.5 = (bf16[1,48,1408]{2,1,0:T(8,128)(2,1)}, bf16[1,48,1408]{2,1,0:T(8,128)(2,1)S(1)}, u32[]{:S(2)}) copy-start(bf16[1,48,1408]{2,1,0:T(8,128)(2,1)S(1)} %collective-permute-done.4.two_ref) | copy-start | bytes 405508
  60.1 13.3 %collective-permute-start.5 = (bf16[2,48,1408]{2,1,0:T(8,128)(2,1)}, bf16[2,48,1408]{2,1,0:T(8,128)(2,1)S(1)}, u32[]{:S(2)}, u32[]{:S(2)}) collective-permute-start(bf16[2,48,1408]{2,1,0:T(8,128)(2,1)} %pad_maximum_fusion), channel_id=1, source_target_pairs={{0,8},{8,0},{16,24},{24,16},{1,9},{9,1},{17,25},{25,17},{2,10},{10... | collective-permute-start | bytes 811016 | tf_op jit(solution)/shard_map/ppermute | solution.py:267
  76.1 24.7 %collective-permute-start.14 = (bf16[176,1408]{1,0:T(8,128)(2,1)}, bf16[176,1408]{1,0:T(8,128)(2,1)S(1)}, u32[]{:S(2)}, u32[]{:S(2)}) collective-permute-start(bf16[176,1408]{1,0:T(8,128)(2,1)} %shard_map.80.w_ref.refs_0_), channel_id=1, source_target_pairs={{0,6},{2,0},{4,2},{6,4},{1,7},{3,1},{5,3},{7,5},{8,14},{10,8},{12,... | collective-permute-start | bytes 1486856 | tf_op jit(solution)/shard_map/ppermute | solution.py:256
  77.6 25.2 %collective-permute-start.15 = (bf16[176,1408]{1,0:T(8,128)(2,1)}, bf16[176,1408]{1,0:T(8,128)(2,1)}, u32[]{:S(2)}, u32[]{:S(2)}) collective-permute-start(bf16[176,1408]{1,0:T(8,128)(2,1)} %shard_map.80.w_ref.refs_0_), channel_id=1, source_target_pairs={{0,2},{2,4},{4,6},{6,0},{1,3},{3,5},{5,7},{7,1},{8,10},{10,12},{12... | collective-permute-start | bytes 1486856 | tf_op jit(solution)/shard_map/ppermute | solution.py:256
  78.2 24.7 %collective-permute-start.16 = (bf16[176,1408]{1,0:T(8,128)(2,1)}, bf16[176,1408]{1,0:T(8,128)(2,1)}, u32[]{:S(2)}, u32[]{:S(2)}) collective-permute-start(bf16[176,1408]{1,0:T(8,128)(2,1)} %shard_map.80.w_ref.refs_0_), channel_id=1, source_target_pairs={{0,4},{2,6},{4,0},{6,2},{1,5},{3,7},{5,1},{7,3},{8,12},{10,14},{12... | collective-permute-start | bytes 1486856 | tf_op jit(solution)/shard_map/ppermute | solution.py:256
  79.1 8.2 %collective-permute-start.13 = (bf16[2,48,1408]{2,1,0:T(8,128)(2,1)}, bf16[2,48,1408]{2,1,0:T(8,128)(2,1)S(1)}, u32[]{:S(2)}, u32[]{:S(2)}) collective-permute-start(bf16[2,48,1408]{2,1,0:T(8,128)(2,1)} %get-tuple-element.37), channel_id=1, source_target_pairs={{0,8},{8,0},{16,24},{24,16},{1,9},{9,1},{17,25},{25,17},{2,10},{10... | collective-permute-start | bytes 811016 | tf_op jit(solution)/shard_map/ppermute | solution.py:267
  102.9 52.6 %all-to-all-start.1 = ((bf16[8,192,704]{2,1,0:T(8,128)(2,1)}), bf16[8,192,704]{2,1,0:T(8,128)(2,1)S(1)}, u32[]{:S(2)}, u32[]{:S(2)}) async-start(bf16[8,192,704]{2,1,0:T(8,128)(2,1)} %shard_map.83), calls=%async_computation.1 | async-start | bytes 4718592 | tf_op jit(solution)/shard_map/all_to_all | solution.py:353
  106.5 48.1 %collective-permute-start.17 = (bf16[176,1408]{1,0:T(8,128)(2,1)S(1)}, bf16[176,1408]{1,0:T(8,128)(2,1)S(1)}, u32[]{:S(2)}, u32[]{:S(2)}) collective-permute-start(bf16[176,1408]{1,0:T(8,128)(2,1)S(1)} %copy-done.2), channel_id=1, source_target_pairs={{0,1},{1,0},{2,3},{3,2},{4,5},{5,4},{6,7},{7,6},{8,9},{9,8},{10,11... | collective-permute-start | bytes 1486856 | tf_op jit(solution)/shard_map/ppermute | solution.py:256
  106.9 47.7 %collective-permute-start.18 = (bf16[176,1408]{1,0:T(8,128)(2,1)S(1)}, bf16[176,1408]{1,0:T(8,128)(2,1)}, u32[]{:S(2)}, u32[]{:S(2)}) collective-permute-start(bf16[176,1408]{1,0:T(8,128)(2,1)S(1)} %collective-permute-done.14.refs_2_), channel_id=1, source_target_pairs={{0,1},{1,0},{2,3},{3,2},{4,5},{5,4},{6,7},{7,6},{8,9},{9,8},{10,11... | collective-permute-start | bytes 1486856 | tf_op jit(solution)/shard_map/ppermute | solution.py:256
  107.1 47.5 %collective-permute-start.19 = (bf16[176,1408]{1,0:T(8,128)(2,1)}, bf16[176,1408]{1,0:T(8,128)(2,1)}, u32[]{:S(2)}, u32[]{:S(2)}) collective-permute-start(bf16[176,1408]{1,0:T(8,128)(2,1)} %collective-permute-done.15.refs_4_), channel_id=1, source_target_pairs={{0,1},{1,0},{2,3},{3,2},{4,5},{5,4},{6,7},{7,6},{8,9},{9,8},{10,11... | collective-permute-start | bytes 1486856 | tf_op jit(solution)/shard_map/ppermute | solution.py:256
  107.4 48.0 %collective-permute-start.20 = (bf16[176,1408]{1,0:T(8,128)(2,1)}, bf16[176,1408]{1,0:T(8,128)(2,1)}, u32[]{:S(2)}, u32[]{:S(2)}) collective-permute-start(bf16[176,1408]{1,0:T(8,128)(2,1)} %collective-permute-done.16.refs_6_), channel_id=1, source_target_pairs={{0,1},{1,0},{2,3},{3,2},{4,5},{5,4},{6,7},{7,6},{8,9},{9,8},{10,11... | collective-permute-start | bytes 1486856 | tf_op jit(solution)/shard_map/ppermute | solution.py:256
  107.6 7.5 %collective-permute-start.21 = (bf16[1,48,1408]{2,1,0:T(8,128)(2,1)}, bf16[1,48,1408]{2,1,0:T(8,128)(2,1)S(1)}, u32[]{:S(2)}, u32[]{:S(2)}) collective-permute-start(bf16[1,48,1408]{2,1,0:T(8,128)(2,1)} %get-tuple-element.56), channel_id=1, source_target_pairs={{0,16},{8,24},{16,0},{24,8},{1,17},{9,25},{17,1},{25,9},{2,18},{10... | collective-permute-start | bytes 405512 | tf_op jit(solution)/shard_map/ppermute | solution.py:267
  117.7 4.8 %collective-permute-start.22 = (bf16[4,48,176]{2,1,0:T(8,128)(2,1)}, bf16[4,48,176]{2,1,0:T(8,128)(2,1)S(1)}, u32[]{:S(2)}, u32[]{:S(2)}) collective-permute-start(bf16[4,48,176]{2,1,0:T(8,128)(2,1)} %get-tuple-element.58), channel_id=1, source_target_pairs={{0,32},{32,0},{64,96},{96,64},{128,160},{160,128},{192,224},{224,1... | collective-permute-start | bytes 202760 | tf_op jit(solution)/shard_map/ppermute | solution.py:267
  124.8 5.2 %collective-permute-start.23 = (bf16[2,48,176]{2,1,0:T(8,128)(2,1)}, bf16[2,48,176]{2,1,0:T(8,128)(2,1)S(1)}, u32[]{:S(2)}, u32[]{:S(2)}) collective-permute-start(bf16[2,48,176]{2,1,0:T(8,128)(2,1)} %get-tuple-element.60), channel_id=1, source_target_pairs={{0,64},{32,96},{64,0},{96,32},{128,192},{160,224},{192,128},{224,1... | collective-permute-start | bytes 101384 | tf_op jit(solution)/shard_map/ppermute | solution.py:267
  132.1 7.9 %collective-permute-start.24 = (bf16[1,48,176]{2,1,0:T(8,128)(2,1)}, bf16[1,48,176]{2,1,0:T(8,128)(2,1)S(1)}, u32[]{:S(2)}, u32[]{:S(2)}) collective-permute-start(bf16[1,48,176]{2,1,0:T(8,128)(2,1)} %get-tuple-element.62), channel_id=1, source_target_pairs={{0,128},{32,160},{64,192},{96,224},{128,0},{160,32},{192,64},{224,... | collective-permute-start | bytes 50696 | tf_op jit(solution)/shard_map/ppermute | solution.py:267
  142.1 12.5 %collective-permute-start.25 = (f32[44,176]{1,0:T(8,128)}, f32[44,176]{1,0:T(8,128)S(1)}, u32[]{:S(2)}, u32[]{:S(2)}) collective-permute-start(f32[44,176]{1,0:T(8,128)} %shard_map.88), channel_id=1, source_target_pairs={{0,0},{1,32},{2,64},{3,96},{4,128},{5,160},{6,192},{7,224},{8,8},{... | collective-permute-start | bytes 92936 | tf_op jit(solution)/shard_map/ppermute | solution.py:271
  (15 other events, 38.4 us)

commit v2 on v1

--- a/solution.py
+++ b/solution.py
@@ -17,7 +17,6 @@
 WIDE = D // FRAMES
 HEAD = D // HEADS
 SUB = 44
-SUBP = 48
 PACK = 640
 GROUP = 16
 BLOCK = GROUP * FRAMES
@@ -30,7 +29,7 @@
 STEPS = [(0, 0), (0, 1), (3, 0), (3, 1), (1, 0), (1, 1), (2, 0), (2, 1)]
 ALL = ("z", "y", "x", "core")
 FRAME = ("x", "core")
-WHERE, ORIGIN, Z_FLIP, Y_FLIP = 0, 8, 16, 24
+WHERE, ORIGIN, Z_FLIP, Y_FLIP, Y_NEXT = 0, 8, 16, 24, 28
 
 
 def dot(a, b):
@@ -65,7 +64,7 @@
             in_specs=specs,
             out_specs=jax.tree.map(lambda s: spec(s.shape), out_shape),
             scratch_shapes=list(scratch),
-            compiler_params=pltpu.CompilerParams(vmem_limit_bytes=60 * 1024 * 1024),
+            compiler_params=pltpu.CompilerParams(vmem_limit_bytes=32 * 1024 * 1024),
             cost_estimate=pl.CostEstimate(flops=flops, bytes_accessed=0, transcendentals=0),
         )(*args)
 
@@ -190,27 +189,28 @@
 
 
 def weight_kernel(table_ref, att_ref, *refs):
-    keep_ref, send_ref, scr = refs[FRAMES:]
+    out_refs, scr = refs[FRAMES : FRAMES + 4], refs[FRAMES + 4]
     total = None
     for i in range(FRAMES):
         term = t_dot(att_ref[table_ref[0, WHERE + i]][:, :WIDE], refs[i][...])
         total = term if total is None else total + term
-    down = jnp.zeros((SUBP - SUB, D), f32)
     for s in range(4):
-        scr[s] = jnp.concatenate([total[SUB * s : SUB * (s + 1)], down], axis=0)
-    for r in range(2):
-        keep_ref[r] = scr[table_ref[0, Y_FLIP + r]]
-        send_ref[r] = scr[table_ref[0, Y_FLIP + 2 + r]].astype(bf16)
+        scr[s] = total[SUB * s : SUB * (s + 1)]
+    for k in range(4):
+        out_refs[k][...] = scr[table_ref[0, Y_NEXT + k]].astype(out_refs[k].dtype)
 
 
 def halve_kernel(own_ref, in_ref, keep_ref, send_ref):
     half = own_ref.shape[0] // 2
     keep_ref[...] = own_ref[:half] + in_ref[:half].astype(f32)
-    send_ref[...] = (own_ref[half:] + in_ref[half:].astype(f32)).astype(bf16)
-
-
-def planes_kernel(table_ref, own_ref, in_ref, keep_ref, send_ref, scr):
-    total = own_ref[0] + in_ref[0].astype(f32)
+    send_ref[...] = (own_ref[half:] + in_ref[half:].astype(f32)).astype(send_ref.dtype)
+
+
+def planes_kernel(table_ref, *refs):
+    keep_ref, send_ref, scr = refs[4:]
+    total = refs[0][...]
+    for k in range(1, 4):
+        total = total + refs[k][...].astype(f32)
     for f in range(FRAMES):
         scr[f] = total[:, WIDE * f : WIDE * (f + 1)]
     for r in range(4):
@@ -218,8 +218,8 @@
         send_ref[r] = scr[table_ref[0, Z_FLIP + 4 + r]].astype(bf16)
 
 
-def last_kernel(own_ref, in_ref, out_ref):
-    out_ref[...] = ((own_ref[0] + in_ref[0].astype(f32)) * (1.0 / 32))[:SUB]
+def last_kernel(one_ref, two_ref, out_ref):
+    out_ref[...] = (one_ref[...] + two_ref[...]) * (1.0 / 32)
 
 
 def columns_kernel(table_ref, *refs):
@@ -236,7 +236,7 @@
     subs = [one_ref[0], two_ref[0], four_ref[0], four_ref[1]]
     for r in range(4):
         scr[table_ref[0, Y_FLIP + r]] = subs[r]
-    out_ref[...] = jnp.concatenate([scr[s][:SUB] for s in range(4)], axis=0)
+    out_ref[...] = jnp.concatenate([scr[s] for s in range(4)], axis=0)
 
 
 def final_kernel(table_ref, in_ref, *refs):
@@ -267,8 +267,14 @@
     return lax.ppermute(x, axis, [(i, i ^ mask) for i in range(count)])
 
 
-def turn(x):
-    return lax.ppermute(x, ALL, [(device(z, y, f), device(f, y, z)) for z, y, f in EVERY])
+def turn(x, mask=0):
+    pairs = [(device(z, y, f), device(f, y, z ^ mask)) for z, y, f in EVERY]
+    return lax.ppermute(x, ALL, pairs)
+
+
+def turn_back(x, mask):
+    pairs = [(device(z, y, f), device(f ^ mask, y, z)) for z, y, f in EVERY]
+    return lax.ppermute(x, ALL, pairs)
 
 
 def shards(qkv, keep, counts, grad_out, w_out):
@@ -281,27 +287,29 @@
     table = [2 * lax.rem(x_here + dx, 4) + (core ^ dc) for dx, dc in STEPS]
     table += [2 * lax.rem(x_here + 4 - dx, 4) + (core ^ dc) for dx, dc in STEPS]
     table += [z_here ^ r for r in (0, 4, 2, 6, 1, 5, 3, 7)] + [y_here ^ r for r in (0, 2, 1, 3)]
+    table += [lax.rem(y_here + k, 4) for k in range(4)]
     table = jnp.stack(table)[None]
 
-    w_one = turn(jnp.pad(w_out, ((0, SUBP - SUB), (0, 0))))[None]
+    w_here = w_out[None]
+    w_one, w_two = turn_back(w_here, 0), turn_back(w_here, 4)
     packed = call(pack_kernel, sds((FRAMES, CAP, PACK), bf16), 3, smem=(0,))(counts, qkv, keep)
+    packed, g_own = lax.optimization_barrier((packed, grad_out[0, 0]))
+    g_chips = [g_own]
+    g_chips += [shift(g_chips[0], "x", 4, k) for k in (1, 3, 2)]
+    packed, g_chips, w_one, w_two = lax.optimization_barrier((packed, g_chips, w_one, w_two))
     recv = lax.all_to_all(packed, FRAME, 0, 0, tiled=True)
-    w_two = flip(w_one, "z", 8, 4)
+    g_all = [g for chip in g_chips for g in (chip, swap(chip))]
     w_four = flip(jnp.concatenate([w_one, w_two]), "z", 8, 2)
     w_eight = flip(jnp.concatenate([w_one, w_two, w_four]), "z", 8, 1)
     w_sub = call(
         columns_kernel,
-        sds((1, SUBP, D), bf16),
+        sds((1, SUB, D), bf16),
         5,
-        scratch=[VMEM((8, SUBP, WIDE), bf16)],
+        scratch=[VMEM((8, SUB, WIDE), bf16)],
         smem=(0,),
     )(table, w_one, w_two, w_four, w_eight)
     w_next = flip(w_sub, "y", 4, 2)
     w_last = flip(jnp.concatenate([w_sub, w_next]), "y", 4, 1)
-    g_chips = [grad_out[0, 0]]
-    g_chips += [shift(g_chips[0], "x", 4, k) for k in (1, 3, 2)]
-    g_all = [g for chip in g_chips for g in (chip, swap(chip))]
-
     grid = (FRAMES, PATCHES, PATCHES)
     slim = (FRAMES, PATCHES, WIDE)
     att, *saved = call(
@@ -318,27 +326,23 @@
         1,
         scratch=[VMEM(slim, bf16)],
     )(recv)
-    own, other = call(
-        weight_kernel,
-        (sds((2, SUBP, D), f32), sds((2, SUBP, D), bf16)),
-        10,
-        scratch=[VMEM((4, SUBP, D), f32)],
-        smem=(0,),
-    )(table, att, *g_all)
-    other = flip(other, "y", 4, 1)
-    w_last, own = lax.optimization_barrier((w_last, own))
+    w_last, att = lax.optimization_barrier((w_last, att))
     w_mine = call(
         features_kernel,
         sds((WIDE, D), bf16),
         4,
-        scratch=[VMEM((4, SUBP, D), bf16)],
+        scratch=[VMEM((4, SUB, D), bf16)],
         smem=(0,),
     )(table, w_sub, w_next, w_last)
     grad_att = call(grad_att_kernel, sds((FRAMES, CAP, WIDE), bf16), 9)(w_mine, *g_all)
-    other, _ = lax.optimization_barrier((other, grad_att))
-    own, other = call(
-        halve_kernel, (sds((1, SUBP, D), f32), sds((1, SUBP, D), bf16)), 2
-    )(own, other)
+    own, *other = call(
+        weight_kernel,
+        (sds((SUB, D), f32),) + (sds((SUB, D), bf16),) * 3,
+        10,
+        scratch=[VMEM((4, SUB, D), f32)],
+        smem=(0,),
+    )(table, att, *g_all)
+    other = [shift(piece, "y", 4, k) for k, piece in zip((1, 2, 3), other)]
     grad_att, own = lax.optimization_barrier((grad_att, own))
     grads = call(
         backward_kernel,
@@ -347,32 +351,36 @@
         scratch=[VMEM(slim, bf16)] * 4,
         smem=(0,),
     )(table, grad_att, att, *saved)
+    other, grads = lax.optimization_barrier((other, grads))
+    own, other = call(
+        planes_kernel,
+        (sds((4, SUB, WIDE), f32), sds((4, SUB, WIDE), bf16)),
+        5,
+        scratch=[VMEM((8, SUB, WIDE), f32)],
+        smem=(0,),
+    )(table, own, *other)
+    grads, other = lax.optimization_barrier((grads, other))
+    w_mine, _ = lax.optimization_barrier((w_mine, recv))
     w_chips = [w_mine] + [shift(w_mine, "x", 4, k) for k in (3, 1, 2)]
     grads, w_chips = lax.optimization_barrier((grads, w_chips))
     w_all = [w for chip in w_chips for w in (chip, swap(chip))]
     grad_back = lax.all_to_all(grads, FRAME, 0, 0, tiled=True)
 
-    own, _ = lax.optimization_barrier((own, grads))
-    own, other = call(
-        planes_kernel,
-        (sds((4, SUBP, WIDE), f32), sds((4, SUBP, WIDE), bf16)),
-        3,
-        scratch=[VMEM((8, SUBP, WIDE), f32)],
-        smem=(0,),
-    )(table, own, flip(other, "y", 4, 2))
-    for mask, count in ((1, 2), (2, 1)):
-        half = (count, SUBP, WIDE)
-        own, other = call(halve_kernel, (sds(half, f32), sds(half, bf16)), 2)(
-            own, flip(other, "z", 8, mask)
+    other = flip(other, "z", 8, 1)
+    for mask, count, kind in ((1, 2, bf16), (2, 1, f32)):
+        half = (count, SUB, WIDE)
+        own, other = call(halve_kernel, (sds(half, f32), sds(half, kind)), 2)(
+            own, other if mask == 1 else flip(other, "z", 8, mask)
         )
-    grad_weight = turn(call(last_kernel, sds((SUB, WIDE), f32), 2)(own, flip(other, "z", 8, 4)))
-
+    pieces = [turn(own[0]), turn(other[0], 4)]
     mixed, grad_qkv = call(
         final_kernel,
         (sds((1, 1, CAP, D), bf16), sds((1, 1, CAP, 3 * D), bf16)),
         10,
         smem=(0,),
     )(table, grad_back, *w_all)
+    pieces, grad_qkv = lax.optimization_barrier((pieces, grad_qkv))
+    grad_weight = call(last_kernel, sds((SUB, WIDE), f32), 2)(*pieces)
     return mixed, grad_qkv, grad_weight
 
 

time: 165 us -> 145 us (0.88)
  Pallas kernels: 47 us -> 25.1 us
  starting transfers between devices: 35.5 us -> 47.7 us
  waiting for transfers between devices: 67.9 us -> 56.7 us
  local copies, waits for them, and re-layouts: 9.37 us -> 13.3 us
  other arithmetic: 1.74 us -> 0.08 us
    pallas_call x13 -> x12, Pallas kernels: 47 us -> 25.1 us  [run(): pl.pallas_call(kernel, grid=(1,), out_shape=out_shape, in_specs=specs, ou...]
    ppermute x10 -> x6, waiting for transfers between devices: 40.3 us -> 20.8 us  [flip(): return lax.ppermute(x, axis, [(i, i ^ mask) for i in range(count)])]
    all_to_all x1, waiting for transfers between devices: 0.01 us -> 7.97 us  [shards(): grad_back = lax.all_to_all(grads, FRAME, 0, 0, tiled=True)]
    ppermute x14 -> x17, starting transfers between devices: 9.62 us -> 17.1 us  [shift(): return lax.ppermute(x, axis, [(i, (i + k) % count) for i in range(count)])]
    ppermute x14 -> x17, waiting for transfers between devices: 10.3 us -> 3.56 us  [shift(): return lax.ppermute(x, axis, [(i, (i + k) % count) for i in range(count)])]
    ppermute x2 -> x4, starting transfers between devices: 7.4 us -> 14.1 us  [the longest x2 10.5 us: turn(): return lax.ppermute(x, ALL, pairs)]
    all_to_all x1, waiting for transfers between devices: 0.01 us -> 5.76 us  [shards(): recv = lax.all_to_all(packed, FRAME, 0, 0, tiled=True)]
    unnamed x39 -> x36, local copies, waits for them, and re-layouts: 8.71 us -> 13.2 us
  transfers between devices with their start and end apart: 28 -> 29, of which waited for: 12 -> 10; matrix products, arithmetic and copies ran while one was open for 1% -> 0% of each run, Pallas kernels for 22% -> 16%
where the time goes in v2:
time: 145 us
  waiting for transfers between devices  56.7 us (39%)
  starting transfers between devices  47.7 us (33%)
  Pallas kernels  25.1 us (17%)
  local copies, waits for them, and re-layouts  13.3 us (9%)
  between operations  1.62 us (1%)
    pallas_call x12, Pallas kernels, run(): pl.pallas_call(kernel, grid=(1,), out_shape=out_shape, in_specs=specs, ou...  25.1 us
    ppermute x6, waiting for transfers between devices, flip(): return lax.ppermute(x, axis, [(i, i ^ mask) for i in range(count)])  20.8 us
    ppermute x2, waiting for transfers between devices, turn_back(): return lax.ppermute(x, ALL, pairs)  18.6 us
    ppermute x17, starting transfers between devices, shift(): return lax.ppermute(x, axis, [(i, (i + k) % count) for i in range(count)])  17.1 us
    unnamed x36, local copies, waits for them, and re-layouts  13.2 us
    ppermute x2, starting transfers between devices, turn(): return lax.ppermute(x, ALL, pairs)  10.5 us
    ppermute x6, starting transfers between devices, flip(): return lax.ppermute(x, axis, [(i, i ^ mask) for i in range(count)])  8.14 us
    all_to_all x1, waiting for transfers between devices, shards(): grad_back = lax.all_to_all(grads, FRAME, 0, 0, tiled=True)  7.97 us
  transfers between devices with their start and end apart: 29, of which 10 were waited for; matrix products, arithmetic and copies ran while one was open for 0% of the time, Pallas kernels for 16%

profile of v2, /device:TPU:128, one launch (start us, length us, event | category | flops | bytes accessed | tf_op | source)
XLA Modules:
  0.0 144.5 jit_solution(5511727641359589222)
XLA Ops:
  1.4 1.4 copy-done.2
  3.5 2.0 %shard_map.76 = bf16[8,192,640]{2,1,0:T(8,128)(2,1)} custom-call(s32[1,1]{1,0:T(1,128)S(6)} %copy.8.counts_ref, bf16[1,1,192,4224]{3,2,1,0:T(8,128)(2,1)S(1)} %copy-done.2, s32[1,1,192]{2,1,0:T(1,128)S(1)} %copy-done.15), custom_call_target="tpu_custom_call" | custom-call | tf_op jit(solution)/shard_map/pallas_call | solution.py:60
  5.4 3.0 %collective-permute-start.2 = (bf16[192,1408]{1,0:T(8,128)(2,1)S(1)}, bf16[192,1408]{1,0:T(8,128)(2,1)}, u32[]{:S(2)}, u32[]{:S(2)}) collective-permute-start(bf16[192,1408]{1,0:T(8,128)(2,1)S(1)} %bitcast.31), channel_id=1, source_target_pairs={{0,4},{2,6},{4,0},{6,2},{1,5},{3,7},{5,1},{7,3},{8,12},{10,14},{12... | collective-permute-start | bytes 1622024 | tf_op jit(solution)/shard_map/ppermute | solution.py:256
  8.5 1.1 collective-permute-start.1
  11.1 3.0 %collective-permute-start.3 = (bf16[1,44,176]{2,1,0:T(8,128)(2,1)S(1)}, bf16[1,44,176]{2,1,0:T(8,128)(2,1)S(1)}, u32[]{:S(2)}, u32[]{:S(2)}) collective-permute-start(bf16[1,44,176]{2,1,0:T(8,128)(2,1)S(1)} %bitcast.46), channel_id=1, source_target_pairs={{0,0},{1,32},{2,64},{3,96},{4,128},{5,160},{6,192},{7,224},{8,8},{... | collective-permute-start | bytes 46472 | tf_op jit(solution)/shard_map/ppermute | solution.py:277
  14.1 18.6 %collective-permute-done.4.refs_1_ = bf16[1,44,176]{2,1,0:T(8,128)(2,1)S(1)} collective-permute-done((bf16[1,44,176]{2,1,0:T(8,128)(2,1)S(1)}, bf16[1,44,176]{2,1,0:T(8,128)(2,1)S(1)}, u32[]{:S(2)}, u32[]{:S(2)}) %collective-permute-start.4) | collective-permute-done | bytes 15520 | tf_op jit(solution)/shard_map/ppermute | solution.py:277
  33.3 4.7 %all-to-all-start = ((bf16[8,192,640]{2,1,0:T(8,128)(2,1)}), bf16[8,192,640]{2,1,0:T(8,128)(2,1)S(1)}, u32[]{:S(2)}, u32[]{:S(2)}) async-start(bf16[8,192,640]{2,1,0:T(8,128)(2,1)} %shard_map.76), calls=%async_computation | async-start | bytes 3932160 | tf_op jit(solution)/shard_map/all_to_all | solution.py:300
  38.0 1.3 collective-permute-start.5
  39.3 4.9 %collective-permute-done.5.refs_2_ = bf16[2,44,176]{2,1,0:T(8,128)(2,1)S(1)} collective-permute-done((bf16[2,44,176]{2,1,0:T(8,128)(2,1)S(1)}, bf16[2,44,176]{2,1,0:T(8,128)(2,1)S(1)}, u32[]{:S(2)}, u32[]{:S(2)}) %collective-permute-start.5) | collective-permute-done | bytes 31008 | tf_op jit(solution)/shard_map/ppermute | solution.py:267
  44.4 4.6 %collective-permute-done.6.refs_3_ = bf16[4,44,176]{2,1,0:T(8,128)(2,1)S(1)} collective-permute-done((bf16[4,44,176]{2,1,0:T(8,128)(2,1)S(1)}, bf16[4,44,176]{2,1,0:T(8,128)(2,1)S(1)}, u32[]{:S(2)}, u32[]{:S(2)}) %collective-permute-start.6) | collective-permute-done | bytes 61984 | tf_op jit(solution)/shard_map/ppermute | solution.py:267
  49.7 3.3 %collective-permute-start.7 = (bf16[1,44,1408]{2,1,0:T(8,128)(2,1)S(1)}, bf16[1,44,1408]{2,1,0:T(8,128)(2,1)S(1)}, u32[]{:S(2)}, u32[]{:S(2)}) collective-permute-start(bf16[1,44,1408]{2,1,0:T(8,128)(2,1)S(1)} %shard_map.77.one_ref), channel_id=1, source_target_pairs={{0,16},{8,24},{16,0},{24,8},{1,17},{9,25},{17,1},{25,9},{2,18},{10... | collective-permute-start | bytes 371720 | tf_op jit(solution)/shard_map/ppermute | solution.py:267
  54.0 2.3 %collective-permute-done.7.two_ref = bf16[1,44,1408]{2,1,0:T(8,128)(2,1)S(1)} collective-permute-done((bf16[1,44,1408]{2,1,0:T(8,128)(2,1)S(1)}, bf16[1,44,1408]{2,1,0:T(8,128)(2,1)S(1)}, u32[]{:S(2)}, u32[]{:S(2)}) %collective-permute-start.7) | collective-permute-done | bytes 123936 | tf_op jit(solution)/shard_map/ppermute | solution.py:267
  56.4 1.7 %collective-permute-start.8 = (bf16[2,44,1408]{2,1,0:T(8,128)(2,1)S(1)}, bf16[2,44,1408]{2,1,0:T(8,128)(2,1)S(1)}, u32[]{:S(2)}, u32[]{:S(2)}) collective-permute-start(bf16[2,44,1408]{2,1,0:T(8,128)(2,1)S(1)} %pad_maximum_fusion), channel_id=1, source_target_pairs={{0,8},{8,0},{16,24},{24,16},{1,9},{9,1},{17,25},{25,17},{2,10},{10... | collective-permute-start | bytes 743432 | tf_op jit(solution)/shard_map/ppermute | solution.py:267
  58.0 5.8 %all-to-all-done.recv_ref = bf16[8,192,640]{2,1,0:T(8,128)(2,1)S(1)} async-done(((bf16[8,192,640]{2,1,0:T(8,128)(2,1)}), bf16[8,192,640]{2,1,0:T(8,128)(2,1)S(1)}, u32[]{:S(2)}, u32[]{:S(2)}) %all-to-all-start) | async-done | bytes 1966112 | tf_op jit(solution)/shard_map/all_to_all | solution.py:300
  63.8 3.1 %shard_map.78 = (bf16[8,192,256]{2,1,0:T(8,128)(2,1)S(1)}, bf16[8,192,256]{2,1,0:T(8,128)(2,1)S(1)}, bf16[8,256,256]{2,1,0:T(8,128)(2,1)S(1)}, bf16[8,256,256]{2...) custom-call(bf16[8,192,640]{2,1,0:T(8,128)(2,1)S(1)} %all-to-all-don, ...), custom_call_target="tpu_custom_call" | custom-call | tf_op jit(solution)/shard_map/pallas_call | solution.py:60
  69.7 1.7 %collective-permute-start.17 = (bf16[176,1408]{1,0:T(8,128)(2,1)S(1)}, bf16[176,1408]{1,0:T(8,128)(2,1)}, u32[]{:S(2)}, u32[]{:S(2)}) collective-permute-start(bf16[176,1408]{1,0:T(8,128)(2,1)S(1)} %shard_map.80.w_ref.refs_0_), channel_id=1, source_target_pairs={{0,2},{2,4},{4,6},{6,0},{1,3},{3,5},{5,7},{7,1},{8,10},{10,12},{12... | collective-permute-start | bytes 1486856 | tf_op jit(solution)/shard_map/ppermute | solution.py:256
  71.4 1.6 %collective-permute-start.16 = (bf16[176,1408]{1,0:T(8,128)(2,1)S(1)}, bf16[176,1408]{1,0:T(8,128)(2,1)}, u32[]{:S(2)}, u32[]{:S(2)}) collective-permute-start(bf16[176,1408]{1,0:T(8,128)(2,1)S(1)} %shard_map.80.w_ref.refs_0_), channel_id=1, source_target_pairs={{0,6},{2,0},{4,2},{6,4},{1,7},{3,1},{5,3},{7,5},{8,14},{10,8},{12,... | collective-permute-start | bytes 1486856 | tf_op jit(solution)/shard_map/ppermute | solution.py:256
  73.0 3.4 %shard_map.79 = (f32[44,1408]{1,0:T(8,128)S(1)}, bf16[44,1408]{1,0:T(8,128)(2,1)S(1)}, bf16[44,1408]{1,0:T(8,128)(2,1)S(1)}, bf16[44,1408]{1,0:T(8,128)(2,1)S(1)}) custom-call(s32[1,32]{1,0:T(1,128)S(1)} %bitcast.39, bf16[8,192,256]{2,1,0:T(8,128)(2,1)S(1)} %get-tuple-element.56.att_ref, bf16[192,1408]{1,0:T(8,128)(2,1)S(1)} %bitcast.35, ...), custom_call_target="tpu_custom_call" | custom-call | tf_op jit(solution)/shard_map/pallas_call | solution.py:60
  76.4 1.7 %collective-permute-start.13 = (bf16[44,1408]{1,0:T(8,128)(2,1)S(1)}, bf16[44,1408]{1,0:T(8,128)(2,1)S(1)}, u32[]{:S(2)}, u32[]{:S(2)}) collective-permute-start(bf16[44,1408]{1,0:T(8,128)(2,1)S(1)} %get-tuple-element.61), channel_id=1, source_target_pairs={{0,8},{8,16},{16,24},{24,0},{1,9},{9,17},{17,25},{25,1},{2,10},{10... | collective-permute-start | bytes 371720 | tf_op jit(solution)/shard_map/ppermute | solution.py:256
  78.0 2.9 %collective-permute-start.14 = (bf16[44,1408]{1,0:T(8,128)(2,1)S(1)}, bf16[44,1408]{1,0:T(8,128)(2,1)S(1)}, u32[]{:S(2)}, u32[]{:S(2)}) collective-permute-start(bf16[44,1408]{1,0:T(8,128)(2,1)S(1)} %get-tuple-element.62), channel_id=1, source_target_pairs={{0,16},{8,24},{16,0},{24,8},{1,17},{9,25},{17,1},{25,9},{2,18},{10... | collective-permute-start | bytes 371720 | tf_op jit(solution)/shard_map/ppermute | solution.py:256
  80.9 2.9 %collective-permute-done.13.refs_1_ = bf16[44,1408]{1,0:T(8,128)(2,1)S(1)} collective-permute-done((bf16[44,1408]{1,0:T(8,128)(2,1)S(1)}, bf16[44,1408]{1,0:T(8,128)(2,1)S(1)}, u32[]{:S(2)}, u32[]{:S(2)}) %collective-permute-start.13) | collective-permute-done | bytes 123936 | tf_op jit(solution)/shard_map/ppermute | solution.py:256
  83.8 1.7 %collective-permute-start.15 = (bf16[44,1408]{1,0:T(8,128)(2,1)S(1)}, bf16[44,1408]{1,0:T(8,128)(2,1)S(1)}, u32[]{:S(2)}, u32[]{:S(2)}) collective-permute-start(bf16[44,1408]{1,0:T(8,128)(2,1)S(1)} %get-tuple-element.63), channel_id=1, source_target_pairs={{0,24},{8,0},{16,8},{24,16},{1,25},{9,1},{17,9},{25,17},{2,26},{10... | collective-permute-start | bytes 371720 | tf_op jit(solution)/shard_map/ppermute | solution.py:256
  85.5 3.4 %shard_map.81.grad_att_ref = bf16[8,192,176]{2,1,0:T(8,128)(2,1)S(1)} custom-call(bf16[176,1408]{1,0:T(8,128)(2,1)S(1)} %shard_map.80.w_ref.refs_0_, bf16[192,1408]{1,0:T(8,128)(2,1)S(1)} %bitcast.36, bf16[192,1408]{1,0:T(8,128)(2,1)} %collective-permute-done.9.refs_1_, bf16[192,1408]{1,0:T(8,128)(2,1)} %collective-permute-done.refs_2_, ...), custom_call_target="tpu_custom_call" | custom-call | tf_op jit(solution)/shard_map/pallas_call | solution.py:60
  88.9 6.5 %shard_map.82 = bf16[8,192,704]{2,1,0:T(8,128)(2,1)S(1)} custom-call(s32[1,32]{1,0:T(1,128)S(1)} %bitcast.40, bf16[8,192,176]{2,1,0:T(8,128)(2,1)S(1)} %shard_map.81.grad_att_ref, bf16[8,192,256]{2,1,0:T(8,128)(2,1)S(1)} %get-tuple-element.56.att_ref, bf16[8,192,256]{2,1,0:T(8,128)(2,1)S(1)} %get-tuple-element.67.hot_ref, ...), custom_call_target="tpu_custom_call" | custom-call | tf_op jit(solution)/shard_map/pallas_call | solution.py:60
  95.5 1.4 copy-done
  98.5 3.7 %all-to-all-start.1 = ((bf16[8,192,704]{2,1,0:T(8,128)(2,1)}), bf16[8,192,704]{2,1,0:T(8,128)(2,1)S(1)}, u32[]{:S(2)}, u32[]{:S(2)}) async-start(bf16[8,192,704]{2,1,0:T(8,128)(2,1)} %copy-done), calls=%async_computation.1 | async-start | bytes 4718592 | tf_op jit(solution)/shard_map/all_to_all | solution.py:367
  103.9 4.7 %collective-permute-done.23.in_ref = bf16[4,44,176]{2,1,0:T(8,128)(2,1)S(1)} collective-permute-done((bf16[4,44,176]{2,1,0:T(8,128)(2,1)}, bf16[4,44,176]{2,1,0:T(8,128)(2,1)S(1)}, u32[]{:S(2)}, u32[]{:S(2)}) %collective-permute-start.23) | collective-permute-done | bytes 61984 | tf_op jit(solution)/shard_map/ppermute | solution.py:267
  108.6 1.3 collective-permute-start.24
  109.9 4.3 %collective-permute-done.24.in_ref = bf16[2,44,176]{2,1,0:T(8,128)(2,1)S(1)} collective-permute-done((bf16[2,44,176]{2,1,0:T(8,128)(2,1)S(1)}, bf16[2,44,176]{2,1,0:T(8,128)(2,1)S(1)}, u32[]{:S(2)}, u32[]{:S(2)}) %collective-permute-start.24) | collective-permute-done | bytes 31008 | tf_op jit(solution)/shard_map/ppermute | solution.py:267
  115.1 10.4 %collective-permute-start.25 = (f32[44,176]{1,0:T(8,128)S(1)}, f32[44,176]{1,0:T(8,128)S(1)}, u32[]{:S(2)}, u32[]{:S(2)}) collective-permute-start(f32[44,176]{1,0:T(8,128)S(1)} %bitcast.43), channel_id=1, source_target_pairs={{0,0},{1,32},{2,64},{3,96},{4,128},{5,160},{6,192},{7,224},{8,8},{... | collective-permute-start | bytes 92936 | tf_op jit(solution)/shard_map/ppermute | solution.py:272
  127.9 8.0 %all-to-all-done.1.in_ref = bf16[8,192,704]{2,1,0:T(8,128)(2,1)S(1)} async-done(((bf16[8,192,704]{2,1,0:T(8,128)(2,1)}), bf16[8,192,704]{2,1,0:T(8,128)(2,1)S(1)}, u32[]{:S(2)}, u32[]{:S(2)}) %all-to-all-start.1) | async-done | bytes 2162720 | tf_op jit(solution)/shard_map/all_to_all | solution.py:367
  140.0 3.9 %shard_map.84 = (bf16[1,1,192,1408]{3,2,1,0:T(8,128)(2,1)}, bf16[1,1,192,4224]{3,2,1,0:T(8,128)(2,1)}) custom-call(s32[1,32]{1,0:T(1,128)S(1)} %bitcast.42, bf16[8,192,704]{2,1,0:T(8,128)(2,1)S(1)} %all-to-all-done.1.in_ref, bf16[176,1408]{1,0:T(8,128)(2,1)S(1)} %shard_map.80.w_ref.refs_0_, bf16[176,1408]{1,0:T(8,128)(2,1)S(1)} %copy-done.6, ...), custom_call_target="tpu_custom_call" | custom-call | tf_op jit(solution)/shard_map/pallas_call | solution.py:60
  (78 shorter events, 18.8 us)
Async XLA Ops:
  0.6 4.8 %copy-start.1 = (bf16[1,1,192,1408]{3,2,1,0:T(8,128)(2,1)S(1)}, bf16[1,1,192,1408]{3,2,1,0:T(8,128)(2,1)}, u32[]{:S(2)}) copy-start(bf16[1,1,192,1408]{3,2,1,0:T(8,128)(2,1)} %param.8) | copy-start | bytes 1622020
  3.5 7.0 %copy-start.17 = (bf16[44,176]{1,0:T(8,128)(2,1)S(1)}, bf16[44,176]{1,0:T(8,128)(2,1)}, u32[]{:S(2)}) copy-start(bf16[44,176]{1,0:T(8,128)(2,1)} %param.9) | copy-start | bytes 46468
  5.4 27.2 %collective-permute-start.2 = (bf16[192,1408]{1,0:T(8,128)(2,1)S(1)}, bf16[192,1408]{1,0:T(8,128)(2,1)}, u32[]{:S(2)}, u32[]{:S(2)}) collective-permute-start(bf16[192,1408]{1,0:T(8,128)(2,1)S(1)} %bitcast.31), channel_id=1, source_target_pairs={{0,4},{2,6},{4,0},{6,2},{1,5},{3,7},{5,1},{7,3},{8,12},{10,14},{12... | collective-permute-start | bytes 1622024 | tf_op jit(solution)/shard_map/ppermute | solution.py:256
  8.5 24.8 %collective-permute-start.1 = (bf16[192,1408]{1,0:T(8,128)(2,1)S(1)}, bf16[192,1408]{1,0:T(8,128)(2,1)}, u32[]{:S(2)}, u32[]{:S(2)}) collective-permute-start(bf16[192,1408]{1,0:T(8,128)(2,1)S(1)} %bitcast.32), channel_id=1, source_target_pairs={{0,6},{2,0},{4,2},{6,4},{1,7},{3,1},{5,3},{7,5},{8,14},{10,8},{12,... | collective-permute-start | bytes 1622024 | tf_op jit(solution)/shard_map/ppermute | solution.py:256
  9.6 23.7 %collective-permute-start = (bf16[192,1408]{1,0:T(8,128)(2,1)S(1)}, bf16[192,1408]{1,0:T(8,128)(2,1)}, u32[]{:S(2)}, u32[]{:S(2)}) collective-permute-start(bf16[192,1408]{1,0:T(8,128)(2,1)S(1)} %bitcast.33), channel_id=1, source_target_pairs={{0,2},{2,4},{4,6},{6,0},{1,3},{3,5},{5,7},{7,1},{8,10},{10,12},{12... | collective-permute-start | bytes 1622024 | tf_op jit(solution)/shard_map/ppermute | solution.py:256
  10.5 22.2 %collective-permute-start.4 = (bf16[1,44,176]{2,1,0:T(8,128)(2,1)S(1)}, bf16[1,44,176]{2,1,0:T(8,128)(2,1)S(1)}, u32[]{:S(2)}, u32[]{:S(2)}) collective-permute-start(bf16[1,44,176]{2,1,0:T(8,128)(2,1)S(1)} %bitcast.45), channel_id=1, source_target_pairs={{0,128},{1,160},{2,192},{3,224},{4,0},{5,32},{6,64},{7,96},{8,136}... | collective-permute-start | bytes 46472 | tf_op jit(solution)/shard_map/ppermute | solution.py:277
  11.1 21.6 %collective-permute-start.3 = (bf16[1,44,176]{2,1,0:T(8,128)(2,1)S(1)}, bf16[1,44,176]{2,1,0:T(8,128)(2,1)S(1)}, u32[]{:S(2)}, u32[]{:S(2)}) collective-permute-start(bf16[1,44,176]{2,1,0:T(8,128)(2,1)S(1)} %bitcast.46), channel_id=1, source_target_pairs={{0,0},{1,32},{2,64},{3,96},{4,128},{5,160},{6,192},{7,224},{8,8},{... | collective-permute-start | bytes 46472 | tf_op jit(solution)/shard_map/ppermute | solution.py:277
  33.3 30.5 %all-to-all-start = ((bf16[8,192,640]{2,1,0:T(8,128)(2,1)}), bf16[8,192,640]{2,1,0:T(8,128)(2,1)S(1)}, u32[]{:S(2)}, u32[]{:S(2)}) async-start(bf16[8,192,640]{2,1,0:T(8,128)(2,1)} %shard_map.76), calls=%async_computation | async-start | bytes 3932160 | tf_op jit(solution)/shard_map/all_to_all | solution.py:300
  38.0 6.1 %collective-permute-start.5 = (bf16[2,44,176]{2,1,0:T(8,128)(2,1)S(1)}, bf16[2,44,176]{2,1,0:T(8,128)(2,1)S(1)}, u32[]{:S(2)}, u32[]{:S(2)}) collective-permute-start(bf16[2,44,176]{2,1,0:T(8,128)(2,1)S(1)} %pad_maximum_fusion.2), channel_id=1, source_target_pairs={{0,64},{32,96},{64,0},{96,32},{128,192},{160,224},{192,128},{224,1... | collective-permute-start | bytes 92936 | tf_op jit(solution)/shard_map/ppermute | solution.py:267
  44.2 4.9 %collective-permute-start.6 = (bf16[4,44,176]{2,1,0:T(8,128)(2,1)S(1)}, bf16[4,44,176]{2,1,0:T(8,128)(2,1)S(1)}, u32[]{:S(2)}, u32[]{:S(2)}) collective-permute-start(bf16[4,44,176]{2,1,0:T(8,128)(2,1)S(1)} %pad_maximum_fusion.1), channel_id=1, source_target_pairs={{0,32},{32,0},{64,96},{96,64},{128,160},{160,128},{192,224},{224,1... | collective-permute-start | bytes 185864 | tf_op jit(solution)/shard_map/ppermute | solution.py:267
  49.7 6.6 %collective-permute-start.7 = (bf16[1,44,1408]{2,1,0:T(8,128)(2,1)S(1)}, bf16[1,44,1408]{2,1,0:T(8,128)(2,1)S(1)}, u32[]{:S(2)}, u32[]{:S(2)}) collective-permute-start(bf16[1,44,1408]{2,1,0:T(8,128)(2,1)S(1)} %shard_map.77.one_ref), channel_id=1, source_target_pairs={{0,16},{8,24},{16,0},{24,8},{1,17},{9,25},{17,1},{25,9},{2,18},{10... | collective-permute-start | bytes 371720 | tf_op jit(solution)/shard_map/ppermute | solution.py:267
  53.0 16.7 %collective-permute-start.9 = (bf16[192,1408]{1,0:T(8,128)(2,1)S(1)}, bf16[192,1408]{1,0:T(8,128)(2,1)}, u32[]{:S(2)}, u32[]{:S(2)}) collective-permute-start(bf16[192,1408]{1,0:T(8,128)(2,1)S(1)} %bitcast.34), channel_id=1, source_target_pairs={{0,1},{1,0},{2,3},{3,2},{4,5},{5,4},{6,7},{7,6},{8,9},{9,8},{10,11... | collective-permute-start | bytes 1622024 | tf_op jit(solution)/shard_map/ppermute | solution.py:256
  53.0 18.4 %collective-permute-start.10 = (bf16[192,1408]{1,0:T(8,128)(2,1)}, bf16[192,1408]{1,0:T(8,128)(2,1)}, u32[]{:S(2)}, u32[]{:S(2)}) collective-permute-start(bf16[192,1408]{1,0:T(8,128)(2,1)} %collective-permute-done.refs_2_), channel_id=1, source_target_pairs={{0,1},{1,0},{2,3},{3,2},{4,5},{5,4},{6,7},{7,6},{8,9},{9,8},{10,11... | collective-permute-start | bytes 1622024 | tf_op jit(solution)/shard_map/ppermute | solution.py:256
  53.5 19.5 %collective-permute-start.11 = (bf16[192,1408]{1,0:T(8,128)(2,1)}, bf16[192,1408]{1,0:T(8,128)(2,1)}, u32[]{:S(2)}, u32[]{:S(2)}) collective-permute-start(bf16[192,1408]{1,0:T(8,128)(2,1)} %collective-permute-done.1.refs_4_), channel_id=1, source_target_pairs={{0,1},{1,0},{2,3},{3,2},{4,5},{5,4},{6,7},{7,6},{8,9},{9,8},{10,11... | collective-permute-start | bytes 1622024 | tf_op jit(solution)/shard_map/ppermute | solution.py:256
  53.5 19.5 %collective-permute-start.12 = (bf16[192,1408]{1,0:T(8,128)(2,1)}, bf16[192,1408]{1,0:T(8,128)(2,1)}, u32[]{:S(2)}, u32[]{:S(2)}) collective-permute-start(bf16[192,1408]{1,0:T(8,128)(2,1)} %collective-permute-done.2.refs_6_), channel_id=1, source_target_pairs={{0,1},{1,0},{2,3},{3,2},{4,5},{5,4},{6,7},{7,6},{8,9},{9,8},{10,11... | collective-permute-start | bytes 1622024 | tf_op jit(solution)/shard_map/ppermute | solution.py:256
  56.4 10.6 %collective-permute-start.8 = (bf16[2,44,1408]{2,1,0:T(8,128)(2,1)S(1)}, bf16[2,44,1408]{2,1,0:T(8,128)(2,1)S(1)}, u32[]{:S(2)}, u32[]{:S(2)}) collective-permute-start(bf16[2,44,1408]{2,1,0:T(8,128)(2,1)S(1)} %pad_maximum_fusion), channel_id=1, source_target_pairs={{0,8},{8,0},{16,24},{24,16},{1,9},{9,1},{17,25},{25,17},{2,10},{10... | collective-permute-start | bytes 743432 | tf_op jit(solution)/shard_map/ppermute | solution.py:267
  69.3 28.4 %collective-permute-start.18 = (bf16[176,1408]{1,0:T(8,128)(2,1)S(1)}, bf16[176,1408]{1,0:T(8,128)(2,1)S(1)}, u32[]{:S(2)}, u32[]{:S(2)}) collective-permute-start(bf16[176,1408]{1,0:T(8,128)(2,1)S(1)} %shard_map.80.w_ref.refs_0_), channel_id=1, source_target_pairs={{0,4},{2,6},{4,0},{6,2},{1,5},{3,7},{5,1},{7,3},{8,12},{10,14},{12... | collective-permute-start | bytes 1486856 | tf_op jit(solution)/shard_map/ppermute | solution.py:256
  69.7 28.0 %collective-permute-start.17 = (bf16[176,1408]{1,0:T(8,128)(2,1)S(1)}, bf16[176,1408]{1,0:T(8,128)(2,1)}, u32[]{:S(2)}, u32[]{:S(2)}) collective-permute-start(bf16[176,1408]{1,0:T(8,128)(2,1)S(1)} %shard_map.80.w_ref.refs_0_), channel_id=1, source_target_pairs={{0,2},{2,4},{4,6},{6,0},{1,3},{3,5},{5,7},{7,1},{8,10},{10,12},{12... | collective-permute-start | bytes 1486856 | tf_op jit(solution)/shard_map/ppermute | solution.py:256
  71.4 27.1 %collective-permute-start.16 = (bf16[176,1408]{1,0:T(8,128)(2,1)S(1)}, bf16[176,1408]{1,0:T(8,128)(2,1)}, u32[]{:S(2)}, u32[]{:S(2)}) collective-permute-start(bf16[176,1408]{1,0:T(8,128)(2,1)S(1)} %shard_map.80.w_ref.refs_0_), channel_id=1, source_target_pairs={{0,6},{2,0},{4,2},{6,4},{1,7},{3,1},{5,3},{7,5},{8,14},{10,8},{12,... | collective-permute-start | bytes 1486856 | tf_op jit(solution)/shard_map/ppermute | solution.py:256
  76.4 7.5 %collective-permute-start.13 = (bf16[44,1408]{1,0:T(8,128)(2,1)S(1)}, bf16[44,1408]{1,0:T(8,128)(2,1)S(1)}, u32[]{:S(2)}, u32[]{:S(2)}) collective-permute-start(bf16[44,1408]{1,0:T(8,128)(2,1)S(1)} %get-tuple-element.61), channel_id=1, source_target_pairs={{0,8},{8,16},{16,24},{24,0},{1,9},{9,17},{17,25},{25,1},{2,10},{10... | collective-permute-start | bytes 371720 | tf_op jit(solution)/shard_map/ppermute | solution.py:256
  78.0 18.9 %collective-permute-start.14 = (bf16[44,1408]{1,0:T(8,128)(2,1)S(1)}, bf16[44,1408]{1,0:T(8,128)(2,1)S(1)}, u32[]{:S(2)}, u32[]{:S(2)}) collective-permute-start(bf16[44,1408]{1,0:T(8,128)(2,1)S(1)} %get-tuple-element.62), channel_id=1, source_target_pairs={{0,16},{8,24},{16,0},{24,8},{1,17},{9,25},{17,1},{25,9},{2,18},{10... | collective-permute-start | bytes 371720 | tf_op jit(solution)/shard_map/ppermute | solution.py:256
  83.8 13.1 %collective-permute-start.15 = (bf16[44,1408]{1,0:T(8,128)(2,1)S(1)}, bf16[44,1408]{1,0:T(8,128)(2,1)S(1)}, u32[]{:S(2)}, u32[]{:S(2)}) collective-permute-start(bf16[44,1408]{1,0:T(8,128)(2,1)S(1)} %get-tuple-element.63), channel_id=1, source_target_pairs={{0,24},{8,0},{16,8},{24,16},{1,25},{9,1},{17,9},{25,17},{2,26},{10... | collective-permute-start | bytes 371720 | tf_op jit(solution)/shard_map/ppermute | solution.py:256
  98.5 4.7 %copy-start.4 = (bf16[176,1408]{1,0:T(8,128)(2,1)S(1)}, bf16[176,1408]{1,0:T(8,128)(2,1)}, u32[]{:S(2)}) copy-start(bf16[176,1408]{1,0:T(8,128)(2,1)} %copy-done.3) | copy-start | bytes 1486852
  98.5 37.4 %all-to-all-start.1 = ((bf16[8,192,704]{2,1,0:T(8,128)(2,1)}), bf16[8,192,704]{2,1,0:T(8,128)(2,1)S(1)}, u32[]{:S(2)}, u32[]{:S(2)}) async-start(bf16[8,192,704]{2,1,0:T(8,128)(2,1)} %copy-done), calls=%async_computation.1 | async-start | bytes 4718592 | tf_op jit(solution)/shard_map/all_to_all | solution.py:367
  102.2 12.1 %collective-permute-start.19 = (bf16[176,1408]{1,0:T(8,128)(2,1)S(1)}, bf16[176,1408]{1,0:T(8,128)(2,1)S(1)}, u32[]{:S(2)}, u32[]{:S(2)}) collective-permute-start(bf16[176,1408]{1,0:T(8,128)(2,1)S(1)} %shard_map.80.w_ref.refs_0_), channel_id=1, source_target_pairs={{0,1},{1,0},{2,3},{3,2},{4,5},{5,4},{6,7},{7,6},{8,9},{9,8},{10,11... | collective-permute-start | bytes 1486856 | tf_op jit(solution)/shard_map/ppermute | solution.py:256
  102.6 22.9 %collective-permute-start.20 = (bf16[176,1408]{1,0:T(8,128)(2,1)}, bf16[176,1408]{1,0:T(8,128)(2,1)S(1)}, u32[]{:S(2)}, u32[]{:S(2)}) collective-permute-start(bf16[176,1408]{1,0:T(8,128)(2,1)} %collective-permute-done.16.refs_2_), channel_id=1, source_target_pairs={{0,1},{1,0},{2,3},{3,2},{4,5},{5,4},{6,7},{7,6},{8,9},{9,8},{10,11... | collective-permute-start | bytes 1486856 | tf_op jit(solution)/shard_map/ppermute | solution.py:256
  102.8 23.5 %collective-permute-start.21 = (bf16[176,1408]{1,0:T(8,128)(2,1)}, bf16[176,1408]{1,0:T(8,128)(2,1)S(1)}, u32[]{:S(2)}, u32[]{:S(2)}) collective-permute-start(bf16[176,1408]{1,0:T(8,128)(2,1)} %collective-permute-done.17.refs_4_), channel_id=1, source_target_pairs={{0,1},{1,0},{2,3},{3,2},{4,5},{5,4},{6,7},{7,6},{8,9},{9,8},{10,11... | collective-permute-start | bytes 1486856 | tf_op jit(solution)/shard_map/ppermute | solution.py:256
  103.1 23.9 %collective-permute-start.22 = (bf16[176,1408]{1,0:T(8,128)(2,1)S(1)}, bf16[176,1408]{1,0:T(8,128)(2,1)S(1)}, u32[]{:S(2)}, u32[]{:S(2)}) collective-permute-start(bf16[176,1408]{1,0:T(8,128)(2,1)S(1)} %copy-done.4), channel_id=1, source_target_pairs={{0,1},{1,0},{2,3},{3,2},{4,5},{5,4},{6,7},{7,6},{8,9},{9,8},{10,11... | collective-permute-start | bytes 1486856 | tf_op jit(solution)/shard_map/ppermute | solution.py:256
  103.3 5.2 %collective-permute-start.23 = (bf16[4,44,176]{2,1,0:T(8,128)(2,1)}, bf16[4,44,176]{2,1,0:T(8,128)(2,1)S(1)}, u32[]{:S(2)}, u32[]{:S(2)}) collective-permute-start(bf16[4,44,176]{2,1,0:T(8,128)(2,1)} %copy-done.16), channel_id=1, source_target_pairs={{0,32},{32,0},{64,96},{96,64},{128,160},{160,128},{192,224},{224,1... | collective-permute-start | bytes 185864 | tf_op jit(solution)/shard_map/ppermute | solution.py:267
  108.6 5.6 %collective-permute-start.24 = (bf16[2,44,176]{2,1,0:T(8,128)(2,1)S(1)}, bf16[2,44,176]{2,1,0:T(8,128)(2,1)S(1)}, u32[]{:S(2)}, u32[]{:S(2)}) collective-permute-start(bf16[2,44,176]{2,1,0:T(8,128)(2,1)S(1)} %get-tuple-element.90), channel_id=1, source_target_pairs={{0,64},{32,96},{64,0},{96,32},{128,192},{160,224},{192,128},{224,1... | collective-permute-start | bytes 92936 | tf_op jit(solution)/shard_map/ppermute | solution.py:267
  114.2 29.7 %collective-permute-start.26 = (f32[44,176]{1,0:T(8,128)S(1)}, f32[44,176]{1,0:T(8,128)S(1)}, u32[]{:S(2)}, u32[]{:S(2)}) collective-permute-start(f32[44,176]{1,0:T(8,128)S(1)} %bitcast.44), channel_id=1, source_target_pairs={{0,4},{1,36},{2,68},{3,100},{4,132},{5,164},{6,196},{7,228},{8,12}... | collective-permute-start | bytes 92936 | tf_op jit(solution)/shard_map/ppermute | solution.py:272
  115.1 28.8 %collective-permute-start.25 = (f32[44,176]{1,0:T(8,128)S(1)}, f32[44,176]{1,0:T(8,128)S(1)}, u32[]{:S(2)}, u32[]{:S(2)}) collective-permute-start(f32[44,176]{1,0:T(8,128)S(1)} %bitcast.43), channel_id=1, source_target_pairs={{0,0},{1,32},{2,64},{3,96},{4,128},{5,160},{6,192},{7,224},{8,8},{... | collective-permute-start | bytes 92936 | tf_op jit(solution)/shard_map/ppermute | solution.py:272
  (15 other events, 13.9 us)

commit v3 on v2

--- a/solution.py
+++ b/solution.py
@@ -17,7 +17,9 @@
 WIDE = D // FRAMES
 HEAD = D // HEADS
 SUB = 44
-PACK = 640
+LINE = 3 * WIDE
+HALF = CAP // 2
+PACK = 1152
 GROUP = 16
 BLOCK = GROUP * FRAMES
 BIG = 1e30
@@ -29,7 +31,7 @@
 STEPS = [(0, 0), (0, 1), (3, 0), (3, 1), (1, 0), (1, 1), (2, 0), (2, 1)]
 ALL = ("z", "y", "x", "core")
 FRAME = ("x", "core")
-WHERE, ORIGIN, Z_FLIP, Y_FLIP, Y_NEXT = 0, 8, 16, 24, 28
+WHERE, ORIGIN, Z_FLIP, Y_FLIP = 0, 8, 16, 24
 
 
 def dot(a, b):
@@ -64,7 +66,7 @@
             in_specs=specs,
             out_specs=jax.tree.map(lambda s: spec(s.shape), out_shape),
             scratch_shapes=list(scratch),
-            compiler_params=pltpu.CompilerParams(vmem_limit_bytes=32 * 1024 * 1024),
+            compiler_params=pltpu.CompilerParams(vmem_limit_bytes=28 * 1024 * 1024),
             cost_estimate=pl.CostEstimate(flops=flops, bytes_accessed=0, transcendentals=0),
         )(*args)
 
@@ -77,12 +79,16 @@
     diag = iota((CAP, CAP), 0) == slot
     held = jnp.where(slot < counts_ref[0, 0], keep.astype(f32), -1.0)
     column = jnp.sum(jnp.where(diag, held, 0.0), axis=1, keepdims=True)
-    tail = jnp.broadcast_to(column, (CAP, PACK - 3 * WIDE)).astype(bf16)
+    column = column.astype(bf16)
+    pad = jnp.zeros((HALF, PACK - 2 * LINE - 2), bf16)
     for f in range(FRAMES):
-        parts = [
-            qkv_ref[0, 0, :, part * D + WIDE * f : part * D + WIDE * (f + 1)] for part in range(3)
-        ]
-        out_ref[f] = jnp.concatenate(parts + [tail], axis=1)
+        parts = []
+        for rows in (slice(0, HALF), slice(HALF, CAP)):
+            for part in range(3):
+                at = part * D + WIDE * f
+                parts.append(qkv_ref[0, 0, rows, at : at + WIDE])
+        parts += [column[:HALF], column[HALF:], pad]
+        out_ref[f] = jnp.concatenate(parts, axis=1)
 
 
 def rows_from(keep_column):
@@ -90,10 +96,7 @@
     return jnp.sum(jnp.where(diag, keep_column, 0.0), axis=0, keepdims=True)
 
 
-def forward_kernel(
-    recv_ref, att_ref, hot_ref, hot_t_ref, qg, kg, vg, probs_ref, ag
-):
-    scaling = 1.0 / math.sqrt(HEAD)
+def place_clip(recv_ref, hot_ref, hot_t_ref, qg, kg, vg):
     lane = iota((PATCHES, PATCHES), 1)
     patch = lax.rem(iota((PATCHES, PATCHES), 0), GROUP)
     extra = lane >= WIDE
@@ -103,8 +106,10 @@
     zeros = jnp.zeros((CAP, PATCHES - WIDE), bf16)
     ones = jnp.ones((CAP, PATCHES - WIDE), bf16)
     for t in range(FRAMES):
-        recv = recv_ref.at[t]
-        column = recv[:, 3 * WIDE : 3 * WIDE + 1].astype(f32)
+        packed = recv_ref[t]
+        recv = jnp.concatenate([packed[:, :LINE], packed[:, LINE : 2 * LINE]], axis=0)
+        column = [packed[:, 2 * LINE + i : 2 * LINE + i + 1] for i in range(2)]
+        column = jnp.concatenate(column, axis=0).astype(f32)
         row = rows_from(column)
         hot = jnp.where(column == iota((CAP, PATCHES), 1).astype(f32), 1.0, 0.0)
         hot_ref[t] = hot.astype(bf16)
@@ -120,6 +125,10 @@
         kg[t] = kk.astype(bf16)
         vg[t] = placed[:, 2 * PATCHES :].astype(bf16)
 
+
+def forward_kernel(recv_ref, att_ref, hot_ref, hot_t_ref, qg, kg, vg, ag):
+    scaling = 1.0 / math.sqrt(HEAD)
+    place_clip(recv_ref, hot_ref, hot_t_ref, qg, kg, vg)
     wide_lane = iota((BLOCK, PATCHES), 1)
     first = (wide_lane < HEAD) | (wide_lane >= WIDE)
     second = wide_lane >= HEAD
@@ -134,7 +143,6 @@
         scores = dot_t(k, q2) * scaling
         expo = jnp.exp(scores - jnp.max(scores, axis=0, keepdims=True))
         probs = expo * (1.0 / jnp.sum(expo, axis=0, keepdims=True))
-        probs_ref[b] = probs
         out = t_dot(probs.astype(bf16), v)
         att = jnp.where(slim, out[:BLOCK], out[BLOCK:]).astype(bf16)
         for t in range(FRAMES):
@@ -146,13 +154,16 @@
 
 
 def backward_kernel(
-    table_ref, grad_att_ref, att_ref, hot_ref, hot_t_ref, qg, kg, vg, probs_ref, *refs
+    table_ref, grad_att_ref, att_ref, recv_ref, grad_ref, hot_ref, hot_t_ref, qg, kg, vg, gg
 ):
-    grad_ref, gg, dq, dk, dv = refs
     scaling = 1.0 / math.sqrt(HEAD)
+    place_clip(recv_ref, hot_ref, hot_t_ref, qg, kg, vg)
     for i in range(FRAMES):
         t = table_ref[0, WHERE + i]
         gg[t] = dot(hot_t_ref[t][:, :CAP], grad_att_ref[i]).astype(bf16)
+    wide_lane = iota((BLOCK, PATCHES), 1)
+    first = (wide_lane < HEAD) | (wide_lane >= WIDE)
+    second = wide_lane >= HEAD
     slim = iota((BLOCK, WIDE), 1) < HEAD
 
     def two(x):
@@ -161,26 +172,33 @@
 
     for b in range(PATCHES // GROUP):
         rows = slice(b * GROUP, (b + 1) * GROUP)
-        q = jnp.concatenate([qg[t, rows, :WIDE] for t in range(FRAMES)], axis=0)
-        k = jnp.concatenate([kg[t, rows, :WIDE] for t in range(FRAMES)], axis=0)
+        q = jnp.concatenate([qg[t, rows, :] for t in range(FRAMES)], axis=0)
+        k = jnp.concatenate([kg[t, rows, :] for t in range(FRAMES)], axis=0)
         v = jnp.concatenate([vg[t, rows, :] for t in range(FRAMES)], axis=0)
         g2 = two(jnp.concatenate([gg[t, rows, :] for t in range(FRAMES)], axis=0))
-        probs = probs_ref[b]
+        zero = jnp.zeros_like(q)
+        q2 = jnp.concatenate([jnp.where(first, q, zero), jnp.where(second, q, zero)], axis=0)
+        scores = dot_t(k, q2) * scaling
+        expo = jnp.exp(scores - jnp.max(scores, axis=0, keepdims=True))
+        probs = expo * (1.0 / jnp.sum(expo, axis=0, keepdims=True))
         grad_probs = dot_t(v, g2)
         grad_v = dot(probs.astype(bf16), g2).astype(bf16)
         inner = jnp.sum(probs * grad_probs, axis=0, keepdims=True)
         grad_scores = (probs * (grad_probs - inner)).astype(bf16)
-        out = t_dot(grad_scores, k)
+        out = t_dot(grad_scores, k[:, :WIDE])
         grad_q = (jnp.where(slim, out[:BLOCK], out[BLOCK:]) * scaling).astype(bf16)
-        grad_k = (dot(grad_scores, two(q)) * scaling).astype(bf16)
+        grad_k = (dot(grad_scores, q2[:, :WIDE]) * scaling).astype(bf16)
         for t in range(FRAMES):
             own = slice(t * GROUP, (t + 1) * GROUP)
-            dq[t, rows, :] = grad_q[own]
-            dk[t, rows, :] = grad_k[own]
-            dv[t, rows, :] = grad_v[own]
+            qg[t, rows, :WIDE] = grad_q[own]
+            kg[t, rows, :WIDE] = grad_k[own]
+            vg[t, rows, :] = grad_v[own]
     for t in range(FRAMES):
-        parts = [dot(hot_ref[t], x[t]).astype(bf16) for x in (dq, dk, dv)]
-        grad_ref[t] = jnp.concatenate(parts + [att_ref[t, :, :WIDE]], axis=1)
+        parts = [dot(hot_ref[t], x[t, :, :WIDE]).astype(bf16) for x in (qg, kg, vg)]
+        parts.append(att_ref[t, :, :WIDE])
+        grad_ref[t] = jnp.concatenate(
+            [x[:HALF] for x in parts] + [x[HALF:] for x in parts], axis=1
+        )
 
 
 def grad_att_kernel(w_ref, *refs):
@@ -189,15 +207,13 @@
 
 
 def weight_kernel(table_ref, att_ref, *refs):
-    out_refs, scr = refs[FRAMES : FRAMES + 4], refs[FRAMES + 4]
+    out_ref = refs[FRAMES]
     total = None
     for i in range(FRAMES):
         term = t_dot(att_ref[table_ref[0, WHERE + i]][:, :WIDE], refs[i][...])
         total = term if total is None else total + term
     for s in range(4):
-        scr[s] = total[SUB * s : SUB * (s + 1)]
-    for k in range(4):
-        out_refs[k][...] = scr[table_ref[0, Y_NEXT + k]].astype(out_refs[k].dtype)
+        out_ref[s] = total[SUB * s : SUB * (s + 1)].astype(bf16)
 
 
 def halve_kernel(own_ref, in_ref, keep_ref, send_ref):
@@ -206,11 +222,10 @@
     send_ref[...] = (own_ref[half:] + in_ref[half:].astype(f32)).astype(send_ref.dtype)
 
 
-def planes_kernel(table_ref, *refs):
-    keep_ref, send_ref, scr = refs[4:]
-    total = refs[0][...]
-    for k in range(1, 4):
-        total = total + refs[k][...].astype(f32)
+def planes_kernel(table_ref, in_ref, keep_ref, send_ref, scr):
+    total = in_ref[0].astype(f32)
+    for s in range(1, 4):
+        total = total + in_ref[s].astype(f32)
     for f in range(FRAMES):
         scr[f] = total[:, WIDE * f : WIDE * (f + 1)]
     for r in range(4):
@@ -240,16 +255,26 @@
 
 
 def final_kernel(table_ref, in_ref, *refs):
-    mixed_ref, grad_ref = refs[FRAMES:]
-    total = None
+    w_refs, mixed_ref, grad_ref = refs[:-2], refs[-2], refs[-1]
+    for half in range(2):
+        rows = slice(half * HALF, (half + 1) * HALF)
+        base = half * 4 * WIDE
+        total = None
+        for i in range(FRAMES):
+            att = in_ref[table_ref[0, ORIGIN + i], :, base + 3 * WIDE : base + 4 * WIDE]
+            w = w_refs[0][i] if len(w_refs) == 1 else w_refs[i][...]
+            term = dot(att, w)
+            total = term if total is None else total + term
+        mixed_ref[0, 0, rows, :] = total.astype(bf16)
+        for part in range(3):
+            at = base + part * WIDE
+            pieces = [in_ref[f, :, at : at + WIDE] for f in range(FRAMES)]
+            grad_ref[0, 0, rows, part * D : (part + 1) * D] = jnp.concatenate(pieces, axis=1)
+
+
+def stack_kernel(*refs):
     for i in range(FRAMES):
-        att = in_ref[table_ref[0, ORIGIN + i], :, 3 * WIDE :]
-        term = dot(att, refs[i][...])
-        total = term if total is None else total + term
-    mixed_ref[0, 0] = total.astype(bf16)
-    for part in range(3):
-        pieces = [in_ref[f, :, part * WIDE : (part + 1) * WIDE] for f in range(FRAMES)]
-        grad_ref[0, 0, :, part * D : (part + 1) * D] = jnp.concatenate(pieces, axis=1)
+        refs[FRAMES][i] = refs[i][...]
 
 
 def shift(x, axis, count, k):
@@ -287,12 +312,11 @@
     table = [2 * lax.rem(x_here + dx, 4) + (core ^ dc) for dx, dc in STEPS]
     table += [2 * lax.rem(x_here + 4 - dx, 4) + (core ^ dc) for dx, dc in STEPS]
     table += [z_here ^ r for r in (0, 4, 2, 6, 1, 5, 3, 7)] + [y_here ^ r for r in (0, 2, 1, 3)]
-    table += [lax.rem(y_here + k, 4) for k in range(4)]
     table = jnp.stack(table)[None]
 
     w_here = w_out[None]
     w_one, w_two = turn_back(w_here, 0), turn_back(w_here, 4)
-    packed = call(pack_kernel, sds((FRAMES, CAP, PACK), bf16), 3, smem=(0,))(counts, qkv, keep)
+    packed = call(pack_kernel, sds((FRAMES, HALF, PACK), bf16), 3, smem=(0,))(counts, qkv, keep)
     packed, g_own = lax.optimization_barrier((packed, grad_out[0, 0]))
     g_chips = [g_own]
     g_chips += [shift(g_chips[0], "x", 4, k) for k in (1, 3, 2)]
@@ -312,19 +336,18 @@
     w_last = flip(jnp.concatenate([w_sub, w_next]), "y", 4, 1)
     grid = (FRAMES, PATCHES, PATCHES)
     slim = (FRAMES, PATCHES, WIDE)
-    att, *saved = call(
+    att = call(
         forward_kernel,
-        (
-            sds((FRAMES, CAP, PATCHES), bf16),
-            sds((FRAMES, CAP, PATCHES), bf16),
-            sds(grid, bf16),
-            sds(grid, bf16),
-            sds(grid, bf16),
-            sds(slim, bf16),
-            sds((PATCHES // GROUP, BLOCK, 2 * BLOCK), f32),
-        ),
+        sds((FRAMES, CAP, PATCHES), bf16),
         1,
-        scratch=[VMEM(slim, bf16)],
+        scratch=[
+            VMEM((FRAMES, CAP, PATCHES), bf16),
+            VMEM(grid, bf16),
+            VMEM(grid, bf16),
+            VMEM(grid, bf16),
+            VMEM(slim, bf16),
+            VMEM(slim, bf16),
+        ],
     )(recv)
     w_last, att = lax.optimization_barrier((w_last, att))
     w_mine = call(
@@ -335,30 +358,24 @@
         smem=(0,),
     )(table, w_sub, w_next, w_last)
     grad_att = call(grad_att_kernel, sds((FRAMES, CAP, WIDE), bf16), 9)(w_mine, *g_all)
-    own, *other = call(
-        weight_kernel,
-        (sds((SUB, D), f32),) + (sds((SUB, D), bf16),) * 3,
-        10,
-        scratch=[VMEM((4, SUB, D), f32)],
-        smem=(0,),
-    )(table, att, *g_all)
-    other = [shift(piece, "y", 4, k) for k, piece in zip((1, 2, 3), other)]
+    own = call(weight_kernel, sds((4, SUB, D), bf16), 10, smem=(0,))(table, att, *g_all)
+    other = lax.all_to_all(own, "y", 0, 0, tiled=True)
     grad_att, own = lax.optimization_barrier((grad_att, own))
     grads = call(
         backward_kernel,
-        sds((FRAMES, CAP, 4 * WIDE), bf16),
-        9,
-        scratch=[VMEM(slim, bf16)] * 4,
+        sds((FRAMES, HALF, 8 * WIDE), bf16),
+        4,
+        scratch=[VMEM((FRAMES, CAP, PATCHES), bf16)] + [VMEM(grid, bf16)] * 3 + [VMEM(slim, bf16)] * 2,
         smem=(0,),
-    )(table, grad_att, att, *saved)
+    )(table, grad_att, att, recv)
     other, grads = lax.optimization_barrier((other, grads))
     own, other = call(
         planes_kernel,
         (sds((4, SUB, WIDE), f32), sds((4, SUB, WIDE), bf16)),
-        5,
+        2,
         scratch=[VMEM((8, SUB, WIDE), f32)],
         smem=(0,),
-    )(table, own, *other)
+    )(table, other)
     grads, other = lax.optimization_barrier((grads, other))
     w_mine, _ = lax.optimization_barrier((w_mine, recv))
     w_chips = [w_mine] + [shift(w_mine, "x", 4, k) for k in (3, 1, 2)]
@@ -367,6 +384,8 @@
     grad_back = lax.all_to_all(grads, FRAME, 0, 0, tiled=True)
 
     other = flip(other, "z", 8, 1)
+    w_stack = call(stack_kernel, sds((FRAMES, WIDE, D), bf16), 8)(*w_all)
+    own, w_stack = lax.optimization_barrier((own, w_stack))
     for mask, count, kind in ((1, 2, bf16), (2, 1, f32)):
         half = (count, SUB, WIDE)
         own, other = call(halve_kernel, (sds(half, f32), sds(half, kind)), 2)(
@@ -376,9 +395,9 @@
     mixed, grad_qkv = call(
         final_kernel,
         (sds((1, 1, CAP, D), bf16), sds((1, 1, CAP, 3 * D), bf16)),
-        10,
+        3,
         smem=(0,),
-    )(table, grad_back, *w_all)
+    )(table, grad_back, w_stack)
     pieces, grad_qkv = lax.optimization_barrier((pieces, grad_qkv))
     grad_weight = call(last_kernel, sds((SUB, WIDE), f32), 2)(*pieces)
     return mixed, grad_qkv, grad_weight

time: 145 us -> 139 us (0.959)
  waiting for transfers between devices: 56.7 us -> 49.7 us
  Pallas kernels: 25.1 us -> 30 us
  local copies, waits for them, and re-layouts: 13.3 us -> 10 us
    ppermute x17 -> x14, starting transfers between devices: 17.1 us -> 12.1 us  [shift(): return lax.ppermute(x, axis, [(i, (i + k) % count) for i in range(count)])]
    pallas_call x12 -> x13, Pallas kernels: 25.1 us -> 30 us  [run(): pl.pallas_call(kernel, grid=(1,), out_shape=out_shape, in_specs=specs, ou...]
    all_to_all x0 -> x1, starting transfers between devices: none -> 4.46 us  [shards(): other = lax.all_to_all(own, 'y', 0, 0, tiled=True)]
    ppermute x6, waiting for transfers between devices: 20.8 us -> 16.7 us  [flip(): return lax.ppermute(x, axis, [(i, i ^ mask) for i in range(count)])]
    unnamed x36 -> x18, local copies, waits for them, and re-layouts: 13.2 us -> 9.92 us
    all_to_all x1, waiting for transfers between devices: 5.76 us -> 3.04 us  [shards(): recv = lax.all_to_all(packed, FRAME, 0, 0, tiled=True)]
    ppermute x17 -> x14, waiting for transfers between devices: 3.56 us -> 3.78 us  [shift(): return lax.ppermute(x, axis, [(i, (i + k) % count) for i in range(count)])]
  transfers between devices with their start and end apart: 29 -> 27, of which waited for: 10 -> 11; matrix products, arithmetic and copies ran while one was open for 0% -> 1% of each run, Pallas kernels for 16% -> 20%
where the time goes in v3:
time: 139 us; the launch traced here: 138 us
  waiting for transfers between devices  49.7 us (36%)
  starting transfers between devices  46.3 us (33%)
  Pallas kernels  30 us (22%)
  local copies, waits for them, and re-layouts  10 us (7%)
  between operations  1.52 us (1%)
    pallas_call x13, Pallas kernels, run(): pl.pallas_call(kernel, grid=(1,), out_shape=out_shape, in_specs=specs, ou...  30 us
    ppermute x2, waiting for transfers between devices, turn_back(): return lax.ppermute(x, ALL, pairs)  18.8 us
    ppermute x6, waiting for transfers between devices, flip(): return lax.ppermute(x, axis, [(i, i ^ mask) for i in range(count)])  16.7 us
    ppermute x14, starting transfers between devices, shift(): return lax.ppermute(x, axis, [(i, (i + k) % count) for i in range(count)])  12.1 us
    ppermute x2, starting transfers between devices, turn(): return lax.ppermute(x, ALL, pairs)  10.8 us
    unnamed x18, local copies, waits for them, and re-layouts  9.92 us
    all_to_all x1, waiting for transfers between devices, shards(): grad_back = lax.all_to_all(grads, FRAME, 0, 0, tiled=True)  7.37 us
    ppermute x6, starting transfers between devices, flip(): return lax.ppermute(x, axis, [(i, i ^ mask) for i in range(count)])  7.07 us
  transfers between devices with their start and end apart: 27, of which 11 were waited for; matrix products, arithmetic and copies ran while one was open for 1% of the time, Pallas kernels for 20%

profile of v3, /device:TPU:128, one launch (start us, length us, event | category | flops | bytes accessed | tf_op | source)
XLA Modules:
  0.0 138.3 jit_solution(92762547265258067)
XLA Ops:
  1.3 1.4 %copy-done.4 = bf16[1,1,192,4224]{3,2,1,0:T(8,128)(2,1)S(1)} copy-done((bf16[1,1,192,4224]{3,2,1,0:T(8,128)(2,1)S(1)}, bf16[1,1,192,4224]{3,2,1,0:T(8,128)(2,1)}, u32[]{:S(2)}) %copy-start.4) | copy-done | bytes 1622040
  3.4 1.9 %shard_map.76 = bf16[8,96,1152]{2,1,0:T(8,128)(2,1)} custom-call(s32[1,1]{1,0:T(1,128)S(6)} %copy.8.counts_ref, bf16[1,1,192,4224]{3,2,1,0:T(8,128)(2,1)S(1)} %copy-done.4, s32[1,1,192]{2,1,0:T(1,128)S(1)} %copy-done.7), custom_call_target="tpu_custom_call" | custom-call | tf_op jit(solution)/shard_map/pallas_call | solution.py:62
  5.3 3.0 %collective-permute-start.2 = (bf16[192,1408]{1,0:T(8,128)(2,1)}, bf16[192,1408]{1,0:T(8,128)(2,1)}, u32[]{:S(2)}, u32[]{:S(2)}) collective-permute-start(bf16[192,1408]{1,0:T(8,128)(2,1)} %bitcast.23.refs_0_), channel_id=1, source_target_pairs={{0,4},{2,6},{4,0},{6,2},{1,5},{3,7},{5,1},{7,3},{8,12},{10,14},{12... | collective-permute-start | bytes 1622024 | tf_op jit(solution)/shard_map/ppermute | solution.py:281
  8.3 1.1 collective-permute-start.1
  11.0 3.0 %collective-permute-start.3 = (bf16[1,44,176]{2,1,0:T(8,128)(2,1)S(1)}, bf16[1,44,176]{2,1,0:T(8,128)(2,1)S(1)}, u32[]{:S(2)}, u32[]{:S(2)}) collective-permute-start(bf16[1,44,176]{2,1,0:T(8,128)(2,1)S(1)} %bitcast.36), channel_id=1, source_target_pairs={{0,0},{1,32},{2,64},{3,96},{4,128},{5,160},{6,192},{7,224},{8,8},{... | collective-permute-start | bytes 46472 | tf_op jit(solution)/shard_map/ppermute | solution.py:302
  14.0 18.8 %collective-permute-done.4.refs_1_ = bf16[1,44,176]{2,1,0:T(8,128)(2,1)S(1)} collective-permute-done((bf16[1,44,176]{2,1,0:T(8,128)(2,1)S(1)}, bf16[1,44,176]{2,1,0:T(8,128)(2,1)S(1)}, u32[]{:S(2)}, u32[]{:S(2)}) %collective-permute-start.4) | collective-permute-done | bytes 15520 | tf_op jit(solution)/shard_map/ppermute | solution.py:302
  33.4 4.7 %all-to-all-start = ((bf16[8,96,1152]{2,1,0:T(8,128)(2,1)}), bf16[8,96,1152]{2,1,0:T(8,128)(2,1)S(1)}, u32[]{:S(2)}, u32[]{:S(2)}) async-start(bf16[8,96,1152]{2,1,0:T(8,128)(2,1)} %shard_map.76), calls=%async_computation | async-start | bytes 3538944 | tf_op jit(solution)/shard_map/all_to_all | solution.py:324
  38.1 1.3 collective-permute-start.5
  39.4 4.9 %collective-permute-done.5.refs_2_ = bf16[2,44,176]{2,1,0:T(8,128)(2,1)S(1)} collective-permute-done((bf16[2,44,176]{2,1,0:T(8,128)(2,1)S(1)}, bf16[2,44,176]{2,1,0:T(8,128)(2,1)S(1)}, u32[]{:S(2)}, u32[]{:S(2)}) %collective-permute-start.5) | collective-permute-done | bytes 31008 | tf_op jit(solution)/shard_map/ppermute | solution.py:292
  44.5 4.6 %collective-permute-done.6.refs_3_ = bf16[4,44,176]{2,1,0:T(8,128)(2,1)S(1)} collective-permute-done((bf16[4,44,176]{2,1,0:T(8,128)(2,1)S(1)}, bf16[4,44,176]{2,1,0:T(8,128)(2,1)S(1)}, u32[]{:S(2)}, u32[]{:S(2)}) %collective-permute-start.6) | collective-permute-done | bytes 61984 | tf_op jit(solution)/shard_map/ppermute | solution.py:292
  49.8 3.3 %collective-permute-start.7 = (bf16[1,44,1408]{2,1,0:T(8,128)(2,1)S(1)}, bf16[1,44,1408]{2,1,0:T(8,128)(2,1)S(1)}, u32[]{:S(2)}, u32[]{:S(2)}) collective-permute-start(bf16[1,44,1408]{2,1,0:T(8,128)(2,1)S(1)} %shard_map.77.one_ref), channel_id=1, source_target_pairs={{0,16},{8,24},{16,0},{24,8},{1,17},{9,25},{17,1},{25,9},{2,18},{10... | collective-permute-start | bytes 371720 | tf_op jit(solution)/shard_map/ppermute | solution.py:292
  54.1 2.3 %collective-permute-done.7.two_ref = bf16[1,44,1408]{2,1,0:T(8,128)(2,1)S(1)} collective-permute-done((bf16[1,44,1408]{2,1,0:T(8,128)(2,1)S(1)}, bf16[1,44,1408]{2,1,0:T(8,128)(2,1)S(1)}, u32[]{:S(2)}, u32[]{:S(2)}) %collective-permute-start.7) | collective-permute-done | bytes 123936 | tf_op jit(solution)/shard_map/ppermute | solution.py:292
  57.1 1.6 %collective-permute-start.8 = (bf16[2,44,1408]{2,1,0:T(8,128)(2,1)}, bf16[2,44,1408]{2,1,0:T(8,128)(2,1)S(1)}, u32[]{:S(2)}, u32[]{:S(2)}) collective-permute-start(bf16[2,44,1408]{2,1,0:T(8,128)(2,1)} %pad_maximum_fusion), channel_id=1, source_target_pairs={{0,8},{8,0},{16,24},{24,16},{1,9},{9,1},{17,25},{25,17},{2,10},{10... | collective-permute-start | bytes 743432 | tf_op jit(solution)/shard_map/ppermute | solution.py:292
  58.7 3.0 %all-to-all-done.recv_ref = bf16[8,96,1152]{2,1,0:T(8,128)(2,1)S(1)} async-done(((bf16[8,96,1152]{2,1,0:T(8,128)(2,1)}), bf16[8,96,1152]{2,1,0:T(8,128)(2,1)S(1)}, u32[]{:S(2)}, u32[]{:S(2)}) %all-to-all-start) | async-done | bytes 1769504 | tf_op jit(solution)/shard_map/all_to_all | solution.py:324
  61.7 3.6 %shard_map.78.att_ref = bf16[8,192,256]{2,1,0:T(8,128)(2,1)S(1)} custom-call(bf16[8,96,1152]{2,1,0:T(8,128)(2,1)S(1)} %all-to-all-done.recv_ref), custom_call_target="tpu_custom_call" | custom-call | tf_op jit(solution)/shard_map/pallas_call | solution.py:62
  67.7 1.7 %collective-permute-start.15 = (bf16[176,1408]{1,0:T(8,128)(2,1)S(1)}, bf16[176,1408]{1,0:T(8,128)(2,1)S(1)}, u32[]{:S(2)}, u32[]{:S(2)}) collective-permute-start(bf16[176,1408]{1,0:T(8,128)(2,1)S(1)} %shard_map.80.w_ref.refs_0_), channel_id=1, source_target_pairs={{0,4},{2,6},{4,0},{6,2},{1,5},{3,7},{5,1},{7,3},{8,12},{10,14},{12... | collective-permute-start | bytes 1486856 | tf_op jit(solution)/shard_map/ppermute | solution.py:281
  70.0 2.7 %collective-permute-start.13 = (bf16[176,1408]{1,0:T(8,128)(2,1)S(1)}, bf16[176,1408]{1,0:T(8,128)(2,1)}, u32[]{:S(2)}, u32[]{:S(2)}) collective-permute-start(bf16[176,1408]{1,0:T(8,128)(2,1)S(1)} %shard_map.80.w_ref.refs_0_), channel_id=1, source_target_pairs={{0,6},{2,0},{4,2},{6,4},{1,7},{3,1},{5,3},{7,5},{8,14},{10,8},{12,... | collective-permute-start | bytes 1486856 | tf_op jit(solution)/shard_map/ppermute | solution.py:281
  72.6 3.5 %shard_map.79 = bf16[4,44,1408]{2,1,0:T(8,128)(2,1)S(1)} custom-call(s32[1,28]{1,0:T(1,128)S(1)} %bitcast.29, bf16[8,192,256]{2,1,0:T(8,128)(2,1)S(1)} %shard_map.78.att_ref, bf16[192,1408]{1,0:T(8,128)(2,1)} %bitcast.23.refs_0_, bf16[192,1408]{1,0:T(8,128)(2,1)} %collective-permute-done.9.refs_1_, bf16[192,1408]{1,0:T(8,128)(2,1)} %collective-permute-done.refs_2_, ...), custom_call_target="tpu_custom_call" | custom-call | tf_op jit(solution)/shard_map/pallas_call | solution.py:62
  77.0 4.5 %all-to-all-start.1 = ((bf16[4,44,1408]{2,1,0:T(8,128)(2,1)}), bf16[4,44,1408]{2,1,0:T(8,128)(2,1)}, u32[]{:S(2)}, u32[]{:S(2)}) async-start(bf16[4,44,1408]{2,1,0:T(8,128)(2,1)} %copy-done.3), calls=%async_computation.1 | async-start | bytes 1081344 | tf_op jit(solution)/shard_map/all_to_all | solution.py:362
  81.4 3.6 %shard_map.81.grad_att_ref = bf16[8,192,176]{2,1,0:T(8,128)(2,1)S(1)} custom-call(bf16[176,1408]{1,0:T(8,128)(2,1)S(1)} %shard_map.80.w_ref.refs_0_, bf16[192,1408]{1,0:T(8,128)(2,1)} %bitcast.23.refs_0_, bf16[192,1408]{1,0:T(8,128)(2,1)} %collective-permute-done.9.refs_1_, bf16[192,1408]{1,0:T(8,128)(2,1)} %collective-permute-done.refs_2_, ...), custom_call_target="tpu_custom_call" | custom-call | tf_op jit(solution)/shard_map/pallas_call | solution.py:62
  85.0 9.3 %shard_map.82 = bf16[8,96,1408]{2,1,0:T(8,128)(2,1)S(1)} custom-call(s32[1,28]{1,0:T(1,128)S(1)} %bitcast.30, bf16[8,192,176]{2,1,0:T(8,128)(2,1)S(1)} %shard_map.81.grad_att_ref, bf16[8,192,256]{2,1,0:T(8,128)(2,1)S(1)} %shard_map.78.att_ref, bf16[8,96,1152]{2,1,0:T(8,128)(2,1)S(1)} %all-to-all-done.recv_ref), custom_call_target="tpu_custom_call" | custom-call | tf_op jit(solution)/shard_map/pallas_call | solution.py:62
  94.3 1.4 copy-done.2
  95.7 1.3 shard_map.83
  97.0 3.6 %all-to-all-start.2 = ((bf16[8,96,1408]{2,1,0:T(8,128)(2,1)}), bf16[8,96,1408]{2,1,0:T(8,128)(2,1)S(1)}, u32[]{:S(2)}, u32[]{:S(2)}) async-start(bf16[8,96,1408]{2,1,0:T(8,128)(2,1)} %copy-done.2), calls=%async_computation.2 | async-start | bytes 4325376 | tf_op jit(solution)/shard_map/all_to_all | solution.py:384
  102.8 1.6 %collective-permute-done.17.refs_3_ = bf16[176,1408]{1,0:T(8,128)(2,1)S(1)} collective-permute-done((bf16[176,1408]{1,0:T(8,128)(2,1)}, bf16[176,1408]{1,0:T(8,128)(2,1)S(1)}, u32[]{:S(2)}, u32[]{:S(2)}) %collective-permute-start.17) | collective-permute-done | bytes 495648 | tf_op jit(solution)/shard_map/ppermute | solution.py:281
  105.1 1.5 %shard_map.84.refs_0_ = bf16[8,176,1408]{2,1,0:T(8,128)(2,1)S(1)} custom-call(bf16[176,1408]{1,0:T(8,128)(2,1)S(1)} %shard_map.80.w_ref.refs_0_, bf16[176,1408]{1,0:T(8,128)(2,1)S(1)} %collective-permute-done.16.refs_1_, bf16[176,1408]{1,0:T(8,128)(2,1)} %collective-permute-done.13.refs_2_, bf16[176,1408]{1,0:T(8,128)(2,1)S(1)} %collective-permute-done.17.refs_3_, ...), custom_call_target="tpu_custom_call" | custom-call | tf_op jit(solution)/shard_map/pallas_call | solution.py:62
  106.6 1.9 %copy-done = bf16[8,176,1408]{2,1,0:T(8,128)(2,1)} copy-done((bf16[8,176,1408]{2,1,0:T(8,128)(2,1)}, bf16[8,176,1408]{2,1,0:T(8,128)(2,1)S(1)}, u32[]{:S(2)}) %copy-start) | copy-done | bytes 3964952
  109.1 4.9 %collective-permute-done.21.in_ref = bf16[2,44,176]{2,1,0:T(8,128)(2,1)S(1)} collective-permute-done((bf16[2,44,176]{2,1,0:T(8,128)(2,1)S(1)}, bf16[2,44,176]{2,1,0:T(8,128)(2,1)S(1)}, u32[]{:S(2)}, u32[]{:S(2)}) %collective-permute-start.21) | collective-permute-done | bytes 31008 | tf_op jit(solution)/shard_map/ppermute | solution.py:292
  114.1 10.7 %collective-permute-start.22 = (f32[44,176]{1,0:T(8,128)S(1)}, f32[44,176]{1,0:T(8,128)S(1)}, u32[]{:S(2)}, u32[]{:S(2)}) collective-permute-start(f32[44,176]{1,0:T(8,128)S(1)} %bitcast.33), channel_id=1, source_target_pairs={{0,0},{1,32},{2,64},{3,96},{4,128},{5,160},{6,192},{7,224},{8,8},{... | collective-permute-start | bytes 92936 | tf_op jit(solution)/shard_map/ppermute | solution.py:297
  124.8 7.4 %all-to-all-done.2.in_ref = bf16[8,96,1408]{2,1,0:T(8,128)(2,1)S(1)} async-done(((bf16[8,96,1408]{2,1,0:T(8,128)(2,1)}), bf16[8,96,1408]{2,1,0:T(8,128)(2,1)S(1)}, u32[]{:S(2)}, u32[]{:S(2)}) %all-to-all-start.2) | async-done | bytes 2162720 | tf_op jit(solution)/shard_map/all_to_all | solution.py:384
  132.1 2.1 %copy-done.1 = bf16[8,176,1408]{2,1,0:T(8,128)(2,1)S(1)} copy-done((bf16[8,176,1408]{2,1,0:T(8,128)(2,1)S(1)}, bf16[8,176,1408]{2,1,0:T(8,128)(2,1)}, u32[]{:S(2)}) %copy-start.1) | copy-done | bytes 3964952
  134.3 3.4 %shard_map.85 = (bf16[1,1,192,1408]{3,2,1,0:T(8,128)(2,1)}, bf16[1,1,192,4224]{3,2,1,0:T(8,128)(2,1)}) custom-call(s32[1,28]{1,0:T(1,128)S(1)} %bitcast.32, bf16[8,96,1408]{2,1,0:T(8,128)(2,1)S(1)} %all-to-all-done.2.in_ref, bf16[8,176,1408]{2,1,0:T(8,128)(2,1)S(1)} %copy-done.1), custom_call_target="tpu_custom_call" | custom-call | tf_op jit(solution)/shard_map/pallas_call | solution.py:62
  (57 shorter events, 13.4 us)
Async XLA Ops:
  1.3 1.4 %copy-start.4 = (bf16[1,1,192,4224]{3,2,1,0:T(8,128)(2,1)S(1)}, bf16[1,1,192,4224]{3,2,1,0:T(8,128)(2,1)}, u32[]{:S(2)}) copy-start(bf16[1,1,192,4224]{3,2,1,0:T(8,128)(2,1)} %qkv_ref.1) | copy-start | bytes 4866052
  3.4 7.0 %copy-start.8 = (bf16[44,176]{1,0:T(8,128)(2,1)S(1)}, bf16[44,176]{1,0:T(8,128)(2,1)}, u32[]{:S(2)}) copy-start(bf16[44,176]{1,0:T(8,128)(2,1)} %param.9) | copy-start | bytes 46468
  5.3 27.5 %collective-permute-start.2 = (bf16[192,1408]{1,0:T(8,128)(2,1)}, bf16[192,1408]{1,0:T(8,128)(2,1)}, u32[]{:S(2)}, u32[]{:S(2)}) collective-permute-start(bf16[192,1408]{1,0:T(8,128)(2,1)} %bitcast.23.refs_0_), channel_id=1, source_target_pairs={{0,4},{2,6},{4,0},{6,2},{1,5},{3,7},{5,1},{7,3},{8,12},{10,14},{12... | collective-permute-start | bytes 1622024 | tf_op jit(solution)/shard_map/ppermute | solution.py:281
  8.3 25.1 %collective-permute-start.1 = (bf16[192,1408]{1,0:T(8,128)(2,1)}, bf16[192,1408]{1,0:T(8,128)(2,1)}, u32[]{:S(2)}, u32[]{:S(2)}) collective-permute-start(bf16[192,1408]{1,0:T(8,128)(2,1)} %bitcast.23.refs_0_), channel_id=1, source_target_pairs={{0,6},{2,0},{4,2},{6,4},{1,7},{3,1},{5,3},{7,5},{8,14},{10,8},{12,... | collective-permute-start | bytes 1622024 | tf_op jit(solution)/shard_map/ppermute | solution.py:281
  9.5 23.9 %collective-permute-start = (bf16[192,1408]{1,0:T(8,128)(2,1)}, bf16[192,1408]{1,0:T(8,128)(2,1)}, u32[]{:S(2)}, u32[]{:S(2)}) collective-permute-start(bf16[192,1408]{1,0:T(8,128)(2,1)} %bitcast.23.refs_0_), channel_id=1, source_target_pairs={{0,2},{2,4},{4,6},{6,0},{1,3},{3,5},{5,7},{7,1},{8,10},{10,12},{12... | collective-permute-start | bytes 1622024 | tf_op jit(solution)/shard_map/ppermute | solution.py:281
  10.4 22.4 %collective-permute-start.4 = (bf16[1,44,176]{2,1,0:T(8,128)(2,1)S(1)}, bf16[1,44,176]{2,1,0:T(8,128)(2,1)S(1)}, u32[]{:S(2)}, u32[]{:S(2)}) collective-permute-start(bf16[1,44,176]{2,1,0:T(8,128)(2,1)S(1)} %bitcast.35), channel_id=1, source_target_pairs={{0,128},{1,160},{2,192},{3,224},{4,0},{5,32},{6,64},{7,96},{8,136}... | collective-permute-start | bytes 46472 | tf_op jit(solution)/shard_map/ppermute | solution.py:302
  11.0 21.8 %collective-permute-start.3 = (bf16[1,44,176]{2,1,0:T(8,128)(2,1)S(1)}, bf16[1,44,176]{2,1,0:T(8,128)(2,1)S(1)}, u32[]{:S(2)}, u32[]{:S(2)}) collective-permute-start(bf16[1,44,176]{2,1,0:T(8,128)(2,1)S(1)} %bitcast.36), channel_id=1, source_target_pairs={{0,0},{1,32},{2,64},{3,96},{4,128},{5,160},{6,192},{7,224},{8,8},{... | collective-permute-start | bytes 46472 | tf_op jit(solution)/shard_map/ppermute | solution.py:302
  33.4 28.4 %all-to-all-start = ((bf16[8,96,1152]{2,1,0:T(8,128)(2,1)}), bf16[8,96,1152]{2,1,0:T(8,128)(2,1)S(1)}, u32[]{:S(2)}, u32[]{:S(2)}) async-start(bf16[8,96,1152]{2,1,0:T(8,128)(2,1)} %shard_map.76), calls=%async_computation | async-start | bytes 3538944 | tf_op jit(solution)/shard_map/all_to_all | solution.py:324
  38.1 6.1 %collective-permute-start.5 = (bf16[2,44,176]{2,1,0:T(8,128)(2,1)S(1)}, bf16[2,44,176]{2,1,0:T(8,128)(2,1)S(1)}, u32[]{:S(2)}, u32[]{:S(2)}) collective-permute-start(bf16[2,44,176]{2,1,0:T(8,128)(2,1)S(1)} %pad_maximum_fusion.2), channel_id=1, source_target_pairs={{0,64},{32,96},{64,0},{96,32},{128,192},{160,224},{192,128},{224,1... | collective-permute-start | bytes 92936 | tf_op jit(solution)/shard_map/ppermute | solution.py:292
  44.2 4.9 %collective-permute-start.6 = (bf16[4,44,176]{2,1,0:T(8,128)(2,1)S(1)}, bf16[4,44,176]{2,1,0:T(8,128)(2,1)S(1)}, u32[]{:S(2)}, u32[]{:S(2)}) collective-permute-start(bf16[4,44,176]{2,1,0:T(8,128)(2,1)S(1)} %pad_maximum_fusion.1), channel_id=1, source_target_pairs={{0,32},{32,0},{64,96},{96,64},{128,160},{160,128},{192,224},{224,1... | collective-permute-start | bytes 185864 | tf_op jit(solution)/shard_map/ppermute | solution.py:292
  49.8 6.6 %collective-permute-start.7 = (bf16[1,44,1408]{2,1,0:T(8,128)(2,1)S(1)}, bf16[1,44,1408]{2,1,0:T(8,128)(2,1)S(1)}, u32[]{:S(2)}, u32[]{:S(2)}) collective-permute-start(bf16[1,44,1408]{2,1,0:T(8,128)(2,1)S(1)} %shard_map.77.one_ref), channel_id=1, source_target_pairs={{0,16},{8,24},{16,0},{24,8},{1,17},{9,25},{17,1},{25,9},{2,18},{10... | collective-permute-start | bytes 371720 | tf_op jit(solution)/shard_map/ppermute | solution.py:292
  53.1 16.3 %collective-permute-start.9 = (bf16[192,1408]{1,0:T(8,128)(2,1)}, bf16[192,1408]{1,0:T(8,128)(2,1)}, u32[]{:S(2)}, u32[]{:S(2)}) collective-permute-start(bf16[192,1408]{1,0:T(8,128)(2,1)} %bitcast.23.refs_0_), channel_id=1, source_target_pairs={{0,1},{1,0},{2,3},{3,2},{4,5},{5,4},{6,7},{7,6},{8,9},{9,8},{10,11... | collective-permute-start | bytes 1622024 | tf_op jit(solution)/shard_map/ppermute | solution.py:281
  53.1 16.9 %collective-permute-start.10 = (bf16[192,1408]{1,0:T(8,128)(2,1)}, bf16[192,1408]{1,0:T(8,128)(2,1)}, u32[]{:S(2)}, u32[]{:S(2)}) collective-permute-start(bf16[192,1408]{1,0:T(8,128)(2,1)} %collective-permute-done.refs_2_), channel_id=1, source_target_pairs={{0,1},{1,0},{2,3},{3,2},{4,5},{5,4},{6,7},{7,6},{8,9},{9,8},{10,11... | collective-permute-start | bytes 1622024 | tf_op jit(solution)/shard_map/ppermute | solution.py:281
  53.6 19.1 %collective-permute-start.11 = (bf16[192,1408]{1,0:T(8,128)(2,1)}, bf16[192,1408]{1,0:T(8,128)(2,1)}, u32[]{:S(2)}, u32[]{:S(2)}) collective-permute-start(bf16[192,1408]{1,0:T(8,128)(2,1)} %collective-permute-done.1.refs_4_), channel_id=1, source_target_pairs={{0,1},{1,0},{2,3},{3,2},{4,5},{5,4},{6,7},{7,6},{8,9},{9,8},{10,11... | collective-permute-start | bytes 1622024 | tf_op jit(solution)/shard_map/ppermute | solution.py:281
  53.6 19.1 %collective-permute-start.12 = (bf16[192,1408]{1,0:T(8,128)(2,1)}, bf16[192,1408]{1,0:T(8,128)(2,1)}, u32[]{:S(2)}, u32[]{:S(2)}) collective-permute-start(bf16[192,1408]{1,0:T(8,128)(2,1)} %collective-permute-done.2.refs_6_), channel_id=1, source_target_pairs={{0,1},{1,0},{2,3},{3,2},{4,5},{5,4},{6,7},{7,6},{8,9},{9,8},{10,11... | collective-permute-start | bytes 1622024 | tf_op jit(solution)/shard_map/ppermute | solution.py:281
  57.1 8.2 %collective-permute-start.8 = (bf16[2,44,1408]{2,1,0:T(8,128)(2,1)}, bf16[2,44,1408]{2,1,0:T(8,128)(2,1)S(1)}, u32[]{:S(2)}, u32[]{:S(2)}) collective-permute-start(bf16[2,44,1408]{2,1,0:T(8,128)(2,1)} %pad_maximum_fusion), channel_id=1, source_target_pairs={{0,8},{8,0},{16,24},{24,16},{1,9},{9,1},{17,25},{25,17},{2,10},{10... | collective-permute-start | bytes 743432 | tf_op jit(solution)/shard_map/ppermute | solution.py:292
  67.7 29.3 %collective-permute-start.15 = (bf16[176,1408]{1,0:T(8,128)(2,1)S(1)}, bf16[176,1408]{1,0:T(8,128)(2,1)S(1)}, u32[]{:S(2)}, u32[]{:S(2)}) collective-permute-start(bf16[176,1408]{1,0:T(8,128)(2,1)S(1)} %shard_map.80.w_ref.refs_0_), channel_id=1, source_target_pairs={{0,4},{2,6},{4,0},{6,2},{1,5},{3,7},{5,1},{7,3},{8,12},{10,14},{12... | collective-permute-start | bytes 1486856 | tf_op jit(solution)/shard_map/ppermute | solution.py:281
  69.4 27.6 %collective-permute-start.14 = (bf16[176,1408]{1,0:T(8,128)(2,1)S(1)}, bf16[176,1408]{1,0:T(8,128)(2,1)}, u32[]{:S(2)}, u32[]{:S(2)}) collective-permute-start(bf16[176,1408]{1,0:T(8,128)(2,1)S(1)} %shard_map.80.w_ref.refs_0_), channel_id=1, source_target_pairs={{0,2},{2,4},{4,6},{6,0},{1,3},{3,5},{5,7},{7,1},{8,10},{10,12},{12... | collective-permute-start | bytes 1486856 | tf_op jit(solution)/shard_map/ppermute | solution.py:281
  70.0 27.0 %collective-permute-start.13 = (bf16[176,1408]{1,0:T(8,128)(2,1)S(1)}, bf16[176,1408]{1,0:T(8,128)(2,1)}, u32[]{:S(2)}, u32[]{:S(2)}) collective-permute-start(bf16[176,1408]{1,0:T(8,128)(2,1)S(1)} %shard_map.80.w_ref.refs_0_), channel_id=1, source_target_pairs={{0,6},{2,0},{4,2},{6,4},{1,7},{3,1},{5,3},{7,5},{8,14},{10,8},{12,... | collective-permute-start | bytes 1486856 | tf_op jit(solution)/shard_map/ppermute | solution.py:281
  77.0 18.7 %all-to-all-start.1 = ((bf16[4,44,1408]{2,1,0:T(8,128)(2,1)}), bf16[4,44,1408]{2,1,0:T(8,128)(2,1)}, u32[]{:S(2)}, u32[]{:S(2)}) async-start(bf16[4,44,1408]{2,1,0:T(8,128)(2,1)} %copy-done.3), calls=%async_computation.1 | async-start | bytes 1081344 | tf_op jit(solution)/shard_map/all_to_all | solution.py:362
  94.3 1.4 %copy-start.2 = (bf16[8,96,1408]{2,1,0:T(8,128)(2,1)}, bf16[8,96,1408]{2,1,0:T(8,128)(2,1)S(1)}, u32[]{:S(2)}) copy-start(bf16[8,96,1408]{2,1,0:T(8,128)(2,1)S(1)} %shard_map.82) | copy-start | bytes 6488068
  97.0 35.1 %all-to-all-start.2 = ((bf16[8,96,1408]{2,1,0:T(8,128)(2,1)}), bf16[8,96,1408]{2,1,0:T(8,128)(2,1)S(1)}, u32[]{:S(2)}, u32[]{:S(2)}) async-start(bf16[8,96,1408]{2,1,0:T(8,128)(2,1)} %copy-done.2), calls=%async_computation.2 | async-start | bytes 4325376 | tf_op jit(solution)/shard_map/all_to_all | solution.py:384
  100.6 2.1 %collective-permute-start.16 = (bf16[176,1408]{1,0:T(8,128)(2,1)S(1)}, bf16[176,1408]{1,0:T(8,128)(2,1)S(1)}, u32[]{:S(2)}, u32[]{:S(2)}) collective-permute-start(bf16[176,1408]{1,0:T(8,128)(2,1)S(1)} %shard_map.80.w_ref.refs_0_), channel_id=1, source_target_pairs={{0,1},{1,0},{2,3},{3,2},{4,5},{5,4},{6,7},{7,6},{8,9},{9,8},{10,11... | collective-permute-start | bytes 1486856 | tf_op jit(solution)/shard_map/ppermute | solution.py:281
  101.0 3.4 %collective-permute-start.17 = (bf16[176,1408]{1,0:T(8,128)(2,1)}, bf16[176,1408]{1,0:T(8,128)(2,1)S(1)}, u32[]{:S(2)}, u32[]{:S(2)}) collective-permute-start(bf16[176,1408]{1,0:T(8,128)(2,1)} %collective-permute-done.13.refs_2_), channel_id=1, source_target_pairs={{0,1},{1,0},{2,3},{3,2},{4,5},{5,4},{6,7},{7,6},{8,9},{9,8},{10,11... | collective-permute-start | bytes 1486856 | tf_op jit(solution)/shard_map/ppermute | solution.py:281
  101.2 3.9 %collective-permute-start.18 = (bf16[176,1408]{1,0:T(8,128)(2,1)}, bf16[176,1408]{1,0:T(8,128)(2,1)S(1)}, u32[]{:S(2)}, u32[]{:S(2)}) collective-permute-start(bf16[176,1408]{1,0:T(8,128)(2,1)} %collective-permute-done.14.refs_4_), channel_id=1, source_target_pairs={{0,1},{1,0},{2,3},{3,2},{4,5},{5,4},{6,7},{7,6},{8,9},{9,8},{10,11... | collective-permute-start | bytes 1486856 | tf_op jit(solution)/shard_map/ppermute | solution.py:281
  101.5 3.6 %collective-permute-start.19 = (bf16[176,1408]{1,0:T(8,128)(2,1)S(1)}, bf16[176,1408]{1,0:T(8,128)(2,1)S(1)}, u32[]{:S(2)}, u32[]{:S(2)}) collective-permute-start(bf16[176,1408]{1,0:T(8,128)(2,1)S(1)} %collective-permute-done.15.refs_6_), channel_id=1, source_target_pairs={{0,1},{1,0},{2,3},{3,2},{4,5},{5,4},{6,7},{7,6},{8,9},{9,8},{10,11... | collective-permute-start | bytes 1486856 | tf_op jit(solution)/shard_map/ppermute | solution.py:281
  101.7 6.7 %collective-permute-start.20 = (bf16[4,44,176]{2,1,0:T(8,128)(2,1)S(1)}, bf16[4,44,176]{2,1,0:T(8,128)(2,1)S(1)}, u32[]{:S(2)}, u32[]{:S(2)}) collective-permute-start(bf16[4,44,176]{2,1,0:T(8,128)(2,1)S(1)} %get-tuple-element.64), channel_id=1, source_target_pairs={{0,32},{32,0},{64,96},{96,64},{128,160},{160,128},{192,224},{224,1... | collective-permute-start | bytes 185864 | tf_op jit(solution)/shard_map/ppermute | solution.py:292
  106.6 1.9 %copy-start = (bf16[8,176,1408]{2,1,0:T(8,128)(2,1)}, bf16[8,176,1408]{2,1,0:T(8,128)(2,1)S(1)}, u32[]{:S(2)}) copy-start(bf16[8,176,1408]{2,1,0:T(8,128)(2,1)S(1)} %shard_map.84.refs_0_) | copy-start | bytes 11894788
  108.5 5.5 %collective-permute-start.21 = (bf16[2,44,176]{2,1,0:T(8,128)(2,1)S(1)}, bf16[2,44,176]{2,1,0:T(8,128)(2,1)S(1)}, u32[]{:S(2)}, u32[]{:S(2)}) collective-permute-start(bf16[2,44,176]{2,1,0:T(8,128)(2,1)S(1)} %get-tuple-element.66), channel_id=1, source_target_pairs={{0,64},{32,96},{64,0},{96,32},{128,192},{160,224},{192,128},{224,1... | collective-permute-start | bytes 92936 | tf_op jit(solution)/shard_map/ppermute | solution.py:292
  114.0 23.7 %collective-permute-start.23 = (f32[44,176]{1,0:T(8,128)S(1)}, f32[44,176]{1,0:T(8,128)S(1)}, u32[]{:S(2)}, u32[]{:S(2)}) collective-permute-start(f32[44,176]{1,0:T(8,128)S(1)} %bitcast.34), channel_id=1, source_target_pairs={{0,4},{1,36},{2,68},{3,100},{4,132},{5,164},{6,196},{7,228},{8,12}... | collective-permute-start | bytes 92936 | tf_op jit(solution)/shard_map/ppermute | solution.py:297
  114.1 23.6 %collective-permute-start.22 = (f32[44,176]{1,0:T(8,128)S(1)}, f32[44,176]{1,0:T(8,128)S(1)}, u32[]{:S(2)}, u32[]{:S(2)}) collective-permute-start(f32[44,176]{1,0:T(8,128)S(1)} %bitcast.33), channel_id=1, source_target_pairs={{0,0},{1,32},{2,64},{3,96},{4,128},{5,160},{6,192},{7,224},{8,8},{... | collective-permute-start | bytes 92936 | tf_op jit(solution)/shard_map/ppermute | solution.py:297
  132.1 2.1 %copy-start.1 = (bf16[8,176,1408]{2,1,0:T(8,128)(2,1)S(1)}, bf16[8,176,1408]{2,1,0:T(8,128)(2,1)}, u32[]{:S(2)}) copy-start(bf16[8,176,1408]{2,1,0:T(8,128)(2,1)} %copy-done) | copy-start | bytes 11894788
  (4 other events, 3.1 us)

commit v4 on v3

--- a/solution.py
+++ b/solution.py
@@ -50,13 +50,17 @@
     return lax.broadcasted_iota(jnp.int32, shape, dim)
 
 
-def call(kernel, out_shape, n_in, flops=0, scratch=(), smem=()):
+def call(kernel, out_shape, n_in, flops=0, scratch=(), smem=(), hbm=()):
     def spec(shape):
         return pl.BlockSpec(shape, lambda i: (0,) * len(shape), pipeline_mode=pl.Buffered(1))
 
     def run(*args):
         specs = [
-            pl.BlockSpec(memory_space=pltpu.SMEM) if i in smem else spec(a.shape)
+            pl.BlockSpec(memory_space=pltpu.SMEM)
+            if i in smem
+            else pl.BlockSpec(memory_space=pltpu.HBM)
+            if i in hbm
+            else spec(a.shape)
             for i, a in enumerate(args)
         ]
         return pl.pallas_call(
@@ -255,26 +259,27 @@
 
 
 def final_kernel(table_ref, in_ref, *refs):
-    w_refs, mixed_ref, grad_ref = refs[:-2], refs[-2], refs[-1]
+    mixed_ref, grad_ref, w_ref, sems = refs[FRAMES:]
+    copies = [pltpu.make_async_copy(refs[i], w_ref.at[i], sems.at[i]) for i in range(FRAMES)]
+    for copy in copies:
+        copy.start()
+    for half in range(2):
+        rows = slice(half * HALF, (half + 1) * HALF)
+        for part in range(3):
+            at = half * 4 * WIDE + part * WIDE
+            pieces = [in_ref[f, :, at : at + WIDE] for f in range(FRAMES)]
+            grad_ref[0, 0, rows, part * D : (part + 1) * D] = jnp.concatenate(pieces, axis=1)
+    for copy in copies:
+        copy.wait()
     for half in range(2):
         rows = slice(half * HALF, (half + 1) * HALF)
         base = half * 4 * WIDE
         total = None
         for i in range(FRAMES):
             att = in_ref[table_ref[0, ORIGIN + i], :, base + 3 * WIDE : base + 4 * WIDE]
-            w = w_refs[0][i] if len(w_refs) == 1 else w_refs[i][...]
-            term = dot(att, w)
+            term = dot(att, w_ref[i])
             total = term if total is None else total + term
         mixed_ref[0, 0, rows, :] = total.astype(bf16)
-        for part in range(3):
-            at = base + part * WIDE
-            pieces = [in_ref[f, :, at : at + WIDE] for f in range(FRAMES)]
-            grad_ref[0, 0, rows, part * D : (part + 1) * D] = jnp.concatenate(pieces, axis=1)
-
-
-def stack_kernel(*refs):
-    for i in range(FRAMES):
-        refs[FRAMES][i] = refs[i][...]
 
 
 def shift(x, axis, count, k):
@@ -384,8 +389,6 @@
     grad_back = lax.all_to_all(grads, FRAME, 0, 0, tiled=True)
 
     other = flip(other, "z", 8, 1)
-    w_stack = call(stack_kernel, sds((FRAMES, WIDE, D), bf16), 8)(*w_all)
-    own, w_stack = lax.optimization_barrier((own, w_stack))
     for mask, count, kind in ((1, 2, bf16), (2, 1, f32)):
         half = (count, SUB, WIDE)
         own, other = call(halve_kernel, (sds(half, f32), sds(half, kind)), 2)(
@@ -395,9 +398,11 @@
     mixed, grad_qkv = call(
         final_kernel,
         (sds((1, 1, CAP, D), bf16), sds((1, 1, CAP, 3 * D), bf16)),
-        3,
+        10,
+        scratch=[VMEM((FRAMES, WIDE, D), bf16), pltpu.SemaphoreType.DMA((FRAMES,))],
         smem=(0,),
-    )(table, grad_back, w_stack)
+        hbm=range(2, 10),
+    )(table, grad_back, *w_all)
     pieces, grad_qkv = lax.optimization_barrier((pieces, grad_qkv))
     grad_weight = call(last_kernel, sds((SUB, WIDE), f32), 2)(*pieces)
     return mixed, grad_qkv, grad_weight

time: 139 us -> 143 us (1.029)
  starting transfers between devices: 46.3 us -> 36.2 us
  waiting for transfers between devices: 49.7 us -> 58.8 us
  local copies, waits for them, and re-layouts: 10 us -> 13.3 us
    ppermute x2, starting transfers between devices: 10.8 us -> 2.8 us  [turn(): return lax.ppermute(x, ALL, pairs)]
    all_to_all x1, waiting for transfers between devices: 7.37 us -> 13.7 us  [shards(): grad_back = lax.all_to_all(grads, FRAME, 0, 0, tiled=True)]
    ppermute x6, waiting for transfers between devices: 16.7 us -> 21.4 us  [flip(): return lax.ppermute(x, axis, [(i, i ^ mask) for i in range(count)])]
    unnamed x18 -> x30, local copies, waits for them, and re-layouts: 9.92 us -> 13.2 us
    ppermute x2, waiting for transfers between devices: 18.8 us -> 17.2 us  [turn_back(): return lax.ppermute(x, ALL, pairs)]
    pallas_call x13 -> x12, Pallas kernels: 30 us -> 30.8 us  [run(): pl.pallas_call(kernel, grid=(1,), out_shape=out_shape, in_specs=specs, ou...]
where the time goes in v4:
time: 143 us; the launch traced here: 141 us
  waiting for transfers between devices  58.8 us (41%)
  starting transfers between devices  36.2 us (25%)
  Pallas kernels  30.8 us (22%)
  local copies, waits for them, and re-layouts  13.3 us (9%)
  between operations  1.53 us (1%)
    pallas_call x12, Pallas kernels, run(): pl.pallas_call(kernel, grid=(1,), out_shape=out_shape, in_specs=specs, ou...  30.8 us
    ppermute x6, waiting for transfers between devices, flip(): return lax.ppermute(x, axis, [(i, i ^ mask) for i in range(count)])  21.4 us
    ppermute x2, waiting for transfers between devices, turn_back(): return lax.ppermute(x, ALL, pairs)  17.2 us
    all_to_all x1, waiting for transfers between devices, shards(): grad_back = lax.all_to_all(grads, FRAME, 0, 0, tiled=True)  13.7 us
    unnamed x30, local copies, waits for them, and re-layouts  13.2 us
    ppermute x14, starting transfers between devices, shift(): return lax.ppermute(x, axis, [(i, (i + k) % count) for i in range(count)])  11 us
    ppermute x6, starting transfers between devices, flip(): return lax.ppermute(x, axis, [(i, i ^ mask) for i in range(count)])  7.14 us
    all_to_all x1, starting transfers between devices, shards(): other = lax.all_to_all(own, 'y', 0, 0, tiled=True)  4.46 us
  transfers between devices with their start and end apart: 27, of which 11 were waited for; matrix products, arithmetic and copies ran while one was open for 1% of the time, Pallas kernels for 20%

profile of v4, /device:TPU:128, one launch (start us, length us, event | category | flops | bytes accessed | tf_op | source)
XLA Modules:
  0.0 141.4 jit_solution(10203922052140130184)
XLA Ops:
  1.3 1.4 %copy-done.2 = bf16[1,1,192,4224]{3,2,1,0:T(8,128)(2,1)S(1)} copy-done((bf16[1,1,192,4224]{3,2,1,0:T(8,128)(2,1)S(1)}, bf16[1,1,192,4224]{3,2,1,0:T(8,128)(2,1)}, u32[]{:S(2)}) %copy-start.2) | copy-done | bytes 1622040
  3.4 1.9 %shard_map.76 = bf16[8,96,1152]{2,1,0:T(8,128)(2,1)} custom-call(s32[1,1]{1,0:T(1,128)S(6)} %copy.8.counts_ref, bf16[1,1,192,4224]{3,2,1,0:T(8,128)(2,1)S(1)} %copy-done.2, s32[1,1,192]{2,1,0:T(1,128)S(1)} %copy-done.13), custom_call_target="tpu_custom_call" | custom-call | tf_op jit(solution)/shard_map/pallas_call | solution.py:66
  5.3 1.5 %collective-permute-start = (bf16[192,1408]{1,0:T(8,128)(2,1)}, bf16[192,1408]{1,0:T(8,128)(2,1)}, u32[]{:S(2)}, u32[]{:S(2)}) collective-permute-start(bf16[192,1408]{1,0:T(8,128)(2,1)} %bitcast.23.refs_0_), channel_id=1, source_target_pairs={{0,2},{2,4},{4,6},{6,0},{1,3},{3,5},{5,7},{7,1},{8,10},{10,12},{12... | collective-permute-start | bytes 1622024 | tf_op jit(solution)/shard_map/ppermute | solution.py:286
  6.8 1.7 %collective-permute-start.1 = (bf16[192,1408]{1,0:T(8,128)(2,1)}, bf16[192,1408]{1,0:T(8,128)(2,1)}, u32[]{:S(2)}, u32[]{:S(2)}) collective-permute-start(bf16[192,1408]{1,0:T(8,128)(2,1)} %bitcast.23.refs_0_), channel_id=1, source_target_pairs={{0,6},{2,0},{4,2},{6,4},{1,7},{3,1},{5,3},{7,5},{8,14},{10,8},{12,... | collective-permute-start | bytes 1622024 | tf_op jit(solution)/shard_map/ppermute | solution.py:286
  8.5 1.8 %collective-permute-start.2 = (bf16[192,1408]{1,0:T(8,128)(2,1)}, bf16[192,1408]{1,0:T(8,128)(2,1)}, u32[]{:S(2)}, u32[]{:S(2)}) collective-permute-start(bf16[192,1408]{1,0:T(8,128)(2,1)} %bitcast.23.refs_0_), channel_id=1, source_target_pairs={{0,4},{2,6},{4,0},{6,2},{1,5},{3,7},{5,1},{7,3},{8,12},{10,14},{12... | collective-permute-start | bytes 1622024 | tf_op jit(solution)/shard_map/ppermute | solution.py:286
  10.3 3.5 %collective-permute-start.3 = (bf16[1,44,176]{2,1,0:T(8,128)(2,1)S(1)}, bf16[1,44,176]{2,1,0:T(8,128)(2,1)S(1)}, u32[]{:S(2)}, u32[]{:S(2)}) collective-permute-start(bf16[1,44,176]{2,1,0:T(8,128)(2,1)S(1)} %bitcast.35), channel_id=1, source_target_pairs={{0,0},{1,32},{2,64},{3,96},{4,128},{5,160},{6,192},{7,224},{8,8},{... | collective-permute-start | bytes 46472 | tf_op jit(solution)/shard_map/ppermute | solution.py:307
  14.0 8.5 %collective-permute-done.3.refs_0_ = bf16[1,44,176]{2,1,0:T(8,128)(2,1)S(1)} collective-permute-done((bf16[1,44,176]{2,1,0:T(8,128)(2,1)S(1)}, bf16[1,44,176]{2,1,0:T(8,128)(2,1)S(1)}, u32[]{:S(2)}, u32[]{:S(2)}) %collective-permute-start.3) | collective-permute-done | bytes 15520 | tf_op jit(solution)/shard_map/ppermute | solution.py:307
  22.5 8.7 %collective-permute-done.4.refs_1_ = bf16[1,44,176]{2,1,0:T(8,128)(2,1)S(1)} collective-permute-done((bf16[1,44,176]{2,1,0:T(8,128)(2,1)S(1)}, bf16[1,44,176]{2,1,0:T(8,128)(2,1)S(1)}, u32[]{:S(2)}, u32[]{:S(2)}) %collective-permute-start.4) | collective-permute-done | bytes 15520 | tf_op jit(solution)/shard_map/ppermute | solution.py:307
  31.2 1.1 collective-permute-done.1.refs_4_
  32.2 2.2 %collective-permute-done.2.refs_6_ = bf16[192,1408]{1,0:T(8,128)(2,1)} collective-permute-done((bf16[192,1408]{1,0:T(8,128)(2,1)}, bf16[192,1408]{1,0:T(8,128)(2,1)}, u32[]{:S(2)}, u32[]{:S(2)}) %collective-permute-start.2) | collective-permute-done | bytes 540704 | tf_op jit(solution)/shard_map/ppermute | solution.py:286
  34.4 3.6 %all-to-all-start = ((bf16[8,96,1152]{2,1,0:T(8,128)(2,1)}), bf16[8,96,1152]{2,1,0:T(8,128)(2,1)S(1)}, u32[]{:S(2)}, u32[]{:S(2)}) async-start(bf16[8,96,1152]{2,1,0:T(8,128)(2,1)} %shard_map.76), calls=%async_computation | async-start | bytes 3538944 | tf_op jit(solution)/shard_map/all_to_all | solution.py:329
  38.9 5.3 %collective-permute-done.5.refs_2_ = bf16[2,44,176]{2,1,0:T(8,128)(2,1)S(1)} collective-permute-done((bf16[2,44,176]{2,1,0:T(8,128)(2,1)S(1)}, bf16[2,44,176]{2,1,0:T(8,128)(2,1)S(1)}, u32[]{:S(2)}, u32[]{:S(2)}) %collective-permute-start.5) | collective-permute-done | bytes 31008 | tf_op jit(solution)/shard_map/ppermute | solution.py:297
  44.5 4.4 %collective-permute-done.6.refs_3_ = bf16[4,44,176]{2,1,0:T(8,128)(2,1)S(1)} collective-permute-done((bf16[4,44,176]{2,1,0:T(8,128)(2,1)S(1)}, bf16[4,44,176]{2,1,0:T(8,128)(2,1)S(1)}, u32[]{:S(2)}, u32[]{:S(2)}) %collective-permute-start.6) | collective-permute-done | bytes 61984 | tf_op jit(solution)/shard_map/ppermute | solution.py:297
  49.6 3.3 %collective-permute-start.7 = (bf16[1,44,1408]{2,1,0:T(8,128)(2,1)S(1)}, bf16[1,44,1408]{2,1,0:T(8,128)(2,1)S(1)}, u32[]{:S(2)}, u32[]{:S(2)}) collective-permute-start(bf16[1,44,1408]{2,1,0:T(8,128)(2,1)S(1)} %shard_map.77.one_ref), channel_id=1, source_target_pairs={{0,16},{8,24},{16,0},{24,8},{1,17},{9,25},{17,1},{25,9},{2,18},{10... | collective-permute-start | bytes 371720 | tf_op jit(solution)/shard_map/ppermute | solution.py:297
  53.9 2.3 %collective-permute-done.7.two_ref = bf16[1,44,1408]{2,1,0:T(8,128)(2,1)S(1)} collective-permute-done((bf16[1,44,1408]{2,1,0:T(8,128)(2,1)S(1)}, bf16[1,44,1408]{2,1,0:T(8,128)(2,1)S(1)}, u32[]{:S(2)}, u32[]{:S(2)}) %collective-permute-start.7) | collective-permute-done | bytes 123936 | tf_op jit(solution)/shard_map/ppermute | solution.py:297
  56.9 1.6 %collective-permute-start.8 = (bf16[2,44,1408]{2,1,0:T(8,128)(2,1)}, bf16[2,44,1408]{2,1,0:T(8,128)(2,1)S(1)}, u32[]{:S(2)}, u32[]{:S(2)}) collective-permute-start(bf16[2,44,1408]{2,1,0:T(8,128)(2,1)} %pad_maximum_fusion), channel_id=1, source_target_pairs={{0,8},{8,0},{16,24},{24,16},{1,9},{9,1},{17,25},{25,17},{2,10},{10... | collective-permute-start | bytes 743432 | tf_op jit(solution)/shard_map/ppermute | solution.py:297
  58.5 3.1 %all-to-all-done.recv_ref = bf16[8,96,1152]{2,1,0:T(8,128)(2,1)S(1)} async-done(((bf16[8,96,1152]{2,1,0:T(8,128)(2,1)}), bf16[8,96,1152]{2,1,0:T(8,128)(2,1)S(1)}, u32[]{:S(2)}, u32[]{:S(2)}) %all-to-all-start) | async-done | bytes 1769504 | tf_op jit(solution)/shard_map/all_to_all | solution.py:329
  61.7 3.6 %shard_map.78.att_ref = bf16[8,192,256]{2,1,0:T(8,128)(2,1)S(1)} custom-call(bf16[8,96,1152]{2,1,0:T(8,128)(2,1)S(1)} %all-to-all-done.recv_ref), custom_call_target="tpu_custom_call" | custom-call | tf_op jit(solution)/shard_map/pallas_call | solution.py:66
  67.6 1.5 %collective-permute-start.13 = (bf16[176,1408]{1,0:T(8,128)(2,1)S(1)}, bf16[176,1408]{1,0:T(8,128)(2,1)S(1)}, u32[]{:S(2)}, u32[]{:S(2)}) collective-permute-start(bf16[176,1408]{1,0:T(8,128)(2,1)S(1)} %shard_map.80.w_ref.refs_0_), channel_id=1, source_target_pairs={{0,6},{2,0},{4,2},{6,4},{1,7},{3,1},{5,3},{7,5},{8,14},{10,8},{12,... | collective-permute-start | bytes 1486856 | tf_op jit(solution)/shard_map/ppermute | solution.py:286
  69.9 1.5 %collective-permute-start.15 = (bf16[176,1408]{1,0:T(8,128)(2,1)S(1)}, bf16[176,1408]{1,0:T(8,128)(2,1)}, u32[]{:S(2)}, u32[]{:S(2)}) collective-permute-start(bf16[176,1408]{1,0:T(8,128)(2,1)S(1)} %shard_map.80.w_ref.refs_0_), channel_id=1, source_target_pairs={{0,4},{2,6},{4,0},{6,2},{1,5},{3,7},{5,1},{7,3},{8,12},{10,14},{12... | collective-permute-start | bytes 1486856 | tf_op jit(solution)/shard_map/ppermute | solution.py:286
  71.4 3.5 %shard_map.79 = bf16[4,44,1408]{2,1,0:T(8,128)(2,1)S(1)} custom-call(s32[1,28]{1,0:T(1,128)S(1)} %bitcast.29, bf16[8,192,256]{2,1,0:T(8,128)(2,1)S(1)} %shard_map.78.att_ref, bf16[192,1408]{1,0:T(8,128)(2,1)} %bitcast.23.refs_0_, bf16[192,1408]{1,0:T(8,128)(2,1)} %collective-permute-done.9.refs_1_, bf16[192,1408]{1,0:T(8,128)(2,1)} %collective-permute-done.refs_2_, ...), custom_call_target="tpu_custom_call" | custom-call | tf_op jit(solution)/shard_map/pallas_call | solution.py:66
  75.7 4.5 %all-to-all-start.1 = ((bf16[4,44,1408]{2,1,0:T(8,128)(2,1)}), bf16[4,44,1408]{2,1,0:T(8,128)(2,1)}, u32[]{:S(2)}, u32[]{:S(2)}) async-start(bf16[4,44,1408]{2,1,0:T(8,128)(2,1)} %copy-done.1), calls=%async_computation.1 | async-start | bytes 1081344 | tf_op jit(solution)/shard_map/all_to_all | solution.py:367
  80.2 3.6 %shard_map.81.grad_att_ref = bf16[8,192,176]{2,1,0:T(8,128)(2,1)S(1)} custom-call(bf16[176,1408]{1,0:T(8,128)(2,1)S(1)} %shard_map.80.w_ref.refs_0_, bf16[192,1408]{1,0:T(8,128)(2,1)} %bitcast.23.refs_0_, bf16[192,1408]{1,0:T(8,128)(2,1)} %collective-permute-done.9.refs_1_, bf16[192,1408]{1,0:T(8,128)(2,1)} %collective-permute-done.refs_2_, ...), custom_call_target="tpu_custom_call" | custom-call | tf_op jit(solution)/shard_map/pallas_call | solution.py:66
  83.8 9.3 %shard_map.82 = bf16[8,96,1408]{2,1,0:T(8,128)(2,1)S(1)} custom-call(s32[1,28]{1,0:T(1,128)S(1)} %bitcast.30, bf16[8,192,176]{2,1,0:T(8,128)(2,1)S(1)} %shard_map.81.grad_att_ref, bf16[8,192,256]{2,1,0:T(8,128)(2,1)S(1)} %shard_map.78.att_ref, bf16[8,96,1152]{2,1,0:T(8,128)(2,1)S(1)} %all-to-all-done.recv_ref), custom_call_target="tpu_custom_call" | custom-call | tf_op jit(solution)/shard_map/pallas_call | solution.py:66
  93.1 1.4 copy-done
  94.4 1.3 shard_map.83
  95.7 3.6 %all-to-all-start.2 = ((bf16[8,96,1408]{2,1,0:T(8,128)(2,1)}), bf16[8,96,1408]{2,1,0:T(8,128)(2,1)S(1)}, u32[]{:S(2)}, u32[]{:S(2)}) async-start(bf16[8,96,1408]{2,1,0:T(8,128)(2,1)} %copy-done), calls=%async_computation.2 | async-start | bytes 4325376 | tf_op jit(solution)/shard_map/all_to_all | solution.py:389
  101.1 4.4 %collective-permute-done.20.in_ref = bf16[4,44,176]{2,1,0:T(8,128)(2,1)S(1)} collective-permute-done((bf16[4,44,176]{2,1,0:T(8,128)(2,1)S(1)}, bf16[4,44,176]{2,1,0:T(8,128)(2,1)S(1)}, u32[]{:S(2)}, u32[]{:S(2)}) %collective-permute-start.20) | collective-permute-done | bytes 61984 | tf_op jit(solution)/shard_map/ppermute | solution.py:297
  106.2 4.9 %collective-permute-done.21.in_ref = bf16[2,44,176]{2,1,0:T(8,128)(2,1)S(1)} collective-permute-done((bf16[2,44,176]{2,1,0:T(8,128)(2,1)S(1)}, bf16[2,44,176]{2,1,0:T(8,128)(2,1)S(1)}, u32[]{:S(2)}, u32[]{:S(2)}) %collective-permute-start.21) | collective-permute-done | bytes 31008 | tf_op jit(solution)/shard_map/ppermute | solution.py:297
  111.1 2.8 %collective-permute-start.22 = (f32[44,176]{1,0:T(8,128)S(1)}, f32[44,176]{1,0:T(8,128)S(1)}, u32[]{:S(2)}, u32[]{:S(2)}) collective-permute-start(f32[44,176]{1,0:T(8,128)S(1)} %bitcast.34), channel_id=1, source_target_pairs={{0,0},{1,32},{2,64},{3,96},{4,128},{5,160},{6,192},{7,224},{8,8},{... | collective-permute-start | bytes 92936 | tf_op jit(solution)/shard_map/ppermute | solution.py:302
  117.1 13.7 %all-to-all-done.2.in_ref = bf16[8,96,1408]{2,1,0:T(8,128)(2,1)S(1)} async-done(((bf16[8,96,1408]{2,1,0:T(8,128)(2,1)}), bf16[8,96,1408]{2,1,0:T(8,128)(2,1)S(1)}, u32[]{:S(2)}, u32[]{:S(2)}) %all-to-all-start.2) | async-done | bytes 2162720 | tf_op jit(solution)/shard_map/all_to_all | solution.py:389
  135.0 5.7 %shard_map.84 = (bf16[1,1,192,1408]{3,2,1,0:T(8,128)(2,1)}, bf16[1,1,192,4224]{3,2,1,0:T(8,128)(2,1)}) custom-call(s32[1,28]{1,0:T(1,128)S(1)} %bitcast.32, bf16[8,96,1408]{2,1,0:T(8,128)(2,1)S(1)} %all-to-all-done.2.in_ref, bf16[176,1408]{1,0:T(8,128)(2,1)S(1)} %shard_map.80.w_ref.refs_0_, bf16[176,1408]{1,0:T(8,128)(2,1)S(1)} %copy-done.4, ...), custom_call_target="tpu_custom_call" | custom-call | tf_op jit(solution)/shard_map/pallas_call | solution.py:66
  (68 shorter events, 18.6 us)
Async XLA Ops:
  1.3 1.4 %copy-start.2 = (bf16[1,1,192,4224]{3,2,1,0:T(8,128)(2,1)S(1)}, bf16[1,1,192,4224]{3,2,1,0:T(8,128)(2,1)}, u32[]{:S(2)}) copy-start(bf16[1,1,192,4224]{3,2,1,0:T(8,128)(2,1)} %qkv_ref.1) | copy-start | bytes 4866052
  3.4 7.0 %copy-start.14 = (bf16[44,176]{1,0:T(8,128)(2,1)S(1)}, bf16[44,176]{1,0:T(8,128)(2,1)}, u32[]{:S(2)}) copy-start(bf16[44,176]{1,0:T(8,128)(2,1)} %param.9) | copy-start | bytes 46468
  5.3 25.9 %collective-permute-start = (bf16[192,1408]{1,0:T(8,128)(2,1)}, bf16[192,1408]{1,0:T(8,128)(2,1)}, u32[]{:S(2)}, u32[]{:S(2)}) collective-permute-start(bf16[192,1408]{1,0:T(8,128)(2,1)} %bitcast.23.refs_0_), channel_id=1, source_target_pairs={{0,2},{2,4},{4,6},{6,0},{1,3},{3,5},{5,7},{7,1},{8,10},{10,12},{12... | collective-permute-start | bytes 1622024 | tf_op jit(solution)/shard_map/ppermute | solution.py:286
  6.8 25.5 %collective-permute-start.1 = (bf16[192,1408]{1,0:T(8,128)(2,1)}, bf16[192,1408]{1,0:T(8,128)(2,1)}, u32[]{:S(2)}, u32[]{:S(2)}) collective-permute-start(bf16[192,1408]{1,0:T(8,128)(2,1)} %bitcast.23.refs_0_), channel_id=1, source_target_pairs={{0,6},{2,0},{4,2},{6,4},{1,7},{3,1},{5,3},{7,5},{8,14},{10,8},{12,... | collective-permute-start | bytes 1622024 | tf_op jit(solution)/shard_map/ppermute | solution.py:286
  8.5 25.9 %collective-permute-start.2 = (bf16[192,1408]{1,0:T(8,128)(2,1)}, bf16[192,1408]{1,0:T(8,128)(2,1)}, u32[]{:S(2)}, u32[]{:S(2)}) collective-permute-start(bf16[192,1408]{1,0:T(8,128)(2,1)} %bitcast.23.refs_0_), channel_id=1, source_target_pairs={{0,4},{2,6},{4,0},{6,2},{1,5},{3,7},{5,1},{7,3},{8,12},{10,14},{12... | collective-permute-start | bytes 1622024 | tf_op jit(solution)/shard_map/ppermute | solution.py:286
  10.3 12.1 %collective-permute-start.3 = (bf16[1,44,176]{2,1,0:T(8,128)(2,1)S(1)}, bf16[1,44,176]{2,1,0:T(8,128)(2,1)S(1)}, u32[]{:S(2)}, u32[]{:S(2)}) collective-permute-start(bf16[1,44,176]{2,1,0:T(8,128)(2,1)S(1)} %bitcast.35), channel_id=1, source_target_pairs={{0,0},{1,32},{2,64},{3,96},{4,128},{5,160},{6,192},{7,224},{8,8},{... | collective-permute-start | bytes 46472 | tf_op jit(solution)/shard_map/ppermute | solution.py:307
  13.9 17.3 %collective-permute-start.4 = (bf16[1,44,176]{2,1,0:T(8,128)(2,1)S(1)}, bf16[1,44,176]{2,1,0:T(8,128)(2,1)S(1)}, u32[]{:S(2)}, u32[]{:S(2)}) collective-permute-start(bf16[1,44,176]{2,1,0:T(8,128)(2,1)S(1)} %bitcast.36), channel_id=1, source_target_pairs={{0,128},{1,160},{2,192},{3,224},{4,0},{5,32},{6,64},{7,96},{8,136}... | collective-permute-start | bytes 46472 | tf_op jit(solution)/shard_map/ppermute | solution.py:307
  34.4 27.2 %all-to-all-start = ((bf16[8,96,1152]{2,1,0:T(8,128)(2,1)}), bf16[8,96,1152]{2,1,0:T(8,128)(2,1)S(1)}, u32[]{:S(2)}, u32[]{:S(2)}) async-start(bf16[8,96,1152]{2,1,0:T(8,128)(2,1)} %shard_map.76), calls=%async_computation | async-start | bytes 3538944 | tf_op jit(solution)/shard_map/all_to_all | solution.py:329
  38.1 6.1 %collective-permute-start.5 = (bf16[2,44,176]{2,1,0:T(8,128)(2,1)S(1)}, bf16[2,44,176]{2,1,0:T(8,128)(2,1)S(1)}, u32[]{:S(2)}, u32[]{:S(2)}) collective-permute-start(bf16[2,44,176]{2,1,0:T(8,128)(2,1)S(1)} %pad_maximum_fusion.2), channel_id=1, source_target_pairs={{0,64},{32,96},{64,0},{96,32},{128,192},{160,224},{192,128},{224,1... | collective-permute-start | bytes 92936 | tf_op jit(solution)/shard_map/ppermute | solution.py:297
  44.2 4.7 %collective-permute-start.6 = (bf16[4,44,176]{2,1,0:T(8,128)(2,1)S(1)}, bf16[4,44,176]{2,1,0:T(8,128)(2,1)S(1)}, u32[]{:S(2)}, u32[]{:S(2)}) collective-permute-start(bf16[4,44,176]{2,1,0:T(8,128)(2,1)S(1)} %pad_maximum_fusion.1), channel_id=1, source_target_pairs={{0,32},{32,0},{64,96},{96,64},{128,160},{160,128},{192,224},{224,1... | collective-permute-start | bytes 185864 | tf_op jit(solution)/shard_map/ppermute | solution.py:297
  49.6 6.6 %collective-permute-start.7 = (bf16[1,44,1408]{2,1,0:T(8,128)(2,1)S(1)}, bf16[1,44,1408]{2,1,0:T(8,128)(2,1)S(1)}, u32[]{:S(2)}, u32[]{:S(2)}) collective-permute-start(bf16[1,44,1408]{2,1,0:T(8,128)(2,1)S(1)} %shard_map.77.one_ref), channel_id=1, source_target_pairs={{0,16},{8,24},{16,0},{24,8},{1,17},{9,25},{17,1},{25,9},{2,18},{10... | collective-permute-start | bytes 371720 | tf_op jit(solution)/shard_map/ppermute | solution.py:297
  52.9 16.2 %collective-permute-start.10 = (bf16[192,1408]{1,0:T(8,128)(2,1)}, bf16[192,1408]{1,0:T(8,128)(2,1)}, u32[]{:S(2)}, u32[]{:S(2)}) collective-permute-start(bf16[192,1408]{1,0:T(8,128)(2,1)} %collective-permute-done.refs_2_), channel_id=1, source_target_pairs={{0,1},{1,0},{2,3},{3,2},{4,5},{5,4},{6,7},{7,6},{8,9},{9,8},{10,11... | collective-permute-start | bytes 1622024 | tf_op jit(solution)/shard_map/ppermute | solution.py:286
  52.9 17.0 %collective-permute-start.11 = (bf16[192,1408]{1,0:T(8,128)(2,1)}, bf16[192,1408]{1,0:T(8,128)(2,1)}, u32[]{:S(2)}, u32[]{:S(2)}) collective-permute-start(bf16[192,1408]{1,0:T(8,128)(2,1)} %collective-permute-done.1.refs_4_), channel_id=1, source_target_pairs={{0,1},{1,0},{2,3},{3,2},{4,5},{5,4},{6,7},{7,6},{8,9},{9,8},{10,11... | collective-permute-start | bytes 1622024 | tf_op jit(solution)/shard_map/ppermute | solution.py:286
  53.4 18.0 %collective-permute-start.12 = (bf16[192,1408]{1,0:T(8,128)(2,1)}, bf16[192,1408]{1,0:T(8,128)(2,1)}, u32[]{:S(2)}, u32[]{:S(2)}) collective-permute-start(bf16[192,1408]{1,0:T(8,128)(2,1)} %collective-permute-done.2.refs_6_), channel_id=1, source_target_pairs={{0,1},{1,0},{2,3},{3,2},{4,5},{5,4},{6,7},{7,6},{8,9},{9,8},{10,11... | collective-permute-start | bytes 1622024 | tf_op jit(solution)/shard_map/ppermute | solution.py:286
  53.4 18.0 %collective-permute-start.9 = (bf16[192,1408]{1,0:T(8,128)(2,1)}, bf16[192,1408]{1,0:T(8,128)(2,1)}, u32[]{:S(2)}, u32[]{:S(2)}) collective-permute-start(bf16[192,1408]{1,0:T(8,128)(2,1)} %bitcast.23.refs_0_), channel_id=1, source_target_pairs={{0,1},{1,0},{2,3},{3,2},{4,5},{5,4},{6,7},{7,6},{8,9},{9,8},{10,11... | collective-permute-start | bytes 1622024 | tf_op jit(solution)/shard_map/ppermute | solution.py:286
  56.9 8.3 %collective-permute-start.8 = (bf16[2,44,1408]{2,1,0:T(8,128)(2,1)}, bf16[2,44,1408]{2,1,0:T(8,128)(2,1)S(1)}, u32[]{:S(2)}, u32[]{:S(2)}) collective-permute-start(bf16[2,44,1408]{2,1,0:T(8,128)(2,1)} %pad_maximum_fusion), channel_id=1, source_target_pairs={{0,8},{8,0},{16,24},{24,16},{1,9},{9,1},{17,25},{25,17},{2,10},{10... | collective-permute-start | bytes 743432 | tf_op jit(solution)/shard_map/ppermute | solution.py:297
  67.6 28.1 %collective-permute-start.13 = (bf16[176,1408]{1,0:T(8,128)(2,1)S(1)}, bf16[176,1408]{1,0:T(8,128)(2,1)S(1)}, u32[]{:S(2)}, u32[]{:S(2)}) collective-permute-start(bf16[176,1408]{1,0:T(8,128)(2,1)S(1)} %shard_map.80.w_ref.refs_0_), channel_id=1, source_target_pairs={{0,6},{2,0},{4,2},{6,4},{1,7},{3,1},{5,3},{7,5},{8,14},{10,8},{12,... | collective-permute-start | bytes 1486856 | tf_op jit(solution)/shard_map/ppermute | solution.py:286
  69.1 26.6 %collective-permute-start.14 = (bf16[176,1408]{1,0:T(8,128)(2,1)S(1)}, bf16[176,1408]{1,0:T(8,128)(2,1)}, u32[]{:S(2)}, u32[]{:S(2)}) collective-permute-start(bf16[176,1408]{1,0:T(8,128)(2,1)S(1)} %shard_map.80.w_ref.refs_0_), channel_id=1, source_target_pairs={{0,2},{2,4},{4,6},{6,0},{1,3},{3,5},{5,7},{7,1},{8,10},{10,12},{12... | collective-permute-start | bytes 1486856 | tf_op jit(solution)/shard_map/ppermute | solution.py:286
  69.9 25.9 %collective-permute-start.15 = (bf16[176,1408]{1,0:T(8,128)(2,1)S(1)}, bf16[176,1408]{1,0:T(8,128)(2,1)}, u32[]{:S(2)}, u32[]{:S(2)}) collective-permute-start(bf16[176,1408]{1,0:T(8,128)(2,1)S(1)} %shard_map.80.w_ref.refs_0_), channel_id=1, source_target_pairs={{0,4},{2,6},{4,0},{6,2},{1,5},{3,7},{5,1},{7,3},{8,12},{10,14},{12... | collective-permute-start | bytes 1486856 | tf_op jit(solution)/shard_map/ppermute | solution.py:286
  75.7 18.7 %all-to-all-start.1 = ((bf16[4,44,1408]{2,1,0:T(8,128)(2,1)}), bf16[4,44,1408]{2,1,0:T(8,128)(2,1)}, u32[]{:S(2)}, u32[]{:S(2)}) async-start(bf16[4,44,1408]{2,1,0:T(8,128)(2,1)} %copy-done.1), calls=%async_computation.1 | async-start | bytes 1081344 | tf_op jit(solution)/shard_map/all_to_all | solution.py:367
  93.1 1.4 copy-start
  95.7 35.1 %all-to-all-start.2 = ((bf16[8,96,1408]{2,1,0:T(8,128)(2,1)}), bf16[8,96,1408]{2,1,0:T(8,128)(2,1)S(1)}, u32[]{:S(2)}, u32[]{:S(2)}) async-start(bf16[8,96,1408]{2,1,0:T(8,128)(2,1)} %copy-done), calls=%async_computation.2 | async-start | bytes 4325376 | tf_op jit(solution)/shard_map/all_to_all | solution.py:389
  99.4 14.6 %collective-permute-start.16 = (bf16[176,1408]{1,0:T(8,128)(2,1)S(1)}, bf16[176,1408]{1,0:T(8,128)(2,1)S(1)}, u32[]{:S(2)}, u32[]{:S(2)}) collective-permute-start(bf16[176,1408]{1,0:T(8,128)(2,1)S(1)} %shard_map.80.w_ref.refs_0_), channel_id=1, source_target_pairs={{0,1},{1,0},{2,3},{3,2},{4,5},{5,4},{6,7},{7,6},{8,9},{9,8},{10,11... | collective-permute-start | bytes 1486856 | tf_op jit(solution)/shard_map/ppermute | solution.py:286
  99.8 15.0 %collective-permute-start.17 = (bf16[176,1408]{1,0:T(8,128)(2,1)S(1)}, bf16[176,1408]{1,0:T(8,128)(2,1)S(1)}, u32[]{:S(2)}, u32[]{:S(2)}) collective-permute-start(bf16[176,1408]{1,0:T(8,128)(2,1)S(1)} %collective-permute-done.13.refs_2_), channel_id=1, source_target_pairs={{0,1},{1,0},{2,3},{3,2},{4,5},{5,4},{6,7},{7,6},{8,9},{9,8},{10,11... | collective-permute-start | bytes 1486856 | tf_op jit(solution)/shard_map/ppermute | solution.py:286
  100.0 15.6 %collective-permute-start.18 = (bf16[176,1408]{1,0:T(8,128)(2,1)}, bf16[176,1408]{1,0:T(8,128)(2,1)S(1)}, u32[]{:S(2)}, u32[]{:S(2)}) collective-permute-start(bf16[176,1408]{1,0:T(8,128)(2,1)} %collective-permute-done.14.refs_4_), channel_id=1, source_target_pairs={{0,1},{1,0},{2,3},{3,2},{4,5},{5,4},{6,7},{7,6},{8,9},{9,8},{10,11... | collective-permute-start | bytes 1486856 | tf_op jit(solution)/shard_map/ppermute | solution.py:286
  100.3 16.0 %collective-permute-start.19 = (bf16[176,1408]{1,0:T(8,128)(2,1)}, bf16[176,1408]{1,0:T(8,128)(2,1)S(1)}, u32[]{:S(2)}, u32[]{:S(2)}) collective-permute-start(bf16[176,1408]{1,0:T(8,128)(2,1)} %collective-permute-done.15.refs_6_), channel_id=1, source_target_pairs={{0,1},{1,0},{2,3},{3,2},{4,5},{5,4},{6,7},{7,6},{8,9},{9,8},{10,11... | collective-permute-start | bytes 1486856 | tf_op jit(solution)/shard_map/ppermute | solution.py:286
  100.5 5.0 %collective-permute-start.20 = (bf16[4,44,176]{2,1,0:T(8,128)(2,1)S(1)}, bf16[4,44,176]{2,1,0:T(8,128)(2,1)S(1)}, u32[]{:S(2)}, u32[]{:S(2)}) collective-permute-start(bf16[4,44,176]{2,1,0:T(8,128)(2,1)S(1)} %get-tuple-element.60), channel_id=1, source_target_pairs={{0,32},{32,0},{64,96},{96,64},{128,160},{160,128},{192,224},{224,1... | collective-permute-start | bytes 185864 | tf_op jit(solution)/shard_map/ppermute | solution.py:297
  105.5 5.6 %collective-permute-start.21 = (bf16[2,44,176]{2,1,0:T(8,128)(2,1)S(1)}, bf16[2,44,176]{2,1,0:T(8,128)(2,1)S(1)}, u32[]{:S(2)}, u32[]{:S(2)}) collective-permute-start(bf16[2,44,176]{2,1,0:T(8,128)(2,1)S(1)} %get-tuple-element.62), channel_id=1, source_target_pairs={{0,64},{32,96},{64,0},{96,32},{128,192},{160,224},{192,128},{224,1... | collective-permute-start | bytes 92936 | tf_op jit(solution)/shard_map/ppermute | solution.py:297
  111.1 29.6 %collective-permute-start.22 = (f32[44,176]{1,0:T(8,128)S(1)}, f32[44,176]{1,0:T(8,128)S(1)}, u32[]{:S(2)}, u32[]{:S(2)}) collective-permute-start(f32[44,176]{1,0:T(8,128)S(1)} %bitcast.34), channel_id=1, source_target_pairs={{0,0},{1,32},{2,64},{3,96},{4,128},{5,160},{6,192},{7,224},{8,8},{... | collective-permute-start | bytes 92936 | tf_op jit(solution)/shard_map/ppermute | solution.py:302
  114.7 26.0 %collective-permute-start.23 = (f32[44,176]{1,0:T(8,128)S(1)}, f32[44,176]{1,0:T(8,128)S(1)}, u32[]{:S(2)}, u32[]{:S(2)}) collective-permute-start(f32[44,176]{1,0:T(8,128)S(1)} %bitcast.33), channel_id=1, source_target_pairs={{0,4},{1,36},{2,68},{3,100},{4,132},{5,164},{6,196},{7,228},{8,12}... | collective-permute-start | bytes 92936 | tf_op jit(solution)/shard_map/ppermute | solution.py:302
  130.9 1.0 copy-start.4
  131.9 1.0 copy-start.6
  (10 other events, 8.4 us)
